TPU v7x, 32 devices: a whole 2x2x4 slice. The times are simulated.
32 devices in a mesh: dp: 8 (over z, x), fsdp: 4 (over y, core).
Axes of the slice: x: 2, y: 2, z: 4, core: 2. Of those that a mesh axis runs over, the one named last changes fastest.
Arguments:
- byte_states: bfloat16 [8192, 1024], P(('dp', 'fsdp')), may hold values from -6 to 6
- doc_lengths: int32 [8, 2], P('dp'), may hold values from 0 to 128, as said below
- out_grad: bfloat16 [8192, 1024], P(('dp', 'fsdp')), may hold values from -6 to 6
- patch_proj: bfloat16 [8192, 1024], P(('dp', 'fsdp')), may hold values from -0.0625 to 0.0625
- global_gain: bfloat16 [1024], P(('dp', 'fsdp')), may hold values from 0.099609375 to 1.8984375
- in_proj: bfloat16 [1024, 4384], P(('dp', 'fsdp')), may hold values from -0.1875 to 0.1875
- conv_weight: bfloat16 [2304, 4], P(('dp', 'fsdp')), may hold values from -3 to 3
- conv_bias: bfloat16 [2304], P(('dp', 'fsdp')), may hold values from -3 to 3
- dt_bias: float32 [32], replicated, may hold values from -4 to -1
- a_log: float32 [32], replicated, may hold values from -4 to 1
- skip_weight: float32 [32], replicated, may hold values from 0.5 to 1.5
- mixer_gain: bfloat16 [2048], P(('dp', 'fsdp')), may hold values from 0.099609375 to 1.8984375
- out_proj: bfloat16 [2048, 1024], P(('dp', 'fsdp')), may hold values from -0.125 to 0.125
- attn_gain: bfloat16 [1024], P(('dp', 'fsdp')), may hold values from 0.099609375 to 1.8984375
- qkv_proj: bfloat16 [1024, 3072], P(('dp', 'fsdp')), may hold values from -0.1875 to 0.1875
- attn_out: bfloat16 [1024, 1024], P(('dp', 'fsdp')), may hold values from -0.375 to 0.375
- ffn_gain: bfloat16 [1024], P(('dp', 'fsdp')), may hold values from 0.099609375 to 1.8984375
- gate_proj: bfloat16 [1024, 4096], P(('dp', 'fsdp')), may hold values from -0.1875 to 0.1875
- up_proj: bfloat16 [1024, 4096], P(('dp', 'fsdp')), may hold values from -0.1875 to 0.1875
- down_proj: bfloat16 [4096, 1024], P(('dp', 'fsdp')), may hold values from -0.09375 to 0.09375
Outputs:
- block_out: bfloat16 [8192, 1024], P(('dp', 'fsdp'))
- grad_states: float32 [8192, 1024], P(('dp', 'fsdp'))
- grad_patch_proj: float32 [8192, 1024], P(('dp', 'fsdp'))
- grad_global_gain: float32 [1024], P(('dp', 'fsdp'))
- grad_in_proj: float32 [1024, 4384], P(('dp', 'fsdp'))
- grad_conv_weight: float32 [2304, 4], P(('dp', 'fsdp'))
- grad_conv_bias: float32 [2304], P(('dp', 'fsdp'))
- grad_dt_bias: float32 [32], replicated
- grad_a_log: float32 [32], replicated
- grad_skip_weight: float32 [32], replicated
- grad_mixer_gain: float32 [2048], P(('dp', 'fsdp'))
- grad_out_proj: float32 [2048, 1024], P(('dp', 'fsdp'))
- grad_attn_gain: float32 [1024], P(('dp', 'fsdp'))
- grad_qkv_proj: float32 [1024, 3072], P(('dp', 'fsdp'))
- grad_attn_out: float32 [1024, 1024], P(('dp', 'fsdp'))
- grad_ffn_gain: float32 [1024], P(('dp', 'fsdp'))
- grad_gate_proj: float32 [1024, 4096], P(('dp', 'fsdp'))
- grad_up_proj: float32 [1024, 4096], P(('dp', 'fsdp'))
- grad_down_proj: float32 [4096, 1024], P(('dp', 'fsdp'))
Inputs may be any that keep to these rules, and one draw needn't show every extreme that they name: `doc_lengths`: each row gives, in patches, the lengths of the two documents packed from the start of one slot of 128 patches; the rest of the slot is padding and the two lengths sum to at most 128.
All inputs are finite; a program needn't handle non-finite values.
Results may differ from a plain program's by a relative error of at most 0.017.
Values may be sent and summed in bfloat16 or wider, within the bound.
A program may use at most 448 MiB of HBM per device.

v0:
```python
from functools import partial

import jax
import jax.numpy as jnp
from jax import lax
from jax.sharding import PartitionSpec as P

D = 1024
HEAD = 64
HEAD_M = 64
STATE = 128
CONV = 4
PATCH = 8
DI = 2048
MHEADS = 32
CONV_CH = 2304


EPSILON = 1e-05
HIGHEST = lax.Precision.HIGHEST


def shifted(block, axis, distance):
    devices = range(lax.axis_size(axis))
    route = [(i - distance, i) for i in devices if i - distance in devices]
    return lax.ppermute(block, axis, route)


def prefix(value, axis, combine, identity):
    devices, place = (lax.axis_size(axis), lax.axis_index(axis))
    everything = jax.tree.map(
        lambda part, kind: lax.all_gather(part.astype(kind), axis),
        value,
        (jnp.bfloat16, jnp.bfloat16),
    )
    start = jax.tree.map(
        lambda part, zero: jnp.broadcast_to(jnp.asarray(zero, part.dtype), part.shape),
        value,
        identity,
    )

    def prefix_step(k, before):
        reached = k < place
        new = combine(
            before, jax.tree.map(lambda part, own: part[k].astype(own.dtype), everything, value)
        )
        return jax.tree.map(lambda a, b: jnp.where(reached, a, b), new, before)

    return lax.fori_loop(0, devices, prefix_step, start)


def carried_in(value, axis, combine, identity):
    devices, place = (lax.axis_size(axis), lax.axis_index(axis))
    everything = jax.tree.map(
        lambda part, kind: lax.all_gather(part.astype(kind), axis),
        value,
        jax.tree.map(lambda a: jnp.bfloat16 if a.dtype == jnp.float32 else a.dtype, value),
    )
    start = jax.tree.map(
        lambda part, zero: jnp.broadcast_to(jnp.asarray(zero, part.dtype), part.shape),
        value,
        identity,
    )

    def carried_step(k, before):
        at = devices - 1 - k
        reached = at > place
        new = combine(
            before, jax.tree.map(lambda part, own: part[at].astype(own.dtype), everything, value)
        )
        return jax.tree.map(lambda a, b: jnp.where(reached, a, b), new, before)

    return lax.fori_loop(0, devices, carried_step, start)


def product(left, right):
    return jnp.dot(left, right, preferred_element_type=jnp.float32)


def weight_grad(left, right):
    return lax.dot_general(
        left, right, (((0,), (0,)), ((), ())), preferred_element_type=jnp.float32
    )


def input_grad(grad_rows, weight):
    return lax.dot_general(
        grad_rows, weight, (((1,), (1,)), ((), ())), preferred_element_type=jnp.float32
    )


def rms_scale(value, gain):
    return value * lax.rsqrt(jnp.mean(value * value, axis=-1, keepdims=True) + EPSILON) * gain


def gated_norm(core_out, gate_raw, gain):
    count = core_out.shape[0]
    return rms_scale(core_out.reshape(count, DI) * jax.nn.silu(gate_raw), gain)


def patch_docs(doc_lengths, start, count):
    places = start + jnp.arange(count, dtype=jnp.int32)
    first_end = doc_lengths[0, 0]
    second_end = first_end + doc_lengths[0, 1]
    numbers = (places >= first_end).astype(jnp.int32) + (places >= second_end).astype(jnp.int32)
    return jnp.where(places >= 0, numbers, -1)


def chain(earlier, later):
    return (earlier[0] * later[0], later[1] + later[0][:, None, None] * earlier[1])


def mixer_core(
    channels,
    rim,
    step_raw,
    state_in,
    conv_weight,
    conv_bias,
    dt_bias,
    a_log,
    skip_weight,
    docs,
    rim_docs,
    prev_doc,
):
    count = channels.shape[0]
    padded = jnp.concatenate([rim, channels], axis=0)
    padded_docs = jnp.concatenate([rim_docs, docs])
    total = conv_bias[None, :]
    for shift_k in range(CONV):
        same_doc = (padded_docs[shift_k : shift_k + count] == docs).astype(jnp.float32)
        total = (
            total
            + padded[shift_k : shift_k + count]
            * conv_weight[:, shift_k][None, :]
            * same_doc[:, None]
        )
    activated = jax.nn.silu(total)
    inputs = activated[:, :DI].reshape(count, MHEADS, HEAD_M)
    in_map = activated[:, DI : DI + STATE]
    out_map = activated[:, DI + STATE :]
    step_size = jax.nn.softplus(step_raw + dt_bias[None, :])
    rate = -jnp.exp(a_log)
    cumulative = jnp.cumsum(step_size * rate[None, :], axis=0)
    places = jnp.arange(count, dtype=jnp.int32)
    keep = ((places[:, None] >= places[None, :]) & (docs[:, None] == docs[None, :]))[:, :, None]
    spread = cumulative[:, None, :] - cumulative[None, :, :]
    decay_table = jnp.where(keep, jnp.exp(jnp.where(keep, spread, 0.0)), 0.0)
    inner = jnp.dot(out_map, in_map.T, precision=HIGHEST, preferred_element_type=jnp.float32)
    mixing = decay_table * inner[:, :, None] * step_size[None, :, :]
    outputs = jnp.einsum("tsh,shp->thp", mixing, inputs, precision=HIGHEST)
    carry_in = jnp.where((docs == prev_doc)[:, None], jnp.exp(cumulative), 0.0)
    outputs = outputs + carry_in[:, :, None] * jnp.einsum(
        "tn,hpn->thp", out_map, state_in, precision=HIGHEST
    )
    outputs = outputs + skip_weight[None, :, None] * inputs
    last_doc = docs[count - 1]
    tail_keep = (docs == last_doc)[:, None]
    tail_gap = cumulative[count - 1][None, :] - cumulative
    tail_weight = (
        jnp.where(tail_keep, jnp.exp(jnp.where(tail_keep, tail_gap, 0.0)), 0.0) * step_size
    )
    decay_total = jnp.where(prev_doc == last_doc, jnp.exp(cumulative[count - 1]), 0.0)
    state_out = jnp.einsum("sh,shp,sn->hpn", tail_weight, inputs, in_map, precision=HIGHEST)
    state_out = state_out + decay_total[:, None, None] * state_in
    return ((outputs, state_out), (decay_total, carry_in, out_map))


def attend(qkv_low, patches):
    heads = qkv_low.reshape(patches, PATCH, 3, -1, HEAD)
    queries = heads[:, :, 0]
    key_rows = heads[:, :, 1]
    value_rows = heads[:, :, 2]
    scores = jnp.einsum(
        "pihd,pjhd->phij", queries, key_rows, preferred_element_type=jnp.float32
    ) * HEAD ** (-0.5)
    places = jnp.arange(PATCH)
    causal = places[:, None] >= places[None, :]
    scores = jnp.where(causal, scores, -1e30)
    attn_weights = jax.nn.softmax(scores, axis=-1)
    attn_low = attn_weights.astype(jnp.bfloat16)
    mixed = jnp.einsum("phij,pjhd->pihd", attn_low, value_rows, preferred_element_type=jnp.float32)
    mixed = mixed.astype(jnp.bfloat16).reshape(patches * PATCH, -1)
    return ((queries, key_rows, value_rows, attn_weights, attn_low), mixed)


def attend_back(grad_mixed_low, pieces):
    queries, key_rows, value_rows, attn_weights, attn_low = pieces
    patches = queries.shape[0]
    grad_mixed = grad_mixed_low.reshape(patches, PATCH, -1, HEAD)
    grad_values = jnp.einsum(
        "phij,pihd->pjhd", attn_low, grad_mixed, preferred_element_type=jnp.float32
    )
    grad_weights = jnp.einsum(
        "pihd,pjhd->phij", grad_mixed, value_rows, preferred_element_type=jnp.float32
    )
    grad_scores = attn_weights * (
        grad_weights - jnp.sum(attn_weights * grad_weights, axis=-1, keepdims=True)
    )
    scores_low = grad_scores.astype(jnp.bfloat16)
    scale = HEAD ** (-0.5)
    grad_queries = (
        jnp.einsum("phij,pjhd->pihd", scores_low, key_rows, preferred_element_type=jnp.float32)
        * scale
    )
    grad_keys = (
        jnp.einsum("phij,pihd->pjhd", scores_low, queries, preferred_element_type=jnp.float32)
        * scale
    )
    stacked = jnp.stack([grad_queries, grad_keys, grad_values], axis=2).reshape(patches * PATCH, -1)
    return stacked.astype(jnp.bfloat16)


def local_forward(byte_states, mixed_patch, local_set, live):
    attn_gain, qkv_proj, attn_out, ffn_gain, gate_proj, up_proj, down_proj = local_set
    rows = byte_states.shape[0]
    streams = byte_states.astype(jnp.float32) + jnp.repeat(mixed_patch, PATCH, axis=0)
    normed_low = rms_scale(streams, attn_gain.astype(jnp.float32)).astype(jnp.bfloat16)
    qkv_low = product(normed_low, qkv_proj).astype(jnp.bfloat16)
    pieces, mixed_heads = attend(qkv_low, rows // PATCH)
    attended = streams + product(mixed_heads, attn_out)
    ffn_low = rms_scale(attended, ffn_gain.astype(jnp.float32)).astype(jnp.bfloat16)
    gate = product(ffn_low, gate_proj)
    upward = product(ffn_low, up_proj)
    hidden_low = (jax.nn.silu(gate) * upward).astype(jnp.bfloat16)
    block = live * (attended + product(hidden_low, down_proj))
    cache = (streams, normed_low, pieces, mixed_heads, attended, ffn_low, gate, upward, hidden_low)
    return (block, cache)


def local_backward(grad_block, cache, local_set):
    attn_gain, qkv_proj, attn_out, ffn_gain, gate_proj, up_proj, down_proj = local_set
    streams, normed_low, pieces, mixed_heads, attended, ffn_low, gate, upward, hidden_low = cache
    down_low = grad_block.astype(jnp.bfloat16)
    grad_down = weight_grad(hidden_low, down_low)
    grad_hidden = input_grad(down_low, down_proj)
    sigma = jax.nn.sigmoid(gate)
    grad_gate_low = (grad_hidden * upward * sigma * (1.0 + gate * (1.0 - sigma))).astype(
        jnp.bfloat16
    )
    grad_up_low = (grad_hidden * gate * sigma).astype(jnp.bfloat16)
    grad_gate = weight_grad(ffn_low, grad_gate_low)
    grad_up = weight_grad(ffn_low, grad_up_low)
    grad_ffn_in = input_grad(grad_gate_low, gate_proj) + input_grad(grad_up_low, up_proj)
    _, norm_back = jax.vjp(rms_scale, attended, ffn_gain.astype(jnp.float32))
    grad_attended_norm, grad_ffn_gain = norm_back(grad_ffn_in)
    grad_attended = grad_block + grad_attended_norm
    attn_grad_low = grad_attended.astype(jnp.bfloat16)
    grad_attn_out = weight_grad(mixed_heads, attn_grad_low)
    grad_mixed_low = input_grad(attn_grad_low, attn_out).astype(jnp.bfloat16)
    grad_qkv_low = attend_back(grad_mixed_low, pieces)
    grad_qkv = weight_grad(normed_low, grad_qkv_low)
    grad_normed = input_grad(grad_qkv_low, qkv_proj)
    _, norm_back = jax.vjp(rms_scale, streams, attn_gain.astype(jnp.float32))
    grad_streams_norm, grad_attn_gain = norm_back(grad_normed)
    grad_streams = grad_attended + grad_streams_norm
    return (
        grad_streams,
        (grad_qkv, grad_attn_out, grad_gate, grad_up, grad_down, grad_attn_gain, grad_ffn_gain),
    )


def body(
    byte_states,
    doc_lengths,
    out_grad,
    patch_proj,
    global_gain,
    in_proj,
    conv_weight,
    conv_bias,
    dt_bias,
    a_log,
    skip_weight,
    mixer_gain,
    out_proj,
    attn_gain,
    qkv_proj,
    attn_out,
    ffn_gain,
    gate_proj,
    up_proj,
    down_proj,
):
    rows = byte_states.shape[0]
    patches = rows // PATCH
    share = lax.axis_index("fsdp")
    start = share * patches
    docs = patch_docs(doc_lengths, start, patches)
    rim_docs = patch_docs(doc_lengths, start - (CONV - 1), CONV - 1)
    prev_doc = patch_docs(doc_lengths, start - 1, 1)[0]
    live = jnp.repeat((docs < 2).astype(jnp.float32), PATCH)[:, None]
    all_set = (
        lax.all_gather(patch_proj, ("dp", "fsdp"), axis=0, tiled=True),
        lax.all_gather(global_gain, ("dp", "fsdp"), axis=0, tiled=True),
        lax.all_gather(in_proj, ("dp", "fsdp"), axis=0, tiled=True),
        lax.all_gather(conv_weight, ("dp", "fsdp"), axis=0, tiled=True),
        lax.all_gather(conv_bias, ("dp", "fsdp"), axis=0, tiled=True),
        lax.all_gather(mixer_gain, ("dp", "fsdp"), axis=0, tiled=True),
        lax.all_gather(out_proj, ("dp", "fsdp"), axis=0, tiled=True),
        lax.all_gather(attn_gain, ("dp", "fsdp"), axis=0, tiled=True),
        lax.all_gather(qkv_proj, ("dp", "fsdp"), axis=0, tiled=True),
        lax.all_gather(attn_out, ("dp", "fsdp"), axis=0, tiled=True),
        lax.all_gather(ffn_gain, ("dp", "fsdp"), axis=0, tiled=True),
        lax.all_gather(gate_proj, ("dp", "fsdp"), axis=0, tiled=True),
        lax.all_gather(up_proj, ("dp", "fsdp"), axis=0, tiled=True),
        lax.all_gather(down_proj, ("dp", "fsdp"), axis=0, tiled=True),
    )
    global_set = all_set[:7]
    local_set = all_set[7:]
    patch_full, gain_g_full, in_full, conv_w_full, conv_b_full, gain_m_full, out_full = global_set
    patch_rows = byte_states.reshape(patches, PATCH * D)
    patch_sum = product(patch_rows, patch_full)
    gain_g = gain_g_full.astype(jnp.float32)
    global_low = rms_scale(patch_sum, gain_g).astype(jnp.bfloat16)
    projected = product(global_low, in_full)
    gate_raw = projected[:, :DI]
    channels = projected[:, DI : DI + CONV_CH]
    step_raw = projected[:, DI + CONV_CH :]
    rim = shifted(channels[patches - (CONV - 1) :], "fsdp", 1)
    core = partial(mixer_core, docs=docs, rim_docs=rim_docs, prev_doc=prev_doc)
    conv_w = conv_w_full.astype(jnp.float32)
    conv_b = conv_b_full.astype(jnp.float32)
    empty_state = jnp.zeros((MHEADS, HEAD_M, STATE), jnp.float32)
    (partial_out, local_state), aux = core(
        channels, rim, step_raw, empty_state, conv_w, conv_b, dt_bias, a_log, skip_weight
    )
    decay_total, carry_in, out_map = aux
    identity = (jnp.ones((MHEADS,), jnp.float32), jnp.zeros((MHEADS, HEAD_M, STATE), jnp.float32))
    arrived = prefix((decay_total, local_state), "fsdp", chain, identity)
    state_in = arrived[1]
    mixer_out = partial_out + carry_in[:, :, None] * jnp.einsum(
        "tn,hpn->thp", out_map, state_in, precision=HIGHEST
    )
    gain_m = gain_m_full.astype(jnp.float32)
    mixer_low = gated_norm(mixer_out, gate_raw, gain_m).astype(jnp.bfloat16)
    mixed_patch = patch_sum + product(mixer_low, out_full)
    block, cache = local_forward(byte_states, mixed_patch, local_set, live)
    block_out = block.astype(jnp.bfloat16)
    back_set = (
        lax.all_gather(patch_proj, ("dp", "fsdp"), axis=0, tiled=True),
        lax.all_gather(global_gain, ("dp", "fsdp"), axis=0, tiled=True),
        lax.all_gather(in_proj, ("dp", "fsdp"), axis=0, tiled=True),
        lax.all_gather(conv_weight, ("dp", "fsdp"), axis=0, tiled=True),
        lax.all_gather(conv_bias, ("dp", "fsdp"), axis=0, tiled=True),
        lax.all_gather(mixer_gain, ("dp", "fsdp"), axis=0, tiled=True),
        lax.all_gather(out_proj, ("dp", "fsdp"), axis=0, tiled=True),
        lax.all_gather(attn_gain, ("dp", "fsdp"), axis=0, tiled=True),
        lax.all_gather(qkv_proj, ("dp", "fsdp"), axis=0, tiled=True),
        lax.all_gather(attn_out, ("dp", "fsdp"), axis=0, tiled=True),
        lax.all_gather(ffn_gain, ("dp", "fsdp"), axis=0, tiled=True),
        lax.all_gather(gate_proj, ("dp", "fsdp"), axis=0, tiled=True),
        lax.all_gather(up_proj, ("dp", "fsdp"), axis=0, tiled=True),
        lax.all_gather(down_proj, ("dp", "fsdp"), axis=0, tiled=True),
    )
    global_back = back_set[:7]
    local_back = back_set[7:]
    _, cache = local_forward(byte_states, mixed_patch, local_back, live)
    patch_back, _, in_back, conv_w_back, conv_b_back, _, out_back = global_back
    grad_block = live * out_grad.astype(jnp.float32)
    grad_streams, local_grads = local_backward(grad_block, cache, local_back)
    reduced_local = (
        lax.psum_scatter(local_grads[0], ("dp", "fsdp"), scatter_dimension=0, tiled=True),
        lax.psum_scatter(local_grads[1], ("dp", "fsdp"), scatter_dimension=0, tiled=True),
        lax.psum_scatter(local_grads[2], ("dp", "fsdp"), scatter_dimension=0, tiled=True),
        lax.psum_scatter(local_grads[3], ("dp", "fsdp"), scatter_dimension=0, tiled=True),
        lax.psum_scatter(local_grads[4], ("dp", "fsdp"), scatter_dimension=0, tiled=True),
        lax.psum_scatter(local_grads[5], ("dp", "fsdp"), scatter_dimension=0, tiled=True),
        lax.psum_scatter(local_grads[6], ("dp", "fsdp"), scatter_dimension=0, tiled=True),
    )
    grad_patch_mix = grad_streams.reshape(patches, PATCH, D).sum(axis=1)
    mix_low = grad_patch_mix.astype(jnp.bfloat16)
    grad_out_proj = weight_grad(mixer_low, mix_low)
    grad_mixer_low = input_grad(mix_low, out_back)
    _, norm_back = jax.vjp(gated_norm, mixer_out, gate_raw, gain_m)
    grad_core, grad_gate_raw, grad_mixer_gain = norm_back(grad_mixer_low)
    state_part = jnp.einsum("th,thp,tn->hpn", carry_in, grad_core, out_map, precision=HIGHEST)
    returned = carried_in((decay_total, state_part), "fsdp", chain, identity)
    _, core_back, _ = jax.vjp(
        core,
        channels,
        rim,
        step_raw,
        state_in,
        conv_w_back.astype(jnp.float32),
        conv_b_back.astype(jnp.float32),
        dt_bias,
        a_log,
        skip_weight,
        has_aux=True,
    )
    core_grads = core_back((grad_core, returned[1]))
    (
        grad_channels,
        grad_rim,
        grad_step,
        _,
        grad_conv_w,
        grad_conv_b,
        grad_dt_bias,
        grad_a_log,
        grad_skip,
    ) = core_grads
    rim_grad = shifted(grad_rim, "fsdp", -1)
    cut = patches - (CONV - 1)
    grad_channels = jnp.concatenate([grad_channels[:cut], grad_channels[cut:] + rim_grad], axis=0)
    proj_low = jnp.concatenate([grad_gate_raw, grad_channels, grad_step], axis=1).astype(
        jnp.bfloat16
    )
    grad_in_proj = weight_grad(global_low, proj_low)
    grad_global_norm = input_grad(proj_low, in_back)
    _, norm_back = jax.vjp(rms_scale, patch_sum, gain_g)
    grad_sum_norm, grad_global_gain = norm_back(grad_global_norm)
    sum_low = (grad_patch_mix + grad_sum_norm).astype(jnp.bfloat16)
    grad_patch_proj = weight_grad(patch_rows, sum_low)
    grad_states = grad_streams + input_grad(sum_low, patch_back).reshape(rows, D)
    reduced_global = (
        lax.psum_scatter(grad_patch_proj, ("dp", "fsdp"), scatter_dimension=0, tiled=True),
        lax.psum_scatter(grad_global_gain, ("dp", "fsdp"), scatter_dimension=0, tiled=True),
        lax.psum_scatter(grad_in_proj, ("dp", "fsdp"), scatter_dimension=0, tiled=True),
        lax.psum_scatter(grad_conv_w, ("dp", "fsdp"), scatter_dimension=0, tiled=True),
        lax.psum_scatter(grad_conv_b, ("dp", "fsdp"), scatter_dimension=0, tiled=True),
        lax.psum_scatter(grad_mixer_gain, ("dp", "fsdp"), scatter_dimension=0, tiled=True),
        lax.psum_scatter(grad_out_proj, ("dp", "fsdp"), scatter_dimension=0, tiled=True),
    )
    head_sums = lax.psum((grad_dt_bias, grad_a_log, grad_skip), ("dp", "fsdp"))
    return (
        block_out,
        grad_states,
        reduced_global[0],
        reduced_global[1],
        reduced_global[2],
        reduced_global[3],
        reduced_global[4],
        head_sums[0],
        head_sums[1],
        head_sums[2],
        reduced_global[5],
        reduced_global[6],
        reduced_local[5],
        reduced_local[0],
        reduced_local[1],
        reduced_local[6],
        reduced_local[2],
        reduced_local[3],
        reduced_local[4],
    )


def solution(mesh):
    in_specs = (
        P(("dp", "fsdp"), None),
        P("dp", None),
        P(("dp", "fsdp"), None),
        P(("dp", "fsdp"), None),
        P(("dp", "fsdp")),
        P(("dp", "fsdp"), None),
        P(("dp", "fsdp"), None),
        P(("dp", "fsdp")),
        P(),
        P(),
        P(),
        P(("dp", "fsdp")),
        P(("dp", "fsdp"), None),
        P(("dp", "fsdp")),
        P(("dp", "fsdp"), None),
        P(("dp", "fsdp"), None),
        P(("dp", "fsdp")),
        P(("dp", "fsdp"), None),
        P(("dp", "fsdp"), None),
        P(("dp", "fsdp"), None),
    )
    out_specs = (
        P(("dp", "fsdp"), None),
        P(("dp", "fsdp"), None),
        P(("dp", "fsdp"), None),
        P(("dp", "fsdp")),
        P(("dp", "fsdp"), None),
        P(("dp", "fsdp"), None),
        P(("dp", "fsdp")),
        P(),
        P(),
        P(),
        P(("dp", "fsdp")),
        P(("dp", "fsdp"), None),
        P(("dp", "fsdp")),
        P(("dp", "fsdp"), None),
        P(("dp", "fsdp"), None),
        P(("dp", "fsdp")),
        P(("dp", "fsdp"), None),
        P(("dp", "fsdp"), None),
        P(("dp", "fsdp"), None),
    )
    return jax.shard_map(body, mesh=mesh, in_specs=in_specs, out_specs=out_specs, check_vma=False)
```

profile of v0, /device:TPU:8, one launch (start us, length us, event | category | flops | bytes accessed | tf_op | source)
XLA Modules:
  0.0 2510.4 jit_solution(18113398524673671605)
XLA Ops:
  13.0 41.3 %all-reduce.25 = (bf16[1024]{0:T(1024)(128)(2,1)S(1)}, bf16[1024]{0:T(1024)(128)(2,1)S(1)}, bf16[2304]{0:T(1024)(128)(2,1)S(1)}, bf16[2048]{0:T(1024)(128)(2,1)S(1)}, bf16[1024]{0:T(1024)(128)(2,1)S(1)}) all-reduce(bf16[1024]{0:T(1024)(128)(2,1)S(1)} %dynamic-update-slice.3, ...), channel_id=1, replica_groups=mesh['dp'=8,'fsdp'=4] {'dp','fsdp'}, use_global_device_ids=true, to_apply=%add.16 | all-reduce | flops 7424 | bytes 29696
  60.1 34.6 %all-gather.2 = bf16[32,72,4]{1,2,0:T(4,128)(2,1)S(1)} all-gather(bf16[1,72,4]{1,2,0:T(4,128)(2,1)} %bitcast.191), channel_id=1, replica_groups=mesh['dp'=8,'fsdp'=4] {'dp','fsdp'}, dimensions={0}, use_global_device_ids=true | all-gather | bytes 19008 | tf_op jit(solution)/shard_map/all_gather | solution.py:298
  97.8 29.0 %all-gather.15.cloned.1.call-done = bf16[8192,1024]{1,0:T(8,128)(2,1)} async-done(((bf16[256,1024]{1,0:T(8,128)(2,1)}), bf16[8192,1024]{1,0:T(8,128)(2,1)}) %all-gather.15.cloned.1.call-update) | async-done | bytes 16777232 | tf_op jit(solution)/shard_map/all_gather | solution.py:295
  126.8 8.9 multiply_reduce_fusion.22
  135.7 74.1 %all-gather.17.cloned.1.call-done = bf16[1024,4384]{1,0:T(8,128)(2,1)} async-done(((bf16[32,4384]{1,0:T(8,128)(2,1)}), bf16[1024,4384]{1,0:T(8,128)(2,1)}) %all-gather.17.cloned.1.call-update) | async-done | bytes 8978448 | tf_op jit(solution)/shard_map/all_gather | solution.py:297
  209.8 5.3 fusion.138
  215.2 2.2 collective-permute-start
  219.5 2.9 fusion.10
  229.8 7.0 all-gather.3
  238.7 7.3 all-gather.31.cloned.1.call-done
  246.1 5.4 while.30
  251.5 2.9 fusion.103
  256.9 53.9 %all-gather.19.cloned.1.call-done = bf16[2048,1024]{1,0:T(8,128)(2,1)} async-done(((bf16[64,1024]{1,0:T(8,128)(2,1)}), bf16[2048,1024]{1,0:T(8,128)(2,1)}) %all-gather.19.cloned.1.call-update) | async-done | bytes 4194320 | tf_op jit(solution)/shard_map/all_gather | solution.py:301
  310.8 3.1 convolution_add_fusion.4
  314.1 67.6 %all-gather.21.cloned.1.call-done = bf16[1024,3072]{1,0:T(8,128)(2,1)} async-done(((bf16[32,3072]{1,0:T(8,128)(2,1)}), bf16[1024,3072]{1,0:T(8,128)(2,1)}) %all-gather.21.cloned.1.call-update) | async-done | bytes 6291472 | tf_op jit(solution)/shard_map/all_gather | solution.py:303
  381.8 5.8 convolution_convert_fusion
  387.6 5.3 reshape.360
  392.9 4.3 fusion.145
  397.2 4.6 fusion.147
  401.8 2.8 fusion.4
  406.4 32.1 %all-gather.23.cloned.1.call-done = bf16[1024,1024]{1,0:T(8,128)(2,1)} async-done(((bf16[32,1024]{1,0:T(8,128)(2,1)}), bf16[1024,1024]{1,0:T(8,128)(2,1)}) %all-gather.23.cloned.1.call-update) | async-done | bytes 2097168 | tf_op jit(solution)/shard_map/all_gather | solution.py:304
  438.5 2.6 multiply_reduce_fusion.6
  443.0 75.7 %all-gather.25.cloned.1.call-done = bf16[1024,4096]{1,0:T(8,128)(2,1)} async-done(((bf16[32,4096]{1,0:T(8,128)(2,1)}), bf16[1024,4096]{1,0:T(8,128)(2,1)}) %all-gather.25.cloned.1.call-update) | async-done | bytes 8388624 | tf_op jit(solution)/shard_map/all_gather | solution.py:306
  518.8 7.6 fusion.148
  526.4 71.4 %all-gather.27.cloned.1.call-done = bf16[1024,4096]{1,0:T(8,128)(2,1)} async-done(((bf16[32,4096]{1,0:T(8,128)(2,1)}), bf16[1024,4096]{1,0:T(8,128)(2,1)}) %all-gather.27.cloned.1.call-update) | async-done | bytes 8388624 | tf_op jit(solution)/shard_map/all_gather | solution.py:307
  597.8 7.7 fusion.149
  605.5 71.4 %all-gather.29.cloned.1.call-done = bf16[4096,1024]{1,0:T(8,128)(2,1)} async-done(((bf16[128,1024]{1,0:T(8,128)(2,1)}), bf16[4096,1024]{1,0:T(8,128)(2,1)}) %all-gather.29.cloned.1.call-update) | async-done | bytes 8388624 | tf_op jit(solution)/shard_map/all_gather | solution.py:308
  676.8 9.5 multiply_convert_fusion
  686.4 7.3 fusion.150
  693.8 3.3 multiply_reduce_fusion.1
  701.4 3.5 multiply_reduce_fusion
  709.0 2.4 copy.170
  711.4 5.1 convert_element_type.258
  716.6 6.1 multiply_reduce_fusion.2
  726.3 2.5 multiply_reduce_fusion.17
  730.0 2.9 convolution_convert_fusion.3
  732.9 2.2 multiply_reduce_fusion.9
  736.5 3.7 fusion.56
  749.6 2.7 fusion.15
  754.2 10.4 while.31
  764.7 3.7 fusion.99
  768.4 2.9 fusion.16
  776.0 2.6 multiply_reduce_fusion.14
  791.8 7.0 multiply_reduce_fusion.20
  799.1 13.2 convolution_bitcast_fusion
  813.3 2.7 fusion.60
  817.6 6.5 fusion.95
  824.8 4.7 fusion.90
  831.2 8.3 fusion.152
  841.1 8.2 fusion.153
  851.0 8.2 fusion.80
  860.1 7.7 fusion.87
  869.1 7.2 fusion.9
  876.3 10.8 fusion.151
  888.5 38.6 %all-reduce.28.cloned.1.call-done = (f32[1024]{0:T(1024)}, f32[2304,4]{0,1:T(4,128)}, f32[2304]{0:T(1024)}, f32[32]{0:T(128)}, f32[32]{0:T(128)}, /*index=5*/f32...) async-done(((f32[1024]{0:T(1024)}, f32[2304,4]{0,1:T(4,128)}, f32[2304]{0:T(1024)}, f32[32]{0:T(128)}, f32[32]{0:T(128)}, /*index=5*/f32[32]{0:T(128)}, ...) | async-done | bytes 66960
  934.8 347.8 %reduce-scatter.10.cloned.1.call-done = f32[256,1024]{0,1:T(8,128)} async-done(((f32[8192,1024]{0,1:T(8,128)}), f32[256,1024]{0,1:T(8,128)}) %reduce-scatter.10.cloned.1.call-update) | async-done | bytes 1048592 | tf_op jit(solution)/shard_map/reduce_scatter | solution.py:419
  1282.6 2.5 copy.182
  1285.1 126.9 %reduce-scatter.18.cloned.1.call-done = f32[32,1024]{1,0:T(8,128)} async-done(((f32[1024,1024]{1,0:T(8,128)}), f32[32,1024]{1,0:T(8,128)}) %reduce-scatter.18.cloned.1.call-update) | async-done | bytes 131088 | tf_op jit(solution)/shard_map/reduce_scatter | solution.py:365
  1411.9 177.4 %reduce-scatter.16.cloned.1.call-done = f32[32,3072]{1,0:T(8,128)} async-done(((f32[1024,3072]{1,0:T(8,128)}), f32[32,3072]{1,0:T(8,128)}) %reduce-scatter.16.cloned.1.call-update) | async-done | bytes 393232 | tf_op jit(solution)/shard_map/reduce_scatter | solution.py:364
  1589.3 133.2 %reduce-scatter.14.cloned.1.call-done = f32[64,1024]{1,0:T(8,128)} async-done(((f32[2048,1024]{1,0:T(8,128)}), f32[64,1024]{1,0:T(8,128)}) %reduce-scatter.14.cloned.1.call-update) | async-done | bytes 262160 | tf_op jit(solution)/shard_map/reduce_scatter | solution.py:425
  1722.5 199.9 %reduce-scatter.20.cloned.1.call-done = f32[32,4096]{1,0:T(8,128)} async-done(((f32[1024,4096]{1,0:T(8,128)}), f32[32,4096]{1,0:T(8,128)}) %reduce-scatter.20.cloned.1.call-update) | async-done | bytes 524304 | tf_op jit(solution)/shard_map/reduce_scatter | solution.py:366
  1922.4 186.7 %reduce-scatter.22.cloned.1.call-done = f32[32,4096]{1,0:T(8,128)} async-done(((f32[1024,4096]{1,0:T(8,128)}), f32[32,4096]{1,0:T(8,128)}) %reduce-scatter.22.cloned.1.call-update) | async-done | bytes 524304 | tf_op jit(solution)/shard_map/reduce_scatter | solution.py:367
  2109.1 187.4 %reduce-scatter.24.cloned.1.call-done = f32[128,1024]{1,0:T(8,128)} async-done(((f32[4096,1024]{1,0:T(8,128)}), f32[128,1024]{1,0:T(8,128)}) %reduce-scatter.24.cloned.1.call-update) | async-done | bytes 524304 | tf_op jit(solution)/shard_map/reduce_scatter | solution.py:368
  2296.6 203.8 %reduce-scatter.12.cloned.1.call-done = f32[32,4384]{1,0:T(8,128)} async-done(((f32[1024,4384]{1,0:T(8,128)}), f32[32,4384]{1,0:T(8,128)}) %reduce-scatter.12.cloned.1.call-update) | async-done | bytes 561168 | tf_op jit(solution)/shard_map/reduce_scatter | solution.py:421
  (421 shorter events, 111.1 us)
Async XLA Ops:
  7.2 119.6 %all-gather.15.cloned.1.call-start = ((), (), s32[]{:S(2)}) async-start(), calls=%async_computation.8 | async-start | bytes 17301504 | tf_op jit(solution)/shard_map/all_gather | solution.py:295
  7.9 201.9 %all-gather.17.cloned.1.call-start = ((), (), s32[]{:S(2)}) async-start(), calls=%async_computation.9 | async-start | bytes 9461760 | tf_op jit(solution)/shard_map/all_gather | solution.py:297
  8.7 237.4 %all-gather.31.cloned.1.call-start = ((), (), s32[]{:S(2)}) async-start(), calls=%async_computation.24 | async-start | bytes 2621440 | tf_op jit(solution)/shard_map/all_gather | solution.py:32
  54.3 155.5 %copy-start.53 = (f32[1024]{0:T(1024)}, f32[1024]{0:T(1024)S(1)}, u32[]{:S(2)}) copy-start(f32[1024]{0:T(1024)S(1)} %convert_element_type.227) | copy-start | bytes 12292
  55.6 80.1 %copy-start.7 = (bf16[32,8192]{1,0:T(8,128)(2,1)}, bf16[32,8192]{1,0:T(8,128)(2,1)S(1)}, u32[]{:S(2)}) copy-start(bf16[32,8192]{1,0:T(8,128)(2,1)S(1)} %reshape.356) | copy-start | bytes 1572868
  96.4 121.9 %copy-start.69 = (f32[2304]{0:T(1024)}, f32[2304]{0:T(1024)S(1)}, u32[]{:S(2)}) copy-start(f32[2304]{0:T(1024)S(1)} %get-tuple-element.395) | copy-start | bytes 27652
  96.4 121.9 %copy-start.70 = (f32[2304]{0:T(1024)}, f32[2304]{0:T(1024)S(1)}, u32[]{:S(2)}) copy-start(f32[2304]{0:T(1024)S(1)} %get-tuple-element.396) | copy-start | bytes 27652
  96.4 121.9 %copy-start.71 = (f32[2304]{0:T(1024)}, f32[2304]{0:T(1024)S(1)}, u32[]{:S(2)}) copy-start(f32[2304]{0:T(1024)S(1)} %get-tuple-element.397) | copy-start | bytes 27652
  96.4 121.9 %copy-start.72 = (f32[2304]{0:T(1024)}, f32[2304]{0:T(1024)S(1)}, u32[]{:S(2)}) copy-start(f32[2304]{0:T(1024)S(1)} %get-tuple-element.398) | copy-start | bytes 27652
  97.1 120.3 %copy-start.113 = (f32[32]{0:T(128)}, f32[32]{0:T(128)S(1)}, u32[]{:S(2)}) copy-start(f32[32]{0:T(128)S(1)} %exponential_negate_fusion) | copy-start | bytes 388
  97.8 119.7 %copy-start.92 = (pred[32]{0:T(512)(128)(4,1)}, pred[32]{0:T(512)(128)(4,1)S(1)}, u32[]{:S(2)}) copy-start(pred[32]{0:T(512)(128)(4,1)S(1)} %get-tuple-element.468) | copy-start | bytes 100
  97.8 119.7 %copy-start.106 = (pred[32]{0:T(512)(128)(4,1)}, pred[32]{0:T(512)(128)(4,1)S(1)}, u32[]{:S(2)}) copy-start(pred[32]{0:T(512)(128)(4,1)S(1)} %get-tuple-element.467) | copy-start | bytes 100
  97.8 120.5 %copy-start.103 = (f32[32]{0:T(128)}, f32[32]{0:T(128)S(1)}, u32[]{:S(2)}) copy-start(f32[32]{0:T(128)S(1)} %get-tuple-element.469) | copy-start | bytes 388
  97.8 120.5 %copy-start.104 = (f32[32]{0:T(128)}, f32[32]{0:T(128)S(1)}, u32[]{:S(2)}) copy-start(f32[32]{0:T(128)S(1)} %get-tuple-element.470) | copy-start | bytes 388
  97.8 120.5 %copy-start.105 = (f32[32]{0:T(128)}, f32[32]{0:T(128)S(1)}, u32[]{:S(2)}) copy-start(f32[32]{0:T(128)S(1)} %get-tuple-element.471) | copy-start | bytes 388
  135.7 74.2 %copy-start.117 = (f32[32]{0:T(128)}, f32[32]{0:T(128)S(1)}, u32[]{:S(2)}) copy-start(f32[32]{0:T(128)S(1)} %get-tuple-element.474) | copy-start | bytes 388
  135.7 79.5 %copy-start.79 = (f32[32]{0:T(128)}, f32[32]{0:T(128)S(1)}, u32[]{:S(2)}) copy-start(f32[32]{0:T(128)S(1)} %fusion.128) | copy-start | bytes 388
  215.2 23.5 copy-start.12
  215.2 3.0 collective-permute-start
  217.4 21.3 copy-start.50
  218.0 20.7 copy-start.26
  218.1 18.6 copy-start.63
  218.2 20.5 copy-start.65
  219.2 35.2 %copy-start.24 = (f32[32,2304]{1,0:T(8,128)}, f32[32,2304]{1,0:T(8,128)S(1)}, u32[]{:S(2)}) copy-start(f32[32,2304]{1,0:T(8,128)S(1)} %get-tuple-element.446) | copy-start | bytes 884740
  219.5 34.9 %copy-start.1 = (f32[32,32,64]{2,1,0:T(8,128)}, f32[32,32,64]{2,1,0:T(8,128)S(1)}, u32[]{:S(2)}) copy-start(f32[32,32,64]{2,1,0:T(8,128)S(1)} %reshape.357) | copy-start | bytes 786436
  222.4 88.4 %all-gather.19.cloned.1.call-start = ((), (), s32[]{:S(2)}) async-start(), calls=%async_computation.10 | async-start | bytes 4325376 | tf_op jit(solution)/shard_map/all_gather | solution.py:301
  223.0 158.8 %all-gather.21.cloned.1.call-start = ((), (), s32[]{:S(2)}) async-start(), calls=%async_computation.11 | async-start | bytes 6488064 | tf_op jit(solution)/shard_map/all_gather | solution.py:303
  223.6 214.9 %all-gather.23.cloned.1.call-start = ((), (), s32[]{:S(2)}) async-start(), calls=%async_computation.12 | async-start | bytes 2162688 | tf_op jit(solution)/shard_map/all_gather | solution.py:304
  224.2 294.6 %all-gather.25.cloned.1.call-start = ((), (), s32[]{:S(2)}) async-start(), calls=%async_computation.13 | async-start | bytes 8650752 | tf_op jit(solution)/shard_map/all_gather | solution.py:306
  224.9 372.9 %all-gather.27.cloned.1.call-start = ((), (), s32[]{:S(2)}) async-start(), calls=%async_computation.14 | async-start | bytes 8650752 | tf_op jit(solution)/shard_map/all_gather | solution.py:307
  225.7 451.2 %all-gather.29.cloned.1.call-start = ((), (), s32[]{:S(2)}) async-start(), calls=%async_computation.15 | async-start | bytes 8650752 | tf_op jit(solution)/shard_map/all_gather | solution.py:308
  226.4 527.8 %all-gather.33.cloned.1.call-start = ((), (), s32[]{:S(2)}) async-start(), calls=%async_computation.25 | async-start | bytes 2621440 | tf_op jit(solution)/shard_map/all_gather | solution.py:55
  229.6 16.4 copy-start.108
  229.7 16.4 copy-start.83
  229.8 16.3 copy-start.85
  236.8 17.7 copy-start.57
  236.9 9.1 copy-start.81
  246.0 8.4 copy-start.52
  246.0 8.4 copy-start.115
  254.5 59.4 %copy-start.13 = (f32[32,32,64]{2,0,1:T(8,128)}, f32[32,32,64]{2,0,1:T(8,128)S(1)}, u32[]{:S(2)}) copy-start(f32[32,32,64]{2,0,1:T(8,128)S(1)} %fusion.103) | copy-start | bytes 786436
  255.4 58.5 %copy-start.3 = (bf16[256,1024]{1,0:T(8,128)(2,1)S(1)}, bf16[256,1024]{1,0:T(8,128)(2,1)}, u32[]{:S(2)}) copy-start(bf16[256,1024]{1,0:T(8,128)(2,1)} %param.24) | copy-start | bytes 1572868
  255.6 132.0 %copy-start.27 = (f32[32,2048]{1,0:T(8,128)}, f32[32,2048]{1,0:T(8,128)S(1)}, u32[]{:S(2)}) copy-start(f32[32,2048]{1,0:T(8,128)S(1)} %reshape.358) | copy-start | bytes 786436
  255.6 126.2 %copy-start.66 = (f32[1024]{0:T(1024)S(1)}, f32[1024]{0:T(1024)}, u32[]{:S(2)}) copy-start(f32[1024]{0:T(1024)} %convert_element_type.241) | copy-start | bytes 12292
  256.8 53.9 %copy-start.119 = (f32[32]{0:T(128)}, f32[32]{0:T(128)S(1)}, u32[]{:S(2)}) copy-start(f32[32]{0:T(128)S(1)} %get-tuple-element.442) | copy-start | bytes 388
  256.9 130.7 %copy-start.94 = (f32[32]{0:T(128)}, f32[32]{0:T(128)S(1)}, u32[]{:S(2)}) copy-start(f32[32]{0:T(128)S(1)} %fusion.129) | copy-start | bytes 388
  313.9 124.6 %copy-start.29 = (f32[32,1024]{1,0:T(8,128)}, f32[32,1024]{1,0:T(8,128)S(1)}, u32[]{:S(2)}) copy-start(f32[32,1024]{1,0:T(8,128)S(1)} %convolution_add_fusion.4) | copy-start | bytes 393220
  314.1 73.5 %copy-start.99 = (f32[256]{0:T(256)}, f32[256]{0:T(256)S(1)}, u32[]{:S(2)}) copy-start(f32[256]{0:T(256)S(1)} %multiply_reduce_fusion.7) | copy-start | bytes 3076
  314.1 73.4 %copy-start.87 = (f32[256]{0:T(256)}, f32[256]{0:T(256)S(1)}, u32[]{:S(2)}) copy-start(f32[256]{0:T(256)S(1)} %fusion.119) | copy-start | bytes 3076
  441.1 252.6 %copy-start.18 = (f32[256,1024]{1,0:T(8,128)}, f32[256,1024]{1,0:T(8,128)S(1)}, u32[]{:S(2)}) copy-start(f32[256,1024]{1,0:T(8,128)S(1)} %get-tuple-element.479) | copy-start | bytes 3145732
  443.0 154.8 %copy-start.10 = (bf16[256,1024]{1,0:T(8,128)(2,1)}, bf16[256,1024]{1,0:T(8,128)(2,1)S(1)}, u32[]{:S(2)}) copy-start(bf16[256,1024]{1,0:T(8,128)(2,1)S(1)} %multiply_convert_fusion.6) | copy-start | bytes 1572868
  716.6 7.7 copy-start
  732.9 194.2 %all-reduce.28.cloned.1.call-start = ((), (), s32[]{:S(2)}) async-start(), calls=%async_computation.26 | async-start | bytes 142336
  782.1 8.7 collective-permute-start.1
  788.0 10.8 copy-start.73
  799.0 13.3 copy-start.48
  799.0 483.5 %reduce-scatter.10.cloned.1.call-start = ((), (), s32[]{:S(2)}) async-start(), calls=%async_computation.16 | async-start | bytes 34603008 | tf_op jit(solution)/shard_map/reduce_scatter | solution.py:419
  812.3 599.7 %reduce-scatter.18.cloned.1.call-start = ((), (), s32[]{:S(2)}) async-start(), calls=%async_computation.20 | async-start | bytes 4325376 | tf_op jit(solution)/shard_map/reduce_scatter | solution.py:365
  816.1 773.2 %reduce-scatter.16.cloned.1.call-start = ((), (), s32[]{:S(2)}) async-start(), calls=%async_computation.19 | async-start | bytes 12976128 | tf_op jit(solution)/shard_map/reduce_scatter | solution.py:364
  824.1 898.4 %reduce-scatter.14.cloned.1.call-start = ((), (), s32[]{:S(2)}) async-start(), calls=%async_computation.18 | async-start | bytes 8650752 | tf_op jit(solution)/shard_map/reduce_scatter | solution.py:425
  829.5 1093.0 %reduce-scatter.20.cloned.1.call-start = ((), (), s32[]{:S(2)}) async-start(), calls=%async_computation.21 | async-start | bytes 17301504 | tf_op jit(solution)/shard_map/reduce_scatter | solution.py:366
  839.5 1269.6 %reduce-scatter.22.cloned.1.call-start = ((), (), s32[]{:S(2)}) async-start(), calls=%async_computation.22 | async-start | bytes 17301504 | tf_op jit(solution)/shard_map/reduce_scatter | solution.py:367
  849.3 1447.2 %reduce-scatter.24.cloned.1.call-start = ((), (), s32[]{:S(2)}) async-start(), calls=%async_computation.23 | async-start | bytes 17301504 | tf_op jit(solution)/shard_map/reduce_scatter | solution.py:368
  859.3 1641.1 %reduce-scatter.12.cloned.1.call-start = ((), (), s32[]{:S(2)}) async-start(), calls=%async_computation.17 | async-start | bytes 18923520 | tf_op jit(solution)/shard_map/reduce_scatter | solution.py:421
  876.3 11.1 copy-start.20
  (80 other events, 289.0 us)
Sparse Core Ops, SparseCore 0:
  10.9 115.8 all-gather.14
  129.6 80.1 all-gather.16
  222.6 23.4 all-gather.30
  248.8 61.9 all-gather.18
  313.5 68.2 all-gather.20
  384.5 53.9 all-gather.22
  441.4 77.3 all-gather.24
  521.6 76.1 all-gather.26
  600.7 76.1 all-gather.28
  733.0 21.1 all-gather.32
  799.1 127.9 all-reduce.27
  929.4 353.1 reduce-scatter.9
  1285.5 126.3 reduce-scatter.17
  1419.4 169.8 reduce-scatter.15
  1592.0 130.4 reduce-scatter.13
  1725.2 197.1 reduce-scatter.19
  1925.2 183.9 reduce-scatter.21
  2111.8 184.6 reduce-scatter.23
  2299.4 200.8 reduce-scatter.11
where the time goes:
time: 2520 us; the launch traced here: 2510 us
  waiting for transfers between devices  2090 us (83%)
  matrix products  196 us (8%)
  blocking collectives  82.9 us (3%)
  local copies, waits for them, and re-layouts  70.8 us (3%)
  other arithmetic  46.1 us (2%)
    reduce_scatter x1, waiting for transfers between devices, body(): lax.psum_scatter(grad_patch_proj, ('dp', 'fsdp'), scatter_dimension=0, ti...  348 us
    reduce_scatter x1, waiting for transfers between devices, body(): lax.psum_scatter(grad_in_proj, ('dp', 'fsdp'), scatter_dimension=0, tiled...  204 us
    reduce_scatter x1, waiting for transfers between devices, body(): lax.psum_scatter(local_grads[2], ('dp', 'fsdp'), scatter_dimension=0, til...  200 us
    reduce_scatter x1, waiting for transfers between devices, body(): lax.psum_scatter(local_grads[4], ('dp', 'fsdp'), scatter_dimension=0, til...  187 us
    reduce_scatter x1, waiting for transfers between devices, body(): lax.psum_scatter(local_grads[3], ('dp', 'fsdp'), scatter_dimension=0, til...  187 us
    reduce_scatter x1, waiting for transfers between devices, body(): lax.psum_scatter(local_grads[0], ('dp', 'fsdp'), scatter_dimension=0, til...  177 us
    reduce_scatter x1, waiting for transfers between devices, body(): lax.psum_scatter(grad_out_proj, ('dp', 'fsdp'), scatter_dimension=0, tile...  133 us
    reduce_scatter x1, waiting for transfers between devices, body(): lax.psum_scatter(local_grads[1], ('dp', 'fsdp'), scatter_dimension=0, til...  127 us
  transfers between devices with their start and end apart: 21, of which 20 were waited for; matrix products, arithmetic and copies ran while one was open for 8% of the time, Pallas kernels for 0%

commit v1 on v0

--- a/solution.py
+++ b/solution.py
@@ -142,7 +142,8 @@
     out_map = activated[:, DI + STATE :]
     step_size = jax.nn.softplus(step_raw + dt_bias[None, :])
     rate = -jnp.exp(a_log)
-    cumulative = jnp.cumsum(step_size * rate[None, :], axis=0)
+    lower = jnp.tril(jnp.ones((count, count), jnp.float32))
+    cumulative = jnp.dot(lower, step_size * rate[None, :], precision=HIGHEST)
     places = jnp.arange(count, dtype=jnp.int32)
     keep = ((places[:, None] >= places[None, :]) & (docs[:, None] == docs[None, :]))[:, :, None]
     spread = cumulative[:, None, :] - cumulative[None, :, :]
@@ -448,6 +449,456 @@
     )
 
 
+AX = ("dp", "fsdp")
+BC = 2 * STATE
+OWN = 2 * HEAD_M + 1
+
+
+class Grid:
+    def __init__(self, dp, fsdp):
+        self.depth, self.count = dp // 2, dp * fsdp
+        dp_at, fs_at = lax.axis_index("dp"), lax.axis_index("fsdp")
+        self.z, self.x, self.y, self.c = dp_at // 2, dp_at % 2, fs_at // 2, fs_at % 2
+        self.at = {"z": self.z, "x": self.x, "y": self.y, "c": self.c}
+
+    def route(self, dim, step=1):
+        pairs = []
+        for i in range(self.count):
+            z, x, y, c = i // 8, i // 4 % 2, i // 2 % 2, i % 2
+            if dim == "z":
+                z = (z + step) % self.depth
+            elif dim == "x":
+                x = 1 - x
+            elif dim == "y":
+                y = 1 - y
+            else:
+                c = 1 - c
+            pairs.append((i, z * 8 + x * 4 + y * 2 + c))
+        return pairs
+
+    def send(self, block, dim, step=1):
+        return lax.ppermute(block, AX, self.route(dim, step))
+
+
+def put(whole, part, place):
+    return lax.dynamic_update_slice(whole, part, [jnp.asarray(p, jnp.int32) for p in place])
+
+
+def gather_stream(grid, own, order):
+    rows, n = own.shape
+    pieces = [(own[None], {})]
+    zs = 1
+    for dim in order:
+        if dim == "z":
+            stacked = jnp.stack([p for p, _ in pieces], axis=0)
+            blocks = [stacked]
+            for _ in range(grid.depth - 1):
+                blocks.append(grid.send(blocks[-1], "z"))
+            whole = jnp.zeros((len(pieces), grid.depth, rows, n), own.dtype)
+            for k, block in enumerate(blocks):
+                whole = put(whole, block, (0, (grid.z - k) % grid.depth, 0, 0))
+            pieces = [(whole[i], at) for i, (_, at) in enumerate(pieces)]
+        else:
+            pieces = pieces + [(grid.send(p, dim), {**at, dim: True}) for p, at in pieces]
+    out = jnp.zeros((grid.depth, 2, 2, 2, rows, n), own.dtype)
+    for piece, at in pieces:
+        place = [1 - grid.at[d] if d in at else grid.at[d] for d in "xyc"]
+        out = put(out, piece[:, None, None, None], (0, *place, 0, 0))
+    return out.reshape(grid.count, rows, n)
+
+
+def pick(part, where, axis):
+    return lax.dynamic_index_in_dim(part, where, axis, keepdims=False)
+
+
+def scatter_stream(grid, part, order):
+    low = jnp.bfloat16
+    dims = ["z", "x", "y"]
+    for dim in order:
+        axis = dims.index(dim)
+        here = grid.at[dim]
+        if dim == "z":
+            total = None
+            for k in range(1, grid.depth + 1):
+                mine = pick(part, (here - k) % grid.depth, axis).astype(jnp.float32)
+                total = mine if total is None else mine + total.astype(jnp.float32)
+                if k < grid.depth:
+                    total = grid.send(total.astype(low), "z")
+            part = total
+        else:
+            arrived = grid.send(pick(part, 1 - here, axis).astype(low), dim)
+            part = pick(part, here, axis).astype(jnp.float32) + arrived.astype(jnp.float32)
+        dims.pop(axis)
+    return part
+
+
+def gather_small(grid, own):
+    rows, n = own.shape
+    column = jnp.zeros((grid.depth, rows, n), own.dtype)
+    for k in range(grid.depth):
+        block = own if k == 0 else grid.send(own, "z", k)
+        column = put(column, block[None], ((grid.z - k) % grid.depth, 0, 0))
+    half = n // 2
+    plane = jnp.zeros((grid.depth, 2, 2, rows, n), own.dtype)
+    for first, second, at in (("x", "y", 0), ("y", "x", half)):
+        mine = column[:, :, at : at + half]
+        both = jnp.stack([mine, grid.send(mine, first)])
+        far = grid.send(both, second)
+        for i in range(2):
+            for j, block in enumerate((both[i], far[i])):
+                place = {first: grid.at[first] ^ i, second: grid.at[second] ^ j}
+                plane = put(plane, block[:, None, None], (0, place["x"], place["y"], 0, at))
+    other = grid.send(plane, "c")
+    pair = jnp.where(grid.c == 0, jnp.stack([plane, other], 3), jnp.stack([other, plane], 3))
+    return pair.reshape(grid.count * rows, n)
+
+
+def scatter_small(grid, part):
+    low = jnp.bfloat16
+    n = part.shape[1]
+    part = part.reshape(grid.depth, 2, 2, 2, -1, n)
+    arrived = grid.send(pick(part, 1 - grid.c, 3).astype(low), "c")
+    part = pick(part, grid.c, 3) + arrived.astype(jnp.float32)
+    half = n // 2
+    sums = []
+    for order, at in (("yx", 0), ("xy", half)):
+        piece = part[..., at : at + half]
+        dims = ["z", "x", "y"]
+        for dim in order:
+            axis = dims.index(dim)
+            arrived = grid.send(pick(piece, 1 - grid.at[dim], axis).astype(low), dim)
+            piece = pick(piece, grid.at[dim], axis) + arrived.astype(jnp.float32)
+            dims.pop(axis)
+        sums.append(piece)
+    column = jnp.concatenate(sums, axis=-1)
+    total = pick(column, grid.z, 0)
+    for k in range(1, grid.depth):
+        block = pick(column, (grid.z + k) % grid.depth, 0).astype(low)
+        total = total + grid.send(block, "z", k).astype(jnp.float32)
+    return total
+
+
+def exchange(blocks):
+    return lax.all_to_all(blocks, AX, 0, 0, tiled=False)
+
+
+def causal_taps(channels, weight, bias, docs):
+    slots, count = docs.shape
+    padded = jnp.pad(channels, ((0, 0), (CONV - 1, 0), (0, 0)))
+    padded_docs = jnp.pad(docs, ((0, 0), (CONV - 1, 0)), constant_values=-1)
+    total = bias[None, None, :]
+    for k in range(CONV):
+        same = (padded_docs[:, k : k + count] == docs).astype(jnp.float32)
+        total = total + padded[:, k : k + count] * weight[:, k][None, None, :] * same[:, :, None]
+    return total
+
+
+def head_core(channels, maps, step_raw, conv_w, conv_b, maps_w, maps_b, dt_bias, a_log, skip, docs):
+    count = docs.shape[1]
+    inputs = jax.nn.silu(causal_taps(channels, conv_w, conv_b, docs))
+    both = jax.nn.silu(causal_taps(maps, maps_w, maps_b, docs))
+    in_map, out_map = both[..., :STATE], both[..., STATE:]
+    step_size = jax.nn.softplus(step_raw + dt_bias)
+    lower = jnp.tril(jnp.ones((count, count), jnp.float32))
+    cumulative = jnp.dot(step_size * -jnp.exp(a_log), lower.T, precision=HIGHEST)
+    keep = (lower > 0)[None] & (docs[:, :, None] == docs[:, None, :])
+    spread = cumulative[:, :, None] - cumulative[:, None, :]
+    decay = jnp.where(keep, jnp.exp(jnp.where(keep, spread, 0.0)), 0.0)
+    inner = jnp.einsum("gtn,gsn->gts", out_map, in_map, precision=HIGHEST)
+    mixing = decay * inner * step_size[:, None, :]
+    return jnp.einsum("gts,gsp->gtp", mixing, inputs, precision=HIGHEST) + skip * inputs
+
+
+def split_heads(rows_by_cols):
+    rows = rows_by_cols.shape[0]
+    return rows_by_cols.reshape(rows // 128, 128, -1, HEAD).transpose(2, 0, 1, 3)
+
+
+def join_heads(heads):
+    return heads.transpose(1, 2, 0, 3).reshape(heads.shape[1] * heads.shape[2], -1)
+
+
+def patch_mask():
+    places = jnp.arange(128)
+    return (places[:, None] >= places[None, :]) & (places[:, None] // PATCH == places[None, :] // PATCH)
+
+
+def dot_f32(spec, a, b):
+    return jnp.einsum(spec, a, b, preferred_element_type=jnp.float32)
+
+
+def fast_body(
+    depth_fsdp,
+    byte_states,
+    doc_lengths,
+    out_grad,
+    patch_proj,
+    global_gain,
+    in_proj,
+    conv_weight,
+    conv_bias,
+    dt_bias,
+    a_log,
+    skip_weight,
+    mixer_gain,
+    out_proj,
+    attn_gain,
+    qkv_proj,
+    attn_out,
+    ffn_gain,
+    gate_proj,
+    up_proj,
+    down_proj,
+):
+    f32, low = jnp.float32, jnp.bfloat16
+    grid = Grid(*depth_fsdp)
+    n_dev = grid.count
+    me = lax.axis_index("dp") * depth_fsdp[1] + lax.axis_index("fsdp")
+    rows = byte_states.shape[0]
+    patches = rows // PATCH
+    slots = depth_fsdp[0]
+    slot_patches = patches * depth_fsdp[1]
+
+    vector = jnp.concatenate(
+        [
+            global_gain,
+            mixer_gain,
+            attn_gain,
+            ffn_gain,
+            conv_weight.reshape(-1),
+            conv_bias,
+            doc_lengths.reshape(-1).astype(low),
+        ]
+    )
+    shard_rows = in_proj.shape[0]
+    tail = -(-vector.shape[0] // BC)
+    vector = jnp.pad(vector, (0, tail * BC - vector.shape[0])).reshape(tail, BC)
+    small = jnp.concatenate([in_proj[:, 2 * DI : 2 * DI + BC], vector], axis=0)
+    small = gather_small(grid, small).reshape(n_dev, shard_rows + tail, BC)
+    maps_proj = small[:, :shard_rows].reshape(D, BC)
+    flat = small[:, shard_rows:].reshape(n_dev, -1)
+    cuts, at = [], 0
+    for width in (D, DI, D, D, CONV_CH * CONV, CONV_CH, n_dev * 2):
+        width //= n_dev
+        cuts.append(flat[:, at : at + width])
+        at += width
+    gain_g, gain_m, gain_a, gain_f = (cut.reshape(-1).astype(f32) for cut in cuts[:4])
+    conv_w = cuts[4].reshape(CONV_CH, CONV).astype(f32)
+    conv_b = cuts[5].reshape(CONV_CH).astype(f32)
+    lengths = cuts[6].reshape(slots, depth_fsdp[1], 2)[:, 0].astype(jnp.int32)
+    places = jnp.arange(slot_patches, dtype=jnp.int32)[None, :]
+    first_end = lengths[:, :1]
+    docs = (places >= first_end).astype(jnp.int32) + (places >= first_end + lengths[:, 1:]).astype(jnp.int32)
+    my_docs = lax.dynamic_slice(docs.reshape(-1), (me * patches,), (patches,))
+    live = jnp.repeat((my_docs < 2).astype(f32), PATCH)[:, None]
+
+    def gathered(shard, order):
+        return gather_stream(grid, shard, order).reshape(-1, shard.shape[1])
+
+    patch_bytes = byte_states.reshape(patches, n_dev, -1).transpose(1, 0, 2)
+    all_bytes = exchange(patch_bytes).reshape(n_dev * patches, -1)
+    heads_of = lambda cols: cols.reshape(shard_rows, MHEADS, -1)
+    own_cols = jnp.concatenate(
+        [heads_of(in_proj[:, :DI]), heads_of(in_proj[:, DI : 2 * DI]), heads_of(in_proj[:, 2 * DI + BC :])],
+        axis=2,
+    ).transpose(1, 0, 2)
+    own_proj = exchange(own_cols).reshape(D, OWN)
+
+    qk = gathered(qkv_proj[:, : 2 * D], "zxyc")
+    vals = gathered(qkv_proj[:, 2 * D :], "zyxc")
+    attn_o = gathered(attn_out, "zyxc")
+    gate_w = gathered(gate_proj, "zxyc")
+    up_w = gathered(up_proj, "zyxc")
+    down_a = gathered(down_proj[:, : D // 2], "xyzc")
+    down_b = gathered(down_proj[:, D // 2 :], "yxzc")
+
+    patch_sum = scatter_small(grid, product(all_bytes, patch_proj))
+    global_low = rms_scale(patch_sum, gain_g).astype(low)
+    global_all = gather_small(grid, global_low)
+    own = product(global_all, own_proj)
+    maps = product(global_all, maps_proj)
+    by_slot = lambda cols: cols.reshape(slots, slot_patches, -1)
+    gate_raw = own[:, :HEAD_M]
+    mine = lambda vec, width: lax.dynamic_slice_in_dim(vec, me * width, width, 0)
+    core_args = (
+        by_slot(own[:, HEAD_M : 2 * HEAD_M]),
+        by_slot(maps),
+        by_slot(own[:, 2 * HEAD_M :])[..., 0],
+        mine(conv_w, HEAD_M),
+        mine(conv_b, HEAD_M),
+        conv_w[DI:],
+        conv_b[DI:],
+        mine(dt_bias, 1),
+        mine(a_log, 1),
+        mine(skip_weight, 1),
+    )
+    core, core_back = jax.vjp(partial(head_core, docs=docs), *core_args)
+    core = core.reshape(-1, HEAD_M)
+    sig_m = jax.nn.sigmoid(gate_raw)
+    gated = core * gate_raw * sig_m
+    my_gain = mine(gain_m, HEAD_M)[None]
+    mixer_part = product((gated * my_gain).astype(low), out_proj)
+    squares = jnp.sum(gated * gated, axis=1, keepdims=True)
+    mixed = scatter_small(grid, jnp.concatenate([mixer_part, jnp.pad(squares, ((0, 0), (0, 127)))], axis=1))
+    raw_mixed = mixed[:, :D]
+    mixer_r = lax.rsqrt(mixed[:, D : D + 1] / DI + EPSILON)
+    mixed_patch = patch_sum + raw_mixed * mixer_r
+
+    streams = byte_states.astype(f32) + jnp.repeat(mixed_patch, PATCH, axis=0)
+    normed = rms_scale(streams, gain_a).astype(low)
+    queries, key_rows = jnp.split(product(normed, qk).astype(low), 2, axis=1)
+    queries, key_rows = split_heads(queries), split_heads(key_rows)
+    value_rows = split_heads(product(normed, vals).astype(low))
+    scale = HEAD ** (-0.5)
+    scores = dot_f32("hbid,hbjd->hbij", queries, key_rows) * scale
+    attn_weights = jax.nn.softmax(jnp.where(patch_mask(), scores, -1e30), axis=-1)
+    attn_low = attn_weights.astype(low)
+    mixed_heads = join_heads(dot_f32("hbij,hbjd->hbid", attn_low, value_rows).astype(low))
+    attended = streams + product(mixed_heads, attn_o)
+    ffn_low = rms_scale(attended, gain_f).astype(low)
+    gate = product(ffn_low, gate_w)
+    upward = product(ffn_low, up_w)
+    sigma = jax.nn.sigmoid(gate)
+    hidden = (gate * sigma * upward).astype(low)
+    ffn_out = jnp.concatenate([product(hidden, down_a), product(hidden, down_b)], axis=1)
+    block_out = (live * (attended + ffn_out)).astype(low)
+
+    def plane_of(act, which):
+        cols = act.reshape(rows, n_dev // 2, 2, -1)
+        return pick(cols, which, 2).reshape(rows, -1)
+
+    def scattered(act, grad, order):
+        there = weight_grad(plane_of(act, 1 - grid.c), grad).astype(low)
+        arrived = grid.send(there, "c")
+        part = (weight_grad(plane_of(act, grid.c), grad) + arrived.astype(f32)).astype(low)
+        part = part.reshape(grid.depth, 2, 2, -1, grad.shape[1])
+        return scatter_stream(grid, part, order)
+
+    grad_block = live * out_grad.astype(f32)
+    down_low = grad_block.astype(low)
+    grad_down = jnp.concatenate(
+        [scattered(hidden, down_low[:, : D // 2], "zyx"), scattered(hidden, down_low[:, D // 2 :], "zxy")],
+        axis=1,
+    )
+    grad_hidden = input_grad(down_low[:, : D // 2], down_a) + input_grad(down_low[:, D // 2 :], down_b)
+    grad_gate_low = (grad_hidden * upward * sigma * (1.0 + gate * (1.0 - sigma))).astype(low)
+    grad_up_low = (grad_hidden * gate * sigma).astype(low)
+    grad_gate = scattered(ffn_low, grad_gate_low, "yxz")
+    grad_up = scattered(ffn_low, grad_up_low, "xyz")
+    grad_ffn_in = input_grad(grad_gate_low, gate_w) + input_grad(grad_up_low, up_w)
+    _, norm_back = jax.vjp(rms_scale, attended, gain_f)
+    grad_attended_norm, grad_gain_f = norm_back(grad_ffn_in)
+    grad_attended = grad_block + grad_attended_norm
+    attn_grad_low = grad_attended.astype(low)
+    grad_attn_out = scattered(mixed_heads, attn_grad_low, "xyz")
+    grad_mixed = split_heads(input_grad(attn_grad_low, attn_o).astype(low))
+    grad_values = dot_f32("hbij,hbid->hbjd", attn_low, grad_mixed)
+    grad_weights = dot_f32("hbid,hbjd->hbij", grad_mixed, value_rows)
+    grad_scores = attn_weights * (
+        grad_weights - jnp.sum(attn_weights * grad_weights, axis=-1, keepdims=True)
+    )
+    scores_low = grad_scores.astype(low)
+    grad_queries = dot_f32("hbij,hbjd->hbid", scores_low, key_rows) * scale
+    grad_keys = dot_f32("hbij,hbid->hbjd", scores_low, queries) * scale
+    grad_qk = jnp.concatenate([join_heads(grad_queries.astype(low)), join_heads(grad_keys.astype(low))], axis=1)
+    grad_v = join_heads(grad_values.astype(low))
+    grad_qkv = jnp.concatenate(
+        [scattered(normed, grad_qk, "yxz"), scattered(normed, grad_v, "xyz")], axis=1
+    )
+    grad_normed = input_grad(grad_qk, qk) + input_grad(grad_v, vals)
+    _, norm_back = jax.vjp(rms_scale, streams, gain_a)
+    grad_streams_norm, grad_gain_a = norm_back(grad_normed)
+    grad_streams = grad_attended + grad_streams_norm
+
+    grad_patch_mix = grad_streams.reshape(patches, PATCH, D).sum(axis=1)
+    mix_low = grad_patch_mix.astype(low)
+    along = jnp.sum(mix_low.astype(f32) * raw_mixed, axis=1, keepdims=True)
+    pair = jnp.concatenate([mixer_r, along], axis=1)
+    pair_high = pair.astype(low)
+    pair_rest = (pair - pair_high.astype(f32)).astype(low)
+    extra = jnp.pad(jnp.concatenate([pair_high, pair_rest], axis=1), ((0, 0), (0, 124)))
+    mix_all = gather_small(grid, jnp.concatenate([mix_low, extra], axis=1))
+    extra = mix_all[:, D : D + 4].astype(f32)
+    r_all, along_all = extra[:, 0:1] + extra[:, 2:3], extra[:, 1:2] + extra[:, 3:4]
+    mix_all = mix_all[:, :D]
+    grad_out_proj = weight_grad((gated * r_all * my_gain).astype(low), mix_all)
+    back_m = input_grad(mix_all, out_proj)
+    grad_gain_m = jnp.sum(back_m * gated * r_all, axis=0)
+    grad_gated = r_all * my_gain * back_m - gated * (r_all * r_all * r_all * along_all / DI)
+    grad_core = grad_gated * gate_raw * sig_m
+    grad_gate_raw = grad_gated * core * sig_m * (1.0 + gate_raw * (1.0 - sig_m))
+    (d_chan, d_maps, d_step, d_cw, d_cb, d_mw, d_mb, d_dt, d_alog, d_skip) = core_back(by_slot(grad_core))
+    d_own = jnp.concatenate(
+        [grad_gate_raw, d_chan.reshape(-1, HEAD_M), d_step.reshape(-1, 1)], axis=1
+    ).astype(low)
+    d_maps = d_maps.reshape(-1, BC).astype(low)
+    grad_norm = scatter_small(grid, input_grad(d_own, own_proj) + input_grad(d_maps, maps_proj))
+    grad_own_cols = weight_grad(global_all, d_own)
+    grad_maps_cols = weight_grad(global_all, d_maps)
+    _, norm_back = jax.vjp(rms_scale, patch_sum, gain_g)
+    grad_sum_norm, grad_gain_g = norm_back(grad_norm)
+    sum_low = (grad_patch_mix + grad_sum_norm).astype(low)
+    sum_all = gather_small(grid, sum_low)
+    grad_patch_proj = weight_grad(all_bytes, sum_all)
+    back_bytes = input_grad(sum_all, patch_proj).astype(low).reshape(n_dev, patches, -1)
+    back_bytes = exchange(back_bytes).transpose(1, 0, 2).reshape(rows, D)
+    grad_states = grad_streams + back_bytes.astype(f32)
+
+    taps = jnp.zeros((CONV_CH, CONV + 1), f32)
+    taps = put(taps, jnp.concatenate([d_cw, d_cb[:, None]], axis=1), (me * HEAD_M, 0))
+    taps = put(taps, jnp.concatenate([d_mw, d_mb[:, None]], axis=1), (DI, 0))
+    sums = [taps.reshape(n_dev, -1)]
+    sums += [g.reshape(n_dev, -1) for g in (grad_gain_g, grad_gain_a, grad_gain_f)]
+    heads = jnp.zeros((3, MHEADS), f32)
+    heads = put(heads, jnp.stack([d_dt, d_alog, d_skip]), (0, me)).reshape(1, -1)
+    sums += [jnp.broadcast_to(heads, (n_dev, 3 * MHEADS))]
+    sums = jnp.concatenate(sums, axis=1)
+    width = sums.shape[1]
+    extra_cols = -(-width // shard_rows)
+    sums = jnp.pad(sums, ((0, 0), (0, extra_cols * shard_rows - width))).reshape(n_dev, shard_rows, extra_cols)
+    parcel = jnp.concatenate(
+        [
+            grad_own_cols.reshape(n_dev, shard_rows, OWN),
+            grad_maps_cols.reshape(n_dev, shard_rows, BC),
+            sums,
+        ],
+        axis=2,
+    ).astype(low)
+    parcel = exchange(parcel).astype(f32)
+    side = lambda a, b: parcel[:, :, a:b].transpose(1, 0, 2).reshape(shard_rows, -1)
+    summed = jnp.sum(parcel[:, :, OWN:], axis=0)
+    grad_in_proj = jnp.concatenate(
+        [side(0, HEAD_M), side(HEAD_M, 2 * HEAD_M), summed[:, :BC], side(2 * HEAD_M, OWN)], axis=1
+    )
+    flat = summed[:, BC:].reshape(-1)
+    taps = flat[: CONV_CH * (CONV + 1) // n_dev].reshape(-1, CONV + 1)
+    at = CONV_CH * (CONV + 1) // n_dev
+    grad_gain_g, grad_gain_a, grad_gain_f = (flat[at + i * D // n_dev : at + (i + 1) * D // n_dev] for i in range(3))
+    at += 3 * D // n_dev
+    heads = flat[at : at + 3 * MHEADS].reshape(3, MHEADS)
+    return (
+        block_out,
+        grad_states,
+        grad_patch_proj,
+        grad_gain_g,
+        grad_in_proj,
+        taps[:, :CONV],
+        taps[:, CONV],
+        heads[0],
+        heads[1],
+        heads[2],
+        grad_gain_m,
+        grad_out_proj,
+        grad_gain_a,
+        grad_qkv,
+        grad_attn_out,
+        grad_gain_f,
+        grad_gate,
+        grad_up,
+        grad_down,
+    )
+
+
 def solution(mesh):
     in_specs = (
         P(("dp", "fsdp"), None),
@@ -492,4 +943,7 @@
         P(("dp", "fsdp"), None),
         P(("dp", "fsdp"), None),
     )
-    return jax.shard_map(body, mesh=mesh, in_specs=in_specs, out_specs=out_specs, check_vma=False)
+    dp, fsdp = mesh.shape["dp"], mesh.shape["fsdp"]
+    fast = dp * fsdp == MHEADS and fsdp == 4
+    chosen = partial(fast_body, (dp, fsdp)) if fast else body
+    return jax.shard_map(chosen, mesh=mesh, in_specs=in_specs, out_specs=out_specs, check_vma=False)

time: 2520 us -> 1120 us (0.44)
  waiting for transfers between devices: 2090 us -> 465 us
  local copies, waits for them, and re-layouts: 70.8 us -> 249 us
  starting transfers between devices: 4.6 us -> 177 us
  blocking collectives: 82.9 us -> 0 us
  matrix products: 196 us -> 135 us
    reduce_scatter x8 -> x0, waiting for transfers between devices: 1560 us -> none  [the longest x1 348 us: body(): lax.psum_scatter(grad_patch_proj, ('dp', 'fsdp'), scatter_dimension=0, ti...]
    all_gather x10 -> x0, waiting for transfers between devices: 484 us -> none  [the longest x1 75.7 us: body(): lax.all_gather(gate_proj, ('dp', 'fsdp'), axis=0, tiled=True)]
    ppermute x2 -> x168, waiting for transfers between devices: 0.13 us -> 447 us  [send(): return lax.ppermute(block, AX, self.route(dim, step))]
    ppermute x2 -> x168, starting transfers between devices: 3.46 us -> 154 us  [send(): return lax.ppermute(block, AX, self.route(dim, step))]
    dynamic_update_slice x0 -> x129, local copies, waits for them, and re-layouts: none -> 98.5 us  [put(): lax.dynamic_update_slice(whole, part, [jnp.asarray(p, jnp.int32) for p in...]
    unnamed x20 -> x0, waiting for transfers between devices: 43.8 us -> none
    all_gather x2 -> x0, blocking collectives: 41.6 us -> none  [the longest x1 34.6 us: body(): lax.all_gather(conv_weight, ('dp', 'fsdp'), axis=0, tiled=True)]
    unnamed x1 -> x0, blocking collectives: 41.3 us -> none
  transfers between devices with their start and end apart: 21 -> 172, of which waited for: 20 -> 88; matrix products, arithmetic and copies ran while one was open for 8% -> 31% of each run, Pallas kernels for 0% -> 0%
where the time goes in v1:
time: 1120 us; the launch traced here: 1100 us
  waiting for transfers between devices  465 us (42%)
  local copies, waits for them, and re-layouts  249 us (22%)
  starting transfers between devices  177 us (16%)
  matrix products  135 us (12%)
  other arithmetic  67.4 us (6%)
    ppermute x168, waiting for transfers between devices, send(): return lax.ppermute(block, AX, self.route(dim, step))  447 us
    ppermute x168, starting transfers between devices, send(): return lax.ppermute(block, AX, self.route(dim, step))  154 us
    dynamic_update_slice x129, local copies, waits for them, and re-layouts, put(): lax.dynamic_update_slice(whole, part, [jnp.asarray(p, jnp.int32) for p in...  98.5 us
    dot_general x11, matrix products, input_grad(): lax.dot_general(grad_rows, weight, (((1,), (1,)), ((), ())), preferred_el...  40.6 us
    dot_general x18, matrix products, weight_grad(): lax.dot_general(left, right, (((0,), (0,)), ((), ())), preferred_element_...  39.9 us
    dot_general x11, matrix products, product(): return jnp.dot(left, right, preferred_element_type=jnp.float32)  36.4 us
    all_to_all x4, starting transfers between devices, exchange(): return lax.all_to_all(blocks, AX, 0, 0, tiled=False)  23.3 us
    unnamed x333, local copies, waits for them, and re-layouts  22.4 us
  transfers between devices with their start and end apart: 172, of which 88 were waited for; matrix products, arithmetic and copies ran while one was open for 31% of the time, Pallas kernels for 0%

profile of v1, /device:TPU:8, one launch (start us, length us, event | category | flops | bytes accessed | tf_op | source)
XLA Modules:
  0.0 1100.4 jit_solution(13582844977768174617)
XLA Ops:
  18.3 4.3 all-to-all-start
  69.3 5.2 collective-permute-done.32
  75.2 5.3 collective-permute-done.43
  80.5 6.6 collective-permute-done.53
  87.7 5.9 collective-permute-done.44
  96.0 4.4 collective-permute-done.54
  104.2 5.7 collective-permute-done.72
  110.7 7.4 collective-permute-done.62
  119.0 5.9 collective-permute-done.33
  133.2 5.0 collective-permute-done.34
  166.2 4.3 collective-permute-start.95
  172.2 10.6 collective-permute-done.73
  183.5 16.0 %collective-permute-done.63 = bf16[1,1,32,4096]{3,2,1,0:T(8,128)(2,1)S(1)} collective-permute-done((bf16[1,1,32,4096]{3,2,1,0:T(8,128)(2,1)S(1)}, bf16[1,1,32,4096]{3,2,1,0:T(8,128)(2,1)S(1)}, u32[]{:S(2)}, u32[]{:S(2)}) %collective-permute-start.63) | collective-permute-done | bytes 262176 | tf_op jit(solution)/shard_map/ppermute | solution.py:480
  201.0 6.9 collective-permute-done.47
  214.2 5.9 collective-permute-done.57
  224.2 7.7 collective-permute-done.74
  235.5 6.0 collective-permute-done.64
  255.5 7.1 all-to-all-start.1
  268.8 8.8 collective-permute-done.96
  279.5 9.4 collective-permute-done.37
  296.3 13.4 %collective-permute-done.87 = bf16[4,1,128,512]{3,2,1,0:T(8,128)(2,1)S(1)} collective-permute-done((bf16[4,1,128,512]{3,2,1,0:T(8,128)(2,1)}, bf16[4,1,128,512]{3,2,1,0:T(8,128)(2,1)S(1)}, u32[]{:S(2)}, u32[]{:S(2)}) %collective-permute-start.87) | collective-permute-done | bytes 524320 | tf_op jit(solution)/shard_map/ppermute | solution.py:480
  310.4 14.3 %collective-permute-done.97 = bf16[4,1,128,512]{3,2,1,0:T(8,128)(2,1)S(1)} collective-permute-done((bf16[4,1,128,512]{3,2,1,0:T(8,128)(2,1)}, bf16[4,1,128,512]{3,2,1,0:T(8,128)(2,1)S(1)}, u32[]{:S(2)}, u32[]{:S(2)}) %collective-permute-start.97) | collective-permute-done | bytes 524320 | tf_op jit(solution)/shard_map/ppermute | solution.py:480
  339.4 8.9 collective-permute-done.66
  354.4 5.7 collective-permute-done.9
  373.9 5.6 collective-permute-start.14
  400.6 5.6 collective-permute-done.19
  414.4 23.3 %collective-permute-done.20 = bf16[2,4,32,512]{3,2,1,0:T(8,128)(2,1)S(1)} collective-permute-done((bf16[2,4,32,512]{3,2,1,0:T(8,128)(2,1)S(1)}, bf16[2,4,32,512]{3,2,1,0:T(8,128)(2,1)S(1)}, u32[]{:S(2)}, u32[]{:S(2)}) %collective-permute-start.20) | collective-permute-done | bytes 262176 | tf_op jit(solution)/shard_map/ppermute | solution.py:480
  438.3 7.4 collective-permute-done.22
  463.5 6.1 copy.402
  481.6 5.8 collective-permute-done.27
  533.8 6.0 fusion.312
  539.8 9.8 multiply_convert_fusion.1
  549.6 4.9 reshape.806
  554.5 5.0 fusion.313
  564.9 6.5 fusion.315
  577.9 6.7 multiply_reduce_fusion.1
  599.5 4.6 multiply_reduce_fusion.2
  610.1 8.6 constant_dynamic-slice_fusion.5
  627.4 4.8 copy.555
  642.1 4.1 collective-permute-done.106
  676.6 5.0 copy.554
  686.8 8.6 collective-permute-done.133
  712.4 4.0 fusion.217
  726.1 4.9 convolution_add_fusion.1
  741.5 6.5 collective-permute-done.134
  754.3 4.6 collective-permute-done.135
  758.9 6.0 collective-permute-done.142
  764.9 6.5 collective-permute-done.136
  771.4 6.4 collective-permute-done.143
  778.5 5.3 collective-permute-done.137
  796.1 8.8 collective-permute-done.157
  806.9 9.3 collective-permute-done.163
  817.4 17.1 %collective-permute-done.111 = bf16[4,2,32,512]{3,2,0,1:T(8,128)(2,1)S(1)} collective-permute-done((bf16[4,2,32,512]{3,2,0,1:T(8,128)(2,1)S(1)}, bf16[4,2,32,512]{3,2,0,1:T(8,128)(2,1)S(1)}, u32[]{:S(2)}, u32[]{:S(2)}) %collective-permute-start.111) | collective-permute-done | bytes 262176 | tf_op jit(solution)/shard_map/ppermute | solution.py:480
  836.2 5.2 collective-permute-done.113
  851.5 6.2 collective-permute-start.116
  863.8 10.3 collective-permute-done.117
  890.0 5.8 all-to-all-start.3
  899.1 8.9 collective-permute-done.123
  909.6 6.7 collective-permute-done.122
  917.9 6.2 collective-permute-done.124
  932.6 11.2 %collective-permute-done.129 = bf16[32,2048]{1,0:T(8,128)(2,1)S(1)} collective-permute-done((bf16[32,2048]{1,0:T(8,128)(2,1)S(1)}, bf16[32,2048]{1,0:T(8,128)(2,1)S(1)}, u32[]{:S(2)}, u32[]{:S(2)}) %collective-permute-start.129) | collective-permute-done | bytes 131104 | tf_op jit(solution)/shard_map/ppermute | solution.py:480
  989.3 6.1 all-to-all-start.2
  1011.0 17.5 %all-to-all-done.2 = bf16[32,32,256]{2,1,0:T(8,128)(2,1)S(1)} async-done(((bf16[32,32,256]{2,1,0:T(8,128)(2,1)}), bf16[32,32,256]{2,1,0:T(8,128)(2,1)S(1)}, u32[]{:S(2)}, u32[]{:S(2)}) %all-to-all-start.2) | async-done | bytes 524320 | tf_op jit(solution)/shard_map/all_to_all | solution.py:582
  1042.8 20.4 %collective-permute-done.152 = bf16[4,32,4096]{2,1,0:T(8,128)(2,1)S(1)} collective-permute-done((bf16[4,32,4096]{2,1,0:T(8,128)(2,1)S(1)}, bf16[4,32,4096]{2,1,0:T(8,128)(2,1)S(1)}, u32[]{:S(2)}, u32[]{:S(2)}) %collective-permute-start.152) | collective-permute-done | bytes 1048608 | tf_op jit(solution)/shard_map/ppermute | solution.py:480
  (1102 shorter events, 601.3 us)
Async XLA Ops:
  6.5 29.6 %collective-permute-start = (bf16[35,256]{1,0:T(8,128)(2,1)S(1)}, bf16[35,256]{1,0:T(8,128)(2,1)}, u32[]{:S(2)}, u32[]{:S(2)}) collective-permute-start(bf16[35,256]{1,0:T(8,128)(2,1)S(1)} %pad_maximum_fusion.17), channel_id=1, source_target_pairs={{0,8},{1,9},{2,10},{3,11},{4,12},{5,13},{6,14},{7,15},{8,16},{9,17... | collective-permute-start | bytes 53768 | tf_op jit(solution)/shard_map/ppermute | solution.py:480
  8.1 30.2 %collective-permute-start.1 = (bf16[35,256]{1,0:T(8,128)(2,1)S(1)}, bf16[35,256]{1,0:T(8,128)(2,1)}, u32[]{:S(2)}, u32[]{:S(2)}) collective-permute-start(bf16[35,256]{1,0:T(8,128)(2,1)S(1)} %pad_maximum_fusion.17), channel_id=1, source_target_pairs={{0,16},{1,17},{2,18},{3,19},{4,20},{5,21},{6,22},{7,23},{8,24},{9,... | collective-permute-start | bytes 53768 | tf_op jit(solution)/shard_map/ppermute | solution.py:480
  9.2 31.3 %collective-permute-start.2 = (bf16[35,256]{1,0:T(8,128)(2,1)S(1)}, bf16[35,256]{1,0:T(8,128)(2,1)}, u32[]{:S(2)}, u32[]{:S(2)}) collective-permute-start(bf16[35,256]{1,0:T(8,128)(2,1)S(1)} %pad_maximum_fusion.17), channel_id=1, source_target_pairs={{0,24},{1,25},{2,26},{3,27},{4,28},{5,29},{6,30},{7,31},{8,0},{9,1... | collective-permute-start | bytes 53768 | tf_op jit(solution)/shard_map/ppermute | solution.py:480
  12.9 105.3 %collective-permute-start.82 = (bf16[1,128,512]{2,1,0:T(8,128)(2,1)}, bf16[1,128,512]{2,1,0:T(8,128)(2,1)S(1)}, u32[]{:S(2)}, u32[]{:S(2)}) collective-permute-start(bf16[1,128,512]{2,1,0:T(8,128)(2,1)} %get-tuple-element.228), channel_id=1, source_target_pairs={{0,4},{1,5},{2,6},{3,7},{4,0},{5,1},{6,2},{7,3},{8,12},{9,13},{10,... | collective-permute-start | bytes 393224 | tf_op jit(solution)/shard_map/ppermute | solution.py:480
  14.4 111.7 %collective-permute-start.83 = (bf16[1,128,512]{2,1,0:T(8,128)(2,1)}, bf16[1,128,512]{2,1,0:T(8,128)(2,1)}, u32[]{:S(2)}, u32[]{:S(2)}) collective-permute-start(bf16[1,128,512]{2,1,0:T(8,128)(2,1)} %get-tuple-element.228), channel_id=1, source_target_pairs={{0,2},{1,3},{2,0},{3,1},{4,6},{5,7},{6,4},{7,5},{8,10},{9,11},{10,... | collective-permute-start | bytes 393224 | tf_op jit(solution)/shard_map/ppermute | solution.py:480
  18.3 237.2 %all-to-all-start = ((bf16[32,32,256]{2,1,0:T(8,128)(2,1)}), bf16[32,32,256]{2,1,0:T(8,128)(2,1)}, u32[]{:S(2)}, u32[]{:S(2)}) async-start(bf16[32,32,256]{2,1,0:T(8,128)(2,1)} %bitcast.1042), calls=%async_computation | async-start | bytes 1048576 | tf_op jit(solution)/shard_map/all_to_all | solution.py:582
  36.1 82.2 %collective-permute-start.92 = (bf16[1,128,512]{2,1,0:T(8,128)(2,1)}, bf16[1,128,512]{2,1,0:T(8,128)(2,1)S(1)}, u32[]{:S(2)}, u32[]{:S(2)}) collective-permute-start(bf16[1,128,512]{2,1,0:T(8,128)(2,1)} %get-tuple-element.229), channel_id=1, source_target_pairs={{0,2},{1,3},{2,0},{3,1},{4,6},{5,7},{6,4},{7,5},{8,10},{9,11},{10,... | collective-permute-start | bytes 393224 | tf_op jit(solution)/shard_map/ppermute | solution.py:480
  38.3 91.9 %collective-permute-start.93 = (bf16[1,128,512]{2,1,0:T(8,128)(2,1)}, bf16[1,128,512]{2,1,0:T(8,128)(2,1)S(1)}, u32[]{:S(2)}, u32[]{:S(2)}) collective-permute-start(bf16[1,128,512]{2,1,0:T(8,128)(2,1)} %get-tuple-element.229), channel_id=1, source_target_pairs={{0,4},{1,5},{2,6},{3,7},{4,0},{5,1},{6,2},{7,3},{8,12},{9,13},{10,... | collective-permute-start | bytes 393224 | tf_op jit(solution)/shard_map/ppermute | solution.py:480
  118.2 26.5 %collective-permute-start.7 = (bf16[4,2,2,35,256]{4,3,2,1,0:T(8,128)(2,1)S(1)}, bf16[4,2,2,35,256]{4,3,2,1,0:T(8,128)(2,1)S(1)}, u32[]{:S(2)}, u32[]{:S(2)}) collective-permute-start(bf16[4,2,2,35,256]{4,3,2,1,0:T(8,128)(2,1)S(1)} %constant_dynamic-update-slice_fusion.30), channel_id=1, source_target_pairs={{0,1},{1,0},{2,3},{3,2},{4,5},{5,4},{6,7},{7,6},{8,9},{9,8},{10,11... | collective-permute-start | bytes 860168 | tf_op jit(solution)/shard_map/ppermute | solution.py:480
  126.1 32.9 %collective-permute-start.45 = (bf16[4,32,1024]{2,1,0:T(8,128)(2,1)S(1)}, bf16[4,32,1024]{2,1,0:T(8,128)(2,1)}, u32[]{:S(2)}, u32[]{:S(2)}) collective-permute-start(bf16[4,32,1024]{2,1,0:T(8,128)(2,1)S(1)} %bitcast.1113), channel_id=1, source_target_pairs={{0,2},{1,3},{2,0},{3,1},{4,6},{5,7},{6,4},{7,5},{8,10},{9,11},{10,... | collective-permute-start | bytes 786440 | tf_op jit(solution)/shard_map/ppermute | solution.py:480
  126.8 35.5 %collective-permute-start.46 = (bf16[4,32,1024]{2,1,0:T(8,128)(2,1)S(1)}, bf16[4,32,1024]{2,1,0:T(8,128)(2,1)}, u32[]{:S(2)}, u32[]{:S(2)}) collective-permute-start(bf16[4,32,1024]{2,1,0:T(8,128)(2,1)S(1)} %bitcast.1114), channel_id=1, source_target_pairs={{0,4},{1,5},{2,6},{3,7},{4,0},{5,1},{6,2},{7,3},{8,12},{9,13},{10,... | collective-permute-start | bytes 786440 | tf_op jit(solution)/shard_map/ppermute | solution.py:480
  130.2 78.3 %collective-permute-start.48 = (bf16[4,32,1024]{2,1,0:T(8,128)(2,1)S(1)}, bf16[4,32,1024]{2,1,0:T(8,128)(2,1)}, u32[]{:S(2)}, u32[]{:S(2)}) collective-permute-start(bf16[4,32,1024]{2,1,0:T(8,128)(2,1)S(1)} %bitcast.1115), channel_id=1, source_target_pairs={{0,1},{1,0},{2,3},{3,2},{4,5},{5,4},{6,7},{7,6},{8,9},{9,8},{10,11... | collective-permute-start | bytes 786440 | tf_op jit(solution)/shard_map/ppermute | solution.py:480
  138.2 22.4 %collective-permute-start.55 = (bf16[4,32,1024]{2,1,0:T(8,128)(2,1)}, bf16[4,32,1024]{2,1,0:T(8,128)(2,1)}, u32[]{:S(2)}, u32[]{:S(2)}) collective-permute-start(bf16[4,32,1024]{2,1,0:T(8,128)(2,1)} %bitcast.138), channel_id=1, source_target_pairs={{0,2},{1,3},{2,0},{3,1},{4,6},{5,7},{6,4},{7,5},{8,10},{9,11},{10,... | collective-permute-start | bytes 786440 | tf_op jit(solution)/shard_map/ppermute | solution.py:480
  144.7 21.5 %collective-permute-start.56 = (bf16[4,32,1024]{2,1,0:T(8,128)(2,1)}, bf16[4,32,1024]{2,1,0:T(8,128)(2,1)}, u32[]{:S(2)}, u32[]{:S(2)}) collective-permute-start(bf16[4,32,1024]{2,1,0:T(8,128)(2,1)} %bitcast.138), channel_id=1, source_target_pairs={{0,4},{1,5},{2,6},{3,7},{4,0},{5,1},{6,2},{7,3},{8,12},{9,13},{10,... | collective-permute-start | bytes 786440 | tf_op jit(solution)/shard_map/ppermute | solution.py:480
  159.0 61.9 %collective-permute-start.58 = (bf16[4,32,1024]{2,1,0:T(8,128)(2,1)}, bf16[4,32,1024]{2,1,0:T(8,128)(2,1)S(1)}, u32[]{:S(2)}, u32[]{:S(2)}) collective-permute-start(bf16[4,32,1024]{2,1,0:T(8,128)(2,1)} %bitcast.138), channel_id=1, source_target_pairs={{0,1},{1,0},{2,3},{3,2},{4,5},{5,4},{6,7},{7,6},{8,9},{9,8},{10,11... | collective-permute-start | bytes 786440 | tf_op jit(solution)/shard_map/ppermute | solution.py:480
  160.7 82.0 %collective-permute-start.85 = (bf16[4,1,128,512]{3,2,1,0:T(8,128)(2,1)}, bf16[4,1,128,512]{3,2,1,0:T(8,128)(2,1)}, u32[]{:S(2)}, u32[]{:S(2)}) collective-permute-start(bf16[4,1,128,512]{3,2,1,0:T(8,128)(2,1)} %get-tuple-element.200), channel_id=1, source_target_pairs={{0,8},{1,9},{2,10},{3,11},{4,12},{5,13},{6,14},{7,15},{8,16},{9,17... | collective-permute-start | bytes 1572872 | tf_op jit(solution)/shard_map/ppermute | solution.py:480
  162.3 20.5 %collective-permute-start.73 = (bf16[1,1,32,4096]{3,2,1,0:T(8,128)(2,1)}, bf16[1,1,32,4096]{3,2,1,0:T(8,128)(2,1)S(1)}, u32[]{:S(2)}, u32[]{:S(2)}) collective-permute-start(bf16[1,1,32,4096]{3,2,1,0:T(8,128)(2,1)} %copy-done.91), channel_id=1, source_target_pairs={{0,8},{1,9},{2,10},{3,11},{4,12},{5,13},{6,14},{7,15},{8,16},{9,17... | collective-permute-start | bytes 786440 | tf_op jit(solution)/shard_map/ppermute | solution.py:480
  166.2 78.6 %collective-permute-start.95 = (bf16[4,1,128,512]{3,2,1,0:T(8,128)(2,1)}, bf16[4,1,128,512]{3,2,1,0:T(8,128)(2,1)}, u32[]{:S(2)}, u32[]{:S(2)}) collective-permute-start(bf16[4,1,128,512]{3,2,1,0:T(8,128)(2,1)} %get-tuple-element.202), channel_id=1, source_target_pairs={{0,8},{1,9},{2,10},{3,11},{4,12},{5,13},{6,14},{7,15},{8,16},{9,17... | collective-permute-start | bytes 1572872 | tf_op jit(solution)/shard_map/ppermute | solution.py:480
  212.9 34.2 %collective-permute-start.35 = (bf16[4,32,2048]{2,1,0:T(8,128)(2,1)}, bf16[4,32,2048]{2,1,0:T(8,128)(2,1)}, u32[]{:S(2)}, u32[]{:S(2)}) collective-permute-start(bf16[4,32,2048]{2,1,0:T(8,128)(2,1)} %bitcast.98), channel_id=1, source_target_pairs={{0,4},{1,5},{2,6},{3,7},{4,0},{5,1},{6,2},{7,3},{8,12},{9,13},{10,... | collective-permute-start | bytes 1572872 | tf_op jit(solution)/shard_map/ppermute | solution.py:480
  222.8 27.0 %collective-permute-start.36 = (bf16[4,32,2048]{2,1,0:T(8,128)(2,1)}, bf16[4,32,2048]{2,1,0:T(8,128)(2,1)S(1)}, u32[]{:S(2)}, u32[]{:S(2)}) collective-permute-start(bf16[4,32,2048]{2,1,0:T(8,128)(2,1)} %bitcast.98), channel_id=1, source_target_pairs={{0,2},{1,3},{2,0},{3,1},{4,6},{5,7},{6,4},{7,5},{8,10},{9,11},{10,... | collective-permute-start | bytes 1572872 | tf_op jit(solution)/shard_map/ppermute | solution.py:480
  241.5 49.3 %collective-permute-start.38 = (bf16[4,32,2048]{2,1,0:T(8,128)(2,1)}, bf16[4,32,2048]{2,1,0:T(8,128)(2,1)}, u32[]{:S(2)}, u32[]{:S(2)}) collective-permute-start(bf16[4,32,2048]{2,1,0:T(8,128)(2,1)} %bitcast.98), channel_id=1, source_target_pairs={{0,1},{1,0},{2,3},{3,2},{4,5},{5,4},{6,7},{7,6},{8,9},{9,8},{10,11... | collective-permute-start | bytes 1572872 | tf_op jit(solution)/shard_map/ppermute | solution.py:480
  247.1 83.7 %collective-permute-start.75 = (bf16[4,32,4096]{2,1,0:T(8,128)(2,1)}, bf16[4,32,4096]{2,1,0:T(8,128)(2,1)}, u32[]{:S(2)}, u32[]{:S(2)}) collective-permute-start(bf16[4,32,4096]{2,1,0:T(8,128)(2,1)} %bitcast.175), channel_id=1, source_target_pairs={{0,2},{1,3},{2,0},{3,1},{4,6},{5,7},{6,4},{7,5},{8,10},{9,11},{10,... | collective-permute-start | bytes 3145736 | tf_op jit(solution)/shard_map/ppermute | solution.py:480
  251.4 26.2 %collective-permute-start.96 = (bf16[4,1,128,512]{3,2,1,0:T(8,128)(2,1)}, bf16[4,1,128,512]{3,2,1,0:T(8,128)(2,1)}, u32[]{:S(2)}, u32[]{:S(2)}) collective-permute-start(bf16[4,1,128,512]{3,2,1,0:T(8,128)(2,1)} %collective-permute-done.95), channel_id=1, source_target_pairs={{0,8},{1,9},{2,10},{3,11},{4,12},{5,13},{6,14},{7,15},{8,16},{9,17... | collective-permute-start | bytes 1572872 | tf_op jit(solution)/shard_map/ppermute | solution.py:480
  253.6 35.3 %collective-permute-start.37 = (bf16[4,32,2048]{2,1,0:T(8,128)(2,1)}, bf16[4,32,2048]{2,1,0:T(8,128)(2,1)}, u32[]{:S(2)}, u32[]{:S(2)}) collective-permute-start(bf16[4,32,2048]{2,1,0:T(8,128)(2,1)} %collective-permute-done.35), channel_id=1, source_target_pairs={{0,2},{1,3},{2,0},{3,1},{4,6},{5,7},{6,4},{7,5},{8,10},{9,11},{10,... | collective-permute-start | bytes 1572872 | tf_op jit(solution)/shard_map/ppermute | solution.py:480
  255.5 194.5 %all-to-all-start.1 = ((bf16[32,32,129]{2,1,0:T(8,128)(2,1)}), bf16[32,32,129]{2,1,0:T(8,128)(2,1)}, u32[]{:S(2)}, u32[]{:S(2)}) async-start(bf16[32,32,129]{2,1,0:T(8,128)(2,1)} %maximum_bitcast_fusion), calls=%async_computation.1 | async-start | bytes 1048576 | tf_op jit(solution)/shard_map/all_to_all | solution.py:582
  266.4 68.0 %collective-permute-start.76 = (bf16[4,32,4096]{2,1,0:T(8,128)(2,1)}, bf16[4,32,4096]{2,1,0:T(8,128)(2,1)S(1)}, u32[]{:S(2)}, u32[]{:S(2)}) collective-permute-start(bf16[4,32,4096]{2,1,0:T(8,128)(2,1)} %bitcast.175), channel_id=1, source_target_pairs={{0,4},{1,5},{2,6},{3,7},{4,0},{5,1},{6,2},{7,3},{8,12},{9,13},{10,... | collective-permute-start | bytes 3145736 | tf_op jit(solution)/shard_map/ppermute | solution.py:480
  277.6 132.1 %collective-permute-start.78 = (bf16[4,32,4096]{2,1,0:T(8,128)(2,1)}, bf16[4,32,4096]{2,1,0:T(8,128)(2,1)S(1)}, u32[]{:S(2)}, u32[]{:S(2)}) collective-permute-start(bf16[4,32,4096]{2,1,0:T(8,128)(2,1)} %bitcast.175), channel_id=1, source_target_pairs={{0,1},{1,0},{2,3},{3,2},{4,5},{5,4},{6,7},{7,6},{8,9},{9,8},{10,11... | collective-permute-start | bytes 3145736 | tf_op jit(solution)/shard_map/ppermute | solution.py:480
  294.0 42.0 %collective-permute-start.65 = (bf16[4,32,4096]{2,1,0:T(8,128)(2,1)S(1)}, bf16[4,32,4096]{2,1,0:T(8,128)(2,1)}, u32[]{:S(2)}, u32[]{:S(2)}) collective-permute-start(bf16[4,32,4096]{2,1,0:T(8,128)(2,1)S(1)} %bitcast.1086), channel_id=1, source_target_pairs={{0,4},{1,5},{2,6},{3,7},{4,0},{5,1},{6,2},{7,3},{8,12},{9,13},{10,... | collective-permute-start | bytes 3145736 | tf_op jit(solution)/shard_map/ppermute | solution.py:480
  324.7 23.7 %collective-permute-start.66 = (bf16[4,32,4096]{2,1,0:T(8,128)(2,1)S(1)}, bf16[4,32,4096]{2,1,0:T(8,128)(2,1)}, u32[]{:S(2)}, u32[]{:S(2)}) collective-permute-start(bf16[4,32,4096]{2,1,0:T(8,128)(2,1)S(1)} %bitcast.1087), channel_id=1, source_target_pairs={{0,2},{1,3},{2,0},{3,1},{4,6},{5,7},{6,4},{7,5},{8,10},{9,11},{10,... | collective-permute-start | bytes 3145736 | tf_op jit(solution)/shard_map/ppermute | solution.py:480
  330.9 117.8 %collective-permute-start.68 = (bf16[4,32,4096]{2,1,0:T(8,128)(2,1)S(1)}, bf16[4,32,4096]{2,1,0:T(8,128)(2,1)S(1)}, u32[]{:S(2)}, u32[]{:S(2)}) collective-permute-start(bf16[4,32,4096]{2,1,0:T(8,128)(2,1)S(1)} %bitcast.1088), channel_id=1, source_target_pairs={{0,1},{1,0},{2,3},{3,2},{4,5},{5,4},{6,7},{7,6},{8,9},{9,8},{10,11... | collective-permute-start | bytes 3145736 | tf_op jit(solution)/shard_map/ppermute | solution.py:480
  379.6 26.6 %collective-permute-start.77 = (bf16[4,32,4096]{2,1,0:T(8,128)(2,1)}, bf16[4,32,4096]{2,1,0:T(8,128)(2,1)}, u32[]{:S(2)}, u32[]{:S(2)}) collective-permute-start(bf16[4,32,4096]{2,1,0:T(8,128)(2,1)} %collective-permute-done.75), channel_id=1, source_target_pairs={{0,4},{1,5},{2,6},{3,7},{4,0},{5,1},{6,2},{7,3},{8,12},{9,13},{10,... | collective-permute-start | bytes 3145736 | tf_op jit(solution)/shard_map/ppermute | solution.py:480
  406.3 39.5 %collective-permute-start.67 = (bf16[4,32,4096]{2,1,0:T(8,128)(2,1)}, bf16[4,32,4096]{2,1,0:T(8,128)(2,1)}, u32[]{:S(2)}, u32[]{:S(2)}) collective-permute-start(bf16[4,32,4096]{2,1,0:T(8,128)(2,1)} %collective-permute-done.65), channel_id=1, source_target_pairs={{0,2},{1,3},{2,0},{3,1},{4,6},{5,7},{6,4},{7,5},{8,10},{9,11},{10,... | collective-permute-start | bytes 3145736 | tf_op jit(solution)/shard_map/ppermute | solution.py:480
  409.7 62.4 %collective-permute-start.69 = (bf16[4,32,4096]{2,1,0:T(8,128)(2,1)}, bf16[4,32,4096]{2,1,0:T(8,128)(2,1)}, u32[]{:S(2)}, u32[]{:S(2)}) collective-permute-start(bf16[4,32,4096]{2,1,0:T(8,128)(2,1)} %collective-permute-done.65), channel_id=1, source_target_pairs={{0,1},{1,0},{2,3},{3,2},{4,5},{5,4},{6,7},{7,6},{8,9},{9,8},{10,11... | collective-permute-start | bytes 3145736 | tf_op jit(solution)/shard_map/ppermute | solution.py:480
  411.1 63.3 %collective-permute-start.70 = (bf16[4,32,4096]{2,1,0:T(8,128)(2,1)}, bf16[4,32,4096]{2,1,0:T(8,128)(2,1)}, u32[]{:S(2)}, u32[]{:S(2)}) collective-permute-start(bf16[4,32,4096]{2,1,0:T(8,128)(2,1)} %collective-permute-done.66), channel_id=1, source_target_pairs={{0,1},{1,0},{2,3},{3,2},{4,5},{5,4},{6,7},{7,6},{8,9},{9,8},{10,11... | collective-permute-start | bytes 3145736 | tf_op jit(solution)/shard_map/ppermute | solution.py:480
  412.5 25.3 %collective-permute-start.20 = (bf16[2,4,32,512]{3,2,1,0:T(8,128)(2,1)S(1)}, bf16[2,4,32,512]{3,2,1,0:T(8,128)(2,1)S(1)}, u32[]{:S(2)}, u32[]{:S(2)}) collective-permute-start(bf16[2,4,32,512]{3,2,1,0:T(8,128)(2,1)S(1)} %pad_maximum_fusion.9), channel_id=1, source_target_pairs={{0,2},{1,3},{2,0},{3,1},{4,6},{5,7},{6,4},{7,5},{8,10},{9,11},{10,... | collective-permute-start | bytes 786440 | tf_op jit(solution)/shard_map/ppermute | solution.py:480
  445.7 32.5 %collective-permute-start.81 = (bf16[4,32,4096]{2,1,0:T(8,128)(2,1)}, bf16[4,32,4096]{2,1,0:T(8,128)(2,1)}, u32[]{:S(2)}, u32[]{:S(2)}) collective-permute-start(bf16[4,32,4096]{2,1,0:T(8,128)(2,1)} %collective-permute-done.77), channel_id=1, source_target_pairs={{0,1},{1,0},{2,3},{3,2},{4,5},{5,4},{6,7},{7,6},{8,9},{9,8},{10,11... | collective-permute-start | bytes 3145736 | tf_op jit(solution)/shard_map/ppermute | solution.py:480
  448.6 54.0 %collective-permute-start.71 = (bf16[4,32,4096]{2,1,0:T(8,128)(2,1)}, bf16[4,32,4096]{2,1,0:T(8,128)(2,1)}, u32[]{:S(2)}, u32[]{:S(2)}) collective-permute-start(bf16[4,32,4096]{2,1,0:T(8,128)(2,1)} %collective-permute-done.67), channel_id=1, source_target_pairs={{0,1},{1,0},{2,3},{3,2},{4,5},{5,4},{6,7},{7,6},{8,9},{9,8},{10,11... | collective-permute-start | bytes 3145736 | tf_op jit(solution)/shard_map/ppermute | solution.py:480
  620.9 43.1 %collective-permute-start.132 = (bf16[512,1024]{1,0:T(8,128)(2,1)}, bf16[512,1024]{1,0:T(8,128)(2,1)}, u32[]{:S(2)}, u32[]{:S(2)}) collective-permute-start(bf16[512,1024]{1,0:T(8,128)(2,1)} %convolution_convert_fusion.7), channel_id=1, source_target_pairs={{0,1},{1,0},{2,3},{3,2},{4,5},{5,4},{6,7},{7,6},{8,9},{9,8},{10,11... | collective-permute-start | bytes 3145736 | tf_op jit(solution)/shard_map/ppermute | solution.py:480
  632.1 33.7 %collective-permute-start.138 = (bf16[512,1024]{1,0:T(8,128)(2,1)}, bf16[512,1024]{1,0:T(8,128)(2,1)}, u32[]{:S(2)}, u32[]{:S(2)}) collective-permute-start(bf16[512,1024]{1,0:T(8,128)(2,1)} %convolution_convert_fusion.6), channel_id=1, source_target_pairs={{0,1},{1,0},{2,3},{3,2},{4,5},{5,4},{6,7},{7,6},{8,9},{9,8},{10,11... | collective-permute-start | bytes 3145736 | tf_op jit(solution)/shard_map/ppermute | solution.py:480
  634.0 21.8 %collective-permute-start.108 = (bf16[2,4,32,576]{3,2,1,0:T(8,128)(2,1)}, bf16[2,4,32,576]{3,2,1,0:T(8,128)(2,1)}, u32[]{:S(2)}, u32[]{:S(2)}) collective-permute-start(bf16[2,4,32,576]{3,2,1,0:T(8,128)(2,1)} %pad_maximum_fusion.7), channel_id=1, source_target_pairs={{0,4},{1,5},{2,6},{3,7},{4,0},{5,1},{6,2},{7,3},{8,12},{9,13},{10,... | collective-permute-start | bytes 884744 | tf_op jit(solution)/shard_map/ppermute | solution.py:480
  664.0 33.7 %collective-permute-start.109 = (bf16[4,2,2,32,1152]{4,3,2,1,0:T(8,128)(2,1)}, bf16[4,2,2,32,1152]{4,3,2,1,0:T(8,128)(2,1)}, u32[]{:S(2)}, u32[]{:S(2)}) collective-permute-start(bf16[4,2,2,32,1152]{4,3,2,1,0:T(8,128)(2,1)} %dynamic_update_slice.524), channel_id=1, source_target_pairs={{0,1},{1,0},{2,3},{3,2},{4,5},{5,4},{6,7},{7,6},{8,9},{9,8},{10,11... | collective-permute-start | bytes 3538952 | tf_op jit(solution)/shard_map/ppermute | solution.py:480
  674.2 21.3 %collective-permute-start.133 = (bf16[4,2,32,1024]{3,2,0,1:T(8,128)(2,1)}, bf16[4,2,32,1024]{3,2,0,1:T(8,128)(2,1)}, u32[]{:S(2)}, u32[]{:S(2)}) collective-permute-start(bf16[4,2,32,1024]{3,2,0,1:T(8,128)(2,1)} %bitcast.1041), channel_id=1, source_target_pairs={{0,4},{1,5},{2,6},{3,7},{4,0},{5,1},{6,2},{7,3},{8,12},{9,13},{10,... | collective-permute-start | bytes 1572872 | tf_op jit(solution)/shard_map/ppermute | solution.py:480
  676.5 107.9 %collective-permute-start.156 = (bf16[2048,512]{1,0:T(8,128)(2,1)}, bf16[2048,512]{1,0:T(8,128)(2,1)}, u32[]{:S(2)}, u32[]{:S(2)}) collective-permute-start(bf16[2048,512]{1,0:T(8,128)(2,1)} %convolution_convert_fusion.3), channel_id=1, source_target_pairs={{0,1},{1,0},{2,3},{3,2},{4,5},{5,4},{6,7},{7,6},{8,9},{9,8},{10,11... | collective-permute-start | bytes 6291464 | tf_op jit(solution)/shard_map/ppermute | solution.py:480
  681.6 106.7 %collective-permute-start.162 = (bf16[2048,512]{1,0:T(8,128)(2,1)}, bf16[2048,512]{1,0:T(8,128)(2,1)}, u32[]{:S(2)}, u32[]{:S(2)}) collective-permute-start(bf16[2048,512]{1,0:T(8,128)(2,1)} %convolution_convert_fusion.2), channel_id=1, source_target_pairs={{0,1},{1,0},{2,3},{3,2},{4,5},{5,4},{6,7},{7,6},{8,9},{9,8},{10,11... | collective-permute-start | bytes 6291464 | tf_op jit(solution)/shard_map/ppermute | solution.py:480
  684.6 280.7 %collective-permute-start.150 = (bf16[512,4096]{1,0:T(8,128)(2,1)}, bf16[512,4096]{1,0:T(8,128)(2,1)}, u32[]{:S(2)}, u32[]{:S(2)}) collective-permute-start(bf16[512,4096]{1,0:T(8,128)(2,1)} %convolution_convert_fusion), channel_id=1, source_target_pairs={{0,1},{1,0},{2,3},{3,2},{4,5},{5,4},{6,7},{7,6},{8,9},{9,8},{10,11... | collective-permute-start | bytes 12582920 | tf_op jit(solution)/shard_map/ppermute | solution.py:480
  695.4 95.4 %collective-permute-start.126 = (bf16[512,2048]{1,0:T(8,128)(2,1)}, bf16[512,2048]{1,0:T(8,128)(2,1)}, u32[]{:S(2)}, u32[]{:S(2)}) collective-permute-start(bf16[512,2048]{1,0:T(8,128)(2,1)} %convolution_convert_fusion.4), channel_id=1, source_target_pairs={{0,1},{1,0},{2,3},{3,2},{4,5},{5,4},{6,7},{7,6},{8,9},{9,8},{10,11... | collective-permute-start | bytes 6291464 | tf_op jit(solution)/shard_map/ppermute | solution.py:480
  697.7 41.7 %collective-permute-start.140 = (bf16[4,32,1024]{2,1,0:T(8,128)(2,1)}, bf16[4,32,1024]{2,1,0:T(8,128)(2,1)}, u32[]{:S(2)}, u32[]{:S(2)}) collective-permute-start(bf16[4,32,1024]{2,1,0:T(8,128)(2,1)} %fusion.93), channel_id=1, source_target_pairs={{0,2},{1,3},{2,0},{3,1},{4,6},{5,7},{6,4},{7,5},{8,10},{9,11},{10,... | collective-permute-start | bytes 786440 | tf_op jit(solution)/shard_map/ppermute | solution.py:480
  783.8 187.3 %collective-permute-start.144 = (bf16[512,4096]{1,0:T(8,128)(2,1)}, bf16[512,4096]{1,0:T(8,128)(2,1)}, u32[]{:S(2)}, u32[]{:S(2)}) collective-permute-start(bf16[512,4096]{1,0:T(8,128)(2,1)} %convolution_convert_fusion.1), channel_id=1, source_target_pairs={{0,1},{1,0},{2,3},{3,2},{4,5},{5,4},{6,7},{7,6},{8,9},{9,8},{10,11... | collective-permute-start | bytes 12582920 | tf_op jit(solution)/shard_map/ppermute | solution.py:480
  784.4 21.7 %collective-permute-start.110 = (bf16[4,2,2,32,1024]{4,3,0,2,1:T(8,128)(2,1)S(1)}, bf16[4,2,2,32,1024]{4,3,0,2,1:T(8,128)(2,1)S(1)}, u32[]{:S(2)}, u32[]{:S(2)}) collective-permute-start(bf16[4,2,2,32,1024]{4,3,0,2,1:T(8,128)(2,1)S(1)} %copy-done.70), channel_id=1, source_target_pairs={{0,1},{1,0},{2,3},{3,2},{4,5},{5,4},{6,7},{7,6},{8,9},{9,8},{10,11... | collective-permute-start | bytes 3145736 | tf_op jit(solution)/shard_map/ppermute | solution.py:480
  790.9 25.3 %collective-permute-start.163 = (bf16[2,2,128,512]{3,2,1,0:T(8,128)(2,1)S(1)}, bf16[2,2,128,512]{3,2,1,0:T(8,128)(2,1)S(1)}, u32[]{:S(2)}, u32[]{:S(2)}) collective-permute-start(bf16[2,2,128,512]{3,2,1,0:T(8,128)(2,1)S(1)} %dynamic-slice_bitcast_fusion), channel_id=1, source_target_pairs={{0,8},{1,9},{2,10},{3,11},{4,12},{5,13},{6,14},{7,15},{8,16},{9,17... | collective-permute-start | bytes 1572872 | tf_op jit(solution)/shard_map/ppermute | solution.py:480
  804.9 46.5 %collective-permute-start.127 = (bf16[4,2,32,2048]{3,2,0,1:T(8,128)(2,1)S(1)}, bf16[4,2,32,2048]{3,2,0,1:T(8,128)(2,1)S(1)}, u32[]{:S(2)}, u32[]{:S(2)}) collective-permute-start(bf16[4,2,32,2048]{3,2,0,1:T(8,128)(2,1)S(1)} %bitcast.1116), channel_id=1, source_target_pairs={{0,2},{1,3},{2,0},{3,1},{4,6},{5,7},{6,4},{7,5},{8,10},{9,11},{10,... | collective-permute-start | bytes 3145736 | tf_op jit(solution)/shard_map/ppermute | solution.py:480
  806.1 52.8 %collective-permute-start.158 = (bf16[2,2,128,512]{3,2,0,1:T(8,128)(2,1)S(1)}, bf16[2,2,128,512]{3,2,0,1:T(8,128)(2,1)S(1)}, u32[]{:S(2)}, u32[]{:S(2)}) collective-permute-start(bf16[2,2,128,512]{3,2,0,1:T(8,128)(2,1)S(1)} %fusion.27), channel_id=1, source_target_pairs={{0,8},{1,9},{2,10},{3,11},{4,12},{5,13},{6,14},{7,15},{8,16},{9,17... | collective-permute-start | bytes 1572872 | tf_op jit(solution)/shard_map/ppermute | solution.py:480
  816.2 18.3 %collective-permute-start.111 = (bf16[4,2,32,512]{3,2,0,1:T(8,128)(2,1)S(1)}, bf16[4,2,32,512]{3,2,0,1:T(8,128)(2,1)S(1)}, u32[]{:S(2)}, u32[]{:S(2)}) collective-permute-start(bf16[4,2,32,512]{3,2,0,1:T(8,128)(2,1)S(1)} %fusion.90), channel_id=1, source_target_pairs={{0,2},{1,3},{2,0},{3,1},{4,6},{5,7},{6,4},{7,5},{8,10},{9,11},{10,... | collective-permute-start | bytes 786440 | tf_op jit(solution)/shard_map/ppermute | solution.py:480
  862.1 64.6 %collective-permute-start.128 = (bf16[4,32,2048]{2,1,0:T(8,128)(2,1)}, bf16[4,32,2048]{2,1,0:T(8,128)(2,1)}, u32[]{:S(2)}, u32[]{:S(2)}) collective-permute-start(bf16[4,32,2048]{2,1,0:T(8,128)(2,1)} %fusion.38), channel_id=1, source_target_pairs={{0,4},{1,5},{2,6},{3,7},{4,0},{5,1},{6,2},{7,3},{8,12},{9,13},{10,... | collective-permute-start | bytes 1572872 | tf_op jit(solution)/shard_map/ppermute | solution.py:480
  890.0 99.4 %all-to-all-start.3 = ((bf16[32,32,403]{2,1,0:T(8,128)(2,1)}), bf16[32,32,403]{2,1,0:T(8,128)(2,1)}, u32[]{:S(2)}, u32[]{:S(2)}) async-start(bf16[32,32,403]{2,1,0:T(8,128)(2,1)} %pad_maximum_fusion), calls=%async_computation.3 | async-start | bytes 2097152 | tf_op jit(solution)/shard_map/all_to_all | solution.py:582
  898.3 18.1 %collective-permute-start.122 = (bf16[2,4,32,512]{3,2,1,0:T(8,128)(2,1)S(1)}, bf16[2,4,32,512]{3,2,1,0:T(8,128)(2,1)S(1)}, u32[]{:S(2)}, u32[]{:S(2)}) collective-permute-start(bf16[2,4,32,512]{3,2,1,0:T(8,128)(2,1)S(1)} %pad_maximum_fusion.11), channel_id=1, source_target_pairs={{0,2},{1,3},{2,0},{3,1},{4,6},{5,7},{6,4},{7,5},{8,10},{9,11},{10,... | collective-permute-start | bytes 786440 | tf_op jit(solution)/shard_map/ppermute | solution.py:480
  907.9 22.1 %collective-permute-start.159 = (bf16[2,2,128,512]{3,2,0,1:T(8,128)(2,1)}, bf16[2,2,128,512]{3,2,0,1:T(8,128)(2,1)S(1)}, u32[]{:S(2)}, u32[]{:S(2)}) collective-permute-start(bf16[2,2,128,512]{3,2,0,1:T(8,128)(2,1)} %fusion.28), channel_id=1, source_target_pairs={{0,8},{1,9},{2,10},{3,11},{4,12},{5,13},{6,14},{7,15},{8,16},{9,17... | collective-permute-start | bytes 1572872 | tf_op jit(solution)/shard_map/ppermute | solution.py:480
  924.1 21.3 %collective-permute-start.165 = (bf16[2,2,128,512]{3,2,1,0:T(8,128)(2,1)S(1)}, bf16[2,2,128,512]{3,2,1,0:T(8,128)(2,1)S(1)}, u32[]{:S(2)}, u32[]{:S(2)}) collective-permute-start(bf16[2,2,128,512]{3,2,1,0:T(8,128)(2,1)S(1)} %copy-done.77), channel_id=1, source_target_pairs={{0,8},{1,9},{2,10},{3,11},{4,12},{5,13},{6,14},{7,15},{8,16},{9,17... | collective-permute-start | bytes 1572872 | tf_op jit(solution)/shard_map/ppermute | solution.py:480
  926.7 52.3 %collective-permute-start.125 = (bf16[4,2,2,32,1024]{4,3,2,1,0:T(8,128)(2,1)S(1)}, bf16[4,2,2,32,1024]{4,3,2,1,0:T(8,128)(2,1)S(1)}, u32[]{:S(2)}, u32[]{:S(2)}) collective-permute-start(bf16[4,2,2,32,1024]{4,3,2,1,0:T(8,128)(2,1)S(1)} %fusion.194), channel_id=1, source_target_pairs={{0,1},{1,0},{2,3},{3,2},{4,5},{5,4},{6,7},{7,6},{8,9},{9,8},{10,11... | collective-permute-start | bytes 3145736 | tf_op jit(solution)/shard_map/ppermute | solution.py:480
  970.8 64.7 %collective-permute-start.151 = (bf16[4,2,32,4096]{3,2,0,1:T(8,128)(2,1)}, bf16[4,2,32,4096]{3,2,0,1:T(8,128)(2,1)}, u32[]{:S(2)}, u32[]{:S(2)}) collective-permute-start(bf16[4,2,32,4096]{3,2,0,1:T(8,128)(2,1)} %bitcast.1036), channel_id=1, source_target_pairs={{0,4},{1,5},{2,6},{3,7},{4,0},{5,1},{6,2},{7,3},{8,12},{9,13},{10,... | collective-permute-start | bytes 6291464 | tf_op jit(solution)/shard_map/ppermute | solution.py:480
  978.5 60.0 %collective-permute-start.145 = (bf16[4,2,32,4096]{3,2,0,1:T(8,128)(2,1)}, bf16[4,2,32,4096]{3,2,0,1:T(8,128)(2,1)}, u32[]{:S(2)}, u32[]{:S(2)}) collective-permute-start(bf16[4,2,32,4096]{3,2,0,1:T(8,128)(2,1)} %bitcast.1037), channel_id=1, source_target_pairs={{0,2},{1,3},{2,0},{3,1},{4,6},{5,7},{6,4},{7,5},{8,10},{9,11},{10,... | collective-permute-start | bytes 6291464 | tf_op jit(solution)/shard_map/ppermute | solution.py:480
  989.3 39.2 %all-to-all-start.2 = ((bf16[32,32,256]{2,1,0:T(8,128)(2,1)}), bf16[32,32,256]{2,1,0:T(8,128)(2,1)S(1)}, u32[]{:S(2)}, u32[]{:S(2)}) async-start(bf16[32,32,256]{2,1,0:T(8,128)(2,1)} %bitcast.1120), calls=%async_computation.2 | async-start | bytes 1048576 | tf_op jit(solution)/shard_map/all_to_all | solution.py:582
  1037.9 25.2 %collective-permute-start.152 = (bf16[4,32,4096]{2,1,0:T(8,128)(2,1)S(1)}, bf16[4,32,4096]{2,1,0:T(8,128)(2,1)S(1)}, u32[]{:S(2)}, u32[]{:S(2)}) collective-permute-start(bf16[4,32,4096]{2,1,0:T(8,128)(2,1)S(1)} %fusion.20), channel_id=1, source_target_pairs={{0,2},{1,3},{2,0},{3,1},{4,6},{5,7},{6,4},{7,5},{8,10},{9,11},{10,... | collective-permute-start | bytes 3145736 | tf_op jit(solution)/shard_map/ppermute | solution.py:480
  1041.7 25.2 %collective-permute-start.146 = (bf16[4,32,4096]{2,1,0:T(8,128)(2,1)S(1)}, bf16[4,32,4096]{2,1,0:T(8,128)(2,1)S(1)}, u32[]{:S(2)}, u32[]{:S(2)}) collective-permute-start(bf16[4,32,4096]{2,1,0:T(8,128)(2,1)S(1)} %fusion.19), channel_id=1, source_target_pairs={{0,4},{1,5},{2,6},{3,7},{4,0},{5,1},{6,2},{7,3},{8,12},{9,13},{10,... | collective-permute-start | bytes 3145736 | tf_op jit(solution)/shard_map/ppermute | solution.py:480
  (271 other events, 2540.1 us)

commit v2 on v1

--- a/solution.py
+++ b/solution.py
@@ -3,6 +3,8 @@
 import jax
 import jax.numpy as jnp
 from jax import lax
+from jax.experimental import pallas as pl
+from jax.experimental.pallas import tpu as pltpu
 from jax.sharding import PartitionSpec as P
 
 D = 1024
@@ -449,6 +451,613 @@
     )
 
 
+MESH = pl.DeviceIdType.MESH
+WIDE = 12288
+TILE = 32
+SMALL_ROWS, SMALL_COLS = 48, 384
+EXT = D + 128
+
+
+def device(z, x, y, c):
+    return (z * 2 + x, y * 2 + c)
+
+
+class Spot:
+    def __init__(self, depth):
+        dp, fs = lax.axis_index("dp"), lax.axis_index("fsdp")
+        self.depth, self.count = depth, depth * 8
+        self.me = dp * 4 + fs
+        self.z, self.x, self.y, self.c = dp // 2, dp % 2, fs // 2, fs % 2
+        self.q = self.x * 4 + self.y * 2 + self.c
+        self.plane = self.x * 2 + self.y
+        self.column = [(self.z + depth - j) % depth for j in range(depth)]
+
+    def flip(self, way):
+        x = 1 - self.x if way & 2 else self.x
+        y = 1 - self.y if way & 1 else self.y
+        return device(self.z, x, y, self.c), x * 2 + y
+
+    def sibling(self):
+        return device(self.z, self.x, self.y, 1 - self.c)
+
+    def above(self, k):
+        return device((self.z + k) % self.depth, self.x, self.y, self.c)
+
+
+def greet(spot):
+    barrier = pltpu.get_barrier_semaphore()
+
+    def one(i, carry):
+        to = (spot.me + i) % spot.count
+        pl.semaphore_signal(barrier, inc=1, device_id=(to // 4, to % 4), device_id_type=MESH)
+        return carry
+
+    lax.fori_loop(1, spot.count, one, 0)
+    pl.semaphore_wait(barrier, spot.count - 1)
+
+
+class Wires:
+    def __init__(self, send, recv):
+        self.send, self.recv, self.used, self.open = send, recv, 0, []
+
+    def copy(self, src, dst, to):
+        i = self.used
+        self.used += 1
+        copy = pltpu.make_async_remote_copy(
+            src_ref=src,
+            dst_ref=dst,
+            send_sem=self.send.at[i],
+            recv_sem=self.recv.at[i],
+            device_id=to,
+            device_id_type=MESH,
+        )
+        copy.start()
+        self.open.append(copy)
+        return copy
+
+    def drain(self):
+        for copy in self.open:
+            copy.wait_send()
+
+
+def got(copies):
+    for copy in copies:
+        copy.wait_recv()
+
+
+class Swap:
+    def __init__(self, spot, send, recv, src_at, dst_at):
+        self.spot, self.send, self.recv, self.src_at, self.dst_at = spot, send, recv, src_at, dst_at
+
+    def copy(self, i):
+        to = (self.spot.me + i) % self.spot.count
+        return pltpu.make_async_remote_copy(
+            src_ref=self.src_at(to),
+            dst_ref=self.dst_at(self.spot.me),
+            send_sem=self.send.at[i],
+            recv_sem=self.recv.at[i],
+            device_id=(to // 4, to % 4),
+            device_id_type=MESH,
+        )
+
+    def each(self, act):
+        def one(i, carry):
+            act(self.copy(i))
+            return carry
+
+        lax.fori_loop(1, self.spot.count, one, 0)
+
+    def start(self):
+        self.each(lambda copy: copy.start())
+
+    def arrive(self):
+        self.each(lambda copy: copy.wait_recv())
+
+    def leave(self):
+        self.each(lambda copy: copy.wait_send())
+
+
+def block_row(t, plane, c):
+    return (t * 4 + plane) * 2 + c
+
+
+def spread_all(wires, spot, buf, own=None):
+    at = lambda t, plane, c: buf.at[block_row(t, plane, c)]
+    mine = at(spot.z, spot.plane, spot.c)
+    src = mine if own is None else own
+    ring, flat, core = [], [], []
+    for k in range(1, spot.depth):
+        ring.append(wires.copy(src, mine, spot.above(k)))
+    flat.append([wires.copy(src, mine, spot.flip(way)[0]) for way in (1, 2, 3)])
+    core.append(wires.copy(src, mine, spot.sibling()))
+    yield
+    for j in range(1, spot.depth):
+        got([ring[j - 1]])
+        block = at(spot.column[j], spot.plane, spot.c)
+        flat.append([wires.copy(block, block, spot.flip(way)[0]) for way in (1, 2, 3)])
+        core.append(wires.copy(block, block, spot.sibling()))
+    yield
+    for j in range(spot.depth):
+        for way in (1, 2, 3):
+            got([flat[j][way - 1]])
+            block = at(spot.column[j], spot.flip(way)[1], spot.c)
+            core.append(wires.copy(block, block, spot.sibling()))
+    yield
+    got(core)
+
+
+def spread_plane(wires, spot, buf):
+    at = lambda plane: buf.at[plane * 2 + spot.c]
+    mine = at(spot.plane)
+    flat = [wires.copy(mine, mine, spot.flip(way)[0]) for way in (1, 2, 3)]
+    core = [wires.copy(mine, mine, spot.sibling())]
+    yield
+    for way in (1, 2, 3):
+        got([flat[way - 1]])
+        block = at(spot.flip(way)[1])
+        core.append(wires.copy(block, block, spot.sibling()))
+    yield
+    got(core)
+
+
+def sum_plane(wires, spot, parts, pair, near):
+    first = wires.copy(parts.at[:, 1 - spot.c], pair, spot.sibling())
+    yield None
+    got([first])
+    f32 = jnp.float32
+    pair[...] = (parts[:, spot.c].astype(f32) + pair[...].astype(f32)).astype(jnp.bfloat16)
+    flat = [
+        wires.copy(pair.at[spot.flip(way)[1]], near.at[way - 1], spot.flip(way)[0]) for way in (1, 2, 3)
+    ]
+    yield None
+    got(flat)
+    total = pair[spot.plane].astype(f32)
+    for way in range(3):
+        total = total + near[way].astype(f32)
+    yield total
+
+
+def sum_all(wires, spot, parts, pair, near, column, far, out):
+    f32, low = jnp.float32, jnp.bfloat16
+    half = parts.shape[-1] // 2
+    cut = [pl.ds(h * half, half) for h in range(2)]
+    first = [
+        wires.copy(parts.at[:, 1 - spot.c, :, cut[h]], pair.at[:, :, cut[h]], spot.sibling()) for h in range(2)
+    ]
+    yield
+    flat, ring = [], []
+    rows = pair.shape[1]
+    for h in range(2):
+        got([first[h]])
+        for b in range(4 * spot.depth):
+            pair[b, :, cut[h]] = (
+                parts[b, spot.c, :, cut[h]].astype(f32) + pair[b, :, cut[h]].astype(f32)
+            ).astype(low)
+        step = []
+        for way in (1, 2, 3):
+            to, plane = spot.flip(way)
+            for t in range(spot.depth):
+                step.append(
+                    wires.copy(pair.at[t * 4 + plane, :, cut[h]], near.at[way - 1, t, :, cut[h]], to)
+                )
+        flat.append(step)
+    yield
+    for h in range(2):
+        got(flat[h])
+        for t in range(spot.depth):
+            total = pair[t * 4 + spot.plane, :, cut[h]].astype(f32)
+            for way in range(3):
+                total = total + near[way, t, :, cut[h]].astype(f32)
+            column[t, :, cut[h]] = total.astype(low)
+        ring.append(
+            [
+                wires.copy(
+                    column.at[(spot.z + k) % spot.depth, :, cut[h]], far.at[k - 1, :, cut[h]], spot.above(k)
+                )
+                for k in range(1, spot.depth)
+            ]
+        )
+    yield
+    for h in range(2):
+        got(ring[h])
+        total = column[spot.z, :, cut[h]].astype(f32)
+        for k in range(1, spot.depth):
+            total = total + far[k - 1, :, cut[h]].astype(f32)
+        out[:, cut[h]] = total
+    yield
+
+
+def big_gather(wires, spot, ow, od, shards):
+    half, down = WIDE // 2, od.shape[0] // spot.count
+    xn, yn, cn, zn = spot.flip(2)[0], spot.flip(1)[0], spot.sibling(), spot.above(1)
+    here, xp, yp, xy = spot.plane, spot.flip(2)[1], spot.flip(1)[1], spot.flip(3)[1]
+
+    def refs(t, plane, part):
+        r = block_row(t, plane, spot.c)
+        wide, deep = pl.multiple_of(r * TILE, TILE), pl.multiple_of(r * down, down)
+        if part == "A":
+            return [ow.at[pl.ds(wide, TILE), pl.ds(0, half)], od.at[pl.ds(deep, down // 2)]]
+        if part == "B":
+            return [
+                ow.at[pl.ds(wide, TILE), pl.ds(half, half)],
+                od.at[pl.ds(pl.multiple_of(deep + down // 2, down // 2), down // 2)],
+            ]
+        return [ow.at[pl.ds(wide, TILE)], od.at[pl.ds(deep, down)]]
+
+    def go(t, plane, part, to):
+        return [wires.copy(r, r, to) for r in refs(t, plane, part)]
+
+    qkv, attn, gate, up, deep = shards
+    cols, at = [], 0
+    mine = pl.multiple_of(spot.me * TILE, TILE)
+    for ref, a, b in ((qkv, 0, 3072), (attn, 0, 1024), (gate, 0, 2048), (gate, 2048, 2048), (up, 0, 4096)):
+        cols.append((ref.at[:, pl.ds(a, b)], ow.at[pl.ds(mine, TILE), pl.ds(at, b)]))
+        at += b
+    row = pl.multiple_of(spot.me * down, down)
+    deeps = [
+        (deep.at[pl.ds(h * down // 2, down // 2)], od.at[pl.ds(pl.multiple_of(row + h * (down // 2), down // 2), down // 2)])
+        for h in range(2)
+    ]
+
+    def own(part, to):
+        pairs = {"A": cols[:3] + deeps[:1], "B": cols[3:] + deeps[1:], "AB": cols + deeps}[part]
+        return [wires.copy(a, b, to) for a, b in pairs]
+
+    T = spot.column
+    core, ring, fx, fy, sx, sy = [], {}, {}, {}, {}, {}
+
+    def first(j):
+        send = own if j == 0 else (lambda part, to: go(T[j], here, part, to))
+        if j < spot.depth - 1:
+            ring[j] = send("AB", zn)
+        fx[j], fy[j] = send("A", xn), send("B", yn)
+        core.append(send("AB", cn))
+
+    def second(j):
+        got(fx[j])
+        sy[j] = (own("A", yn) if j == 0 else go(T[j], here, "A", yn)) + go(T[j], xp, "A", yn)
+        got(fy[j])
+        sx[j] = (own("B", xn) if j == 0 else go(T[j], here, "B", xn)) + go(T[j], yp, "B", xn)
+        core.append(go(T[j], xp, "A", cn) + go(T[j], yp, "B", cn))
+
+    def third(j):
+        got(sy[j])
+        core.append(go(T[j], yp, "A", cn) + go(T[j], xy, "A", cn))
+        got(sx[j])
+        core.append(go(T[j], xp, "B", cn) + go(T[j], xy, "B", cn))
+
+    first(0)
+    yield
+    for j in range(1, spot.depth):
+        second(j - 1)
+        yield
+        got(ring[j - 1])
+        first(j)
+        yield
+        if j >= 2:
+            third(j - 2)
+            yield
+    second(spot.depth - 1)
+    yield
+    third(spot.depth - 2)
+    third(spot.depth - 1)
+    yield
+    for copies in core:
+        got(copies)
+    yield
+
+
+def run(steps):
+    for _ in steps:
+        pass
+
+
+def sigmoid(v):
+    return 1.0 / (1.0 + jnp.exp(-v))
+
+
+def lanes(shape, axis):
+    return lax.broadcasted_iota(jnp.int32, shape, axis)
+
+
+def flat_dot(a, b, dims=((1,), (0,))):
+    return lax.dot_general(a, b, (dims, ((), ())), preferred_element_type=jnp.float32)
+
+
+def exact_dot(a, b):
+    return jnp.dot(a, b, precision=HIGHEST, preferred_element_type=jnp.float32)
+
+
+def gain_row(values):
+    n_dev, width = values.shape[0], D // values.shape[0]
+    spread = (lanes((128, D), 0) == lanes((128, D), 1) & (width - 1)).astype(jnp.bfloat16)
+    rows = flat_dot(values, spread)
+    return jnp.sum(jnp.where(lanes((n_dev, D), 0) == lanes((n_dev, D), 1) >> (width.bit_length() - 1), rows, 0.0), axis=0, keepdims=True)
+
+
+def tap_rows(spot, small):
+    n_dev = spot.count
+    share = CONV_CH // n_dev
+    col = lanes((1, 512), 1)
+    channel = jnp.where(col < 256, (spot.q + 8 * (col >> 6)) * HEAD_M + (col & 63), DI + col - 256)
+    dev = lanes((n_dev, 512), 0)
+    picks = (channel >= dev * share) & (channel < dev * share + share)
+    owner = jnp.sum(jnp.where(picks, dev, 0), axis=0, keepdims=True)
+    within = lanes((128, 512), 0) == channel - owner * share
+    rows = []
+    for k in range(CONV + 1):
+        values = small[:, TILE + k, 0:128]
+        spread = flat_dot(values, picks.astype(jnp.bfloat16), ((0,), (0,)))
+        rows.append(jnp.sum(jnp.where(within, spread, 0.0), axis=0, keepdims=True))
+    return rows
+
+
+def entry(block, row, lane):
+    at = (lanes(block.shape, 0) == row) & (lanes(block.shape, 1) == lane)
+    return jnp.sum(jnp.where(at, block.astype(jnp.float32), 0.0), keepdims=True).reshape(1, 1)
+
+
+class Slot:
+    def __init__(self, spot, small, x, count):
+        block = small[(spot.z * 2 + x) * 4, TILE : TILE + 16, 0:128].astype(jnp.float32)
+        first = entry(block, 9, 0)
+        second = first + entry(block, 9, 1)
+        number = lambda p: (p >= first).astype(jnp.float32) + (p >= second).astype(jnp.float32)
+        col = lanes((count, 1), 0).astype(jnp.float32)
+        row = lanes((1, count), 1).astype(jnp.float32)
+        docs = number(col)
+        self.keep = (col >= row) & (docs == number(row))
+        self.same = [((col >= s) & (number(col - s) == docs)).astype(jnp.float32) for s in range(CONV)]
+
+
+def shift(block, by):
+    return block if by == 0 else pltpu.roll(block, by % block.shape[0], 0)
+
+
+class Mixed:
+    def __init__(self, spot, slot, own, maps, step_raw, taps, dt_row, rate_row):
+        count = own.shape[0]
+        self.spot, self.slot, self.count = spot, slot, count
+        self.channels = jnp.concatenate([own[:, 256:], maps], axis=1)
+        conv = taps[CONV] + sum(
+            taps[CONV - 1 - s] * (shift(self.channels, s) * slot.same[s]) for s in range(CONV)
+        )
+        self.conv, self.sig = conv, sigmoid(conv)
+        act = conv * self.sig
+        self.inputs = act[:, :256]
+        self.in_map, self.out_map = act[:, 256:384].astype(jnp.bfloat16), act[:, 384:].astype(jnp.bfloat16)
+        self.raw = step_raw + dt_row
+        self.step = jnp.where(self.raw > 20.0, self.raw, jnp.log(1.0 + jnp.exp(jnp.minimum(self.raw, 20.0))))
+        lower = lanes((count, count), 0) >= lanes((count, count), 1)
+        self.upper = (lanes((count, count), 0) <= lanes((count, count), 1)).astype(jnp.float32)
+        self.cum = exact_dot(lower.astype(jnp.float32), self.step * rate_row)
+        self.cum_t, self.step_t = self.cum.T, self.step.T
+        self.inner = flat_dot(self.out_map, self.in_map, ((1,), (1,)))
+
+    def head(self, i):
+        return self.spot.q + 8 * i
+
+    def col(self, by_head, i):
+        return jnp.sum(jnp.where(lanes((1, 128), 1) == self.head(i), by_head, 0.0), axis=1, keepdims=True)
+
+    def row(self, by_head_t, i):
+        return jnp.sum(jnp.where(lanes((128, 1), 0) == self.head(i), by_head_t, 0.0), axis=0, keepdims=True)
+
+    def decay(self, i):
+        gap = jnp.where(self.slot.keep, self.col(self.cum, i) - self.row(self.cum_t, i), 0.0)
+        return jnp.where(self.slot.keep, jnp.exp(gap), 0.0)
+
+
+def pick_lane(row, lane):
+    return jnp.sum(jnp.where(lanes(row.shape, 1) == lane, row, 0.0), axis=1, keepdims=True)
+
+
+N_WIRES = 256
+
+
+def forward_kernel(
+    depth,
+    rows_ref,
+    patch_ref,
+    cols_ref,
+    vec_ref,
+    out_ref,
+    heads_ref,
+    qkv,
+    attn,
+    gate,
+    up,
+    down,
+    ow,
+    od,
+    sum_ref,
+    mixed_ref,
+    small_ref,
+    bytes_ref,
+    norm_ref,
+    proj_ref,
+    head_w_ref,
+    own_ref,
+    maps_ref,
+    step_ref,
+    core_ref,
+    parts,
+    pair,
+    near,
+    column,
+    far,
+    parts8,
+    pair8,
+    near8,
+    send,
+    recv,
+    swap_send,
+    swap_recv,
+    local,
+):
+    f32, low = jnp.float32, jnp.bfloat16
+    spot = Spot(depth)
+    count = 128
+    wires = Wires(send, recv)
+    mine = pl.multiple_of(spot.me * TILE, TILE)
+    bytes_ref[pl.ds(mine, TILE)] = rows_ref[:, pl.ds(pl.multiple_of(spot.me * 256, 256), 256)]
+    small_ref[spot.me] = vec_ref[...]
+    proj_ref[pl.ds(mine, TILE)] = cols_ref[spot.q]
+    head_w_ref[spot.z] = out_ref[...]
+    greet(spot)
+
+    def lanes_of(to):
+        return rows_ref.at[:, pl.ds(pl.multiple_of(to * 256, 256), 256)]
+
+    swap_bytes = Swap(
+        spot,
+        swap_send.at[0],
+        swap_recv.at[0],
+        lanes_of,
+        lambda me: bytes_ref.at[pl.ds(pl.multiple_of(me * TILE, TILE), TILE)],
+    )
+    swap_bytes.start()
+    big = big_gather(wires, spot, ow, od, (qkv, attn, gate, up, down))
+    swap_proj = Swap(
+        spot,
+        swap_send.at[1],
+        swap_recv.at[1],
+        lambda to: cols_ref.at[to % 8],
+        lambda me: proj_ref.at[pl.ds(pl.multiple_of(me * TILE, TILE), TILE)],
+    )
+    swap_proj.start()
+    small = spread_all(wires, spot, small_ref)
+    next(small)
+    head_w = [wires.copy(out_ref, head_w_ref.at[spot.z], spot.above(k)) for k in range(1, depth)]
+    next(big)
+    own_rows = []
+    at = 0
+    for i, ref in enumerate((qkv, attn, gate, up)):
+        width = ref.shape[1]
+        own_rows.append(pltpu.make_async_copy(ref, ow.at[pl.ds(mine, TILE), pl.ds(at, width)], local.at[i]))
+        at += width
+    deep = down.shape[0]
+    own_rows.append(
+        pltpu.make_async_copy(down, od.at[pl.ds(pl.multiple_of(spot.me * deep, deep), deep)], local.at[4])
+    )
+    for copy in own_rows:
+        copy.start()
+    swap_bytes.arrive()
+
+    for b in range(4):
+        block = flat_dot(bytes_ref[pl.ds(b * 256, 256)], patch_ref[...]).astype(low)
+        parts[pl.ds(b * 4, 4)] = block.reshape(4, 2, TILE, D)
+    total = sum_all(wires, spot, parts, pair, near, column, far, sum_ref)
+    next(total)
+    next(small)
+    next(total)
+    next(big)
+    next(total)
+    next(small)
+    next(total)
+    run(small)
+    patch_sum = sum_ref[...]
+    scale = lax.rsqrt(jnp.mean(patch_sum * patch_sum, axis=1, keepdims=True) + EPSILON)
+    gain = gain_row(small_ref[:, TILE + 5, 0:128])
+    norm_ref[spot.q] = (patch_sum * scale * gain).astype(low)
+    plane = spread_plane(wires, spot, norm_ref)
+    next(plane)
+    next(plane)
+    swap_proj.arrive()
+    taps = tap_rows(spot, small_ref)
+    run(plane)
+    next(big)
+
+    norm = norm_ref[...].reshape(2 * count, D)
+    own_ref[...] = flat_dot(norm, proj_ref[...])
+    maps_ref[...] = flat_dot(norm, small_ref[:, :TILE, 0:256].reshape(D, 256))
+    step_ref[...] = flat_dot(norm, small_ref[:, :TILE, 256:384].reshape(D, 128))
+    dt_row, rate_row, skip_row = heads_ref[0:1], heads_ref[1:2], heads_ref[2:3]
+    got(head_w)
+    gains = jnp.concatenate(
+        [small_ref[spot.q + 8 * i, TILE : TILE + 16, 0:HEAD_M][6:7].astype(f32) for i in range(4)], axis=1
+    )
+    for x in range(2):
+        at = pl.ds(x * count, count)
+        slot = Slot(spot, small_ref, x, count)
+        own, maps = own_ref[at], maps_ref[at]
+        mix = Mixed(spot, slot, own, maps, step_ref[at], taps, dt_row, rate_row)
+        outs = []
+        for i in range(4):
+            inputs = mix.inputs[:, i * HEAD_M : (i + 1) * HEAD_M]
+            mixing = (mix.decay(i) * mix.inner * mix.row(mix.step_t, i)).astype(low)
+            skip = pick_lane(skip_row, mix.head(i))
+            outs.append(flat_dot(mixing, inputs.astype(low)) + skip * inputs)
+        core = jnp.concatenate(outs, axis=1)
+        core_ref[at] = core
+        raw = own[:, :256]
+        gated = core * raw * sigmoid(raw)
+        part = flat_dot((gated * gains).astype(low), head_w_ref[...].reshape(256, D))
+        squares = jnp.sum(gated * gated, axis=1, keepdims=True)
+        parts8[pl.ds(x * 2, 2), :, :, pl.ds(0, D)] = part.astype(low).reshape(2, 2, TILE, D)
+        parts8[pl.ds(x * 2, 2), :, :, pl.ds(D, 128)] = (
+            jnp.broadcast_to(squares, (count, 128)).astype(low).reshape(2, 2, TILE, 128)
+        )
+    for total in sum_plane(wires, spot, parts8, pair8, near8):
+        pass
+    mixed_ref[...] = total
+    for copy in own_rows:
+        copy.wait()
+    run(big)
+    wires.drain()
+    swap_bytes.leave()
+    swap_proj.leave()
+
+
+def forward_call(depth, n_dev, rows2, patch_proj, cols, vectors, out_proj, heads, qkv, attn, gate, up, down):
+    f32, low = jnp.float32, jnp.bfloat16
+    vmem = pl.BlockSpec(memory_space=pltpu.VMEM)
+    anywhere = pl.BlockSpec(memory_space=pl.ANY)
+    shape = jax.ShapeDtypeStruct
+    plane_patches = 8 * TILE
+    outs = [
+        shape((D, WIDE), low),
+        shape((down.shape[0] * n_dev, D), low),
+        shape((TILE, D), f32),
+        shape((TILE, EXT), f32),
+        shape((n_dev, SMALL_ROWS, SMALL_COLS), low),
+        shape((n_dev * TILE, 256), low),
+        shape((8, TILE, D), low),
+        shape((n_dev * TILE, 512), low),
+        shape((depth, HEAD_M, D), low),
+        shape((plane_patches, 512), f32),
+        shape((plane_patches, 256), f32),
+        shape((plane_patches, 128), f32),
+        shape((plane_patches, 256), f32),
+    ]
+    scratch = [
+        pltpu.VMEM((16, 2, TILE, D), low),
+        pltpu.VMEM((16, TILE, D), low),
+        pltpu.VMEM((3, depth, TILE, D), low),
+        pltpu.VMEM((depth, TILE, D), low),
+        pltpu.VMEM((depth - 1, TILE, D), low),
+        pltpu.VMEM((4, 2, TILE, EXT), low),
+        pltpu.VMEM((4, TILE, EXT), low),
+        pltpu.VMEM((3, TILE, EXT), low),
+        pltpu.SemaphoreType.DMA((N_WIRES,)),
+        pltpu.SemaphoreType.DMA((N_WIRES,)),
+        pltpu.SemaphoreType.DMA((2, n_dev)),
+        pltpu.SemaphoreType.DMA((2, n_dev)),
+        pltpu.SemaphoreType.DMA((5,)),
+    ]
+    return pl.pallas_call(
+        partial(forward_kernel, depth),
+        out_shape=outs,
+        in_specs=[vmem] * 6 + [anywhere] * 5,
+        out_specs=[anywhere] * 2 + [vmem] * 11,
+        scratch_shapes=scratch,
+        compiler_params=pltpu.CompilerParams(
+            collective_id=0, has_side_effects=True, vmem_limit_bytes=56 * 2**20
+        ),
+        name="global_forward",
+    )(rows2, patch_proj, cols, vectors, out_proj, heads, qkv, attn, gate, up, down)
+
+
 AX = ("dp", "fsdp")
 BC = 2 * STATE
 OWN = 2 * HEAD_M + 1
@@ -659,60 +1268,46 @@
     slots = depth_fsdp[0]
     slot_patches = patches * depth_fsdp[1]
 
-    vector = jnp.concatenate(
-        [
-            global_gain,
-            mixer_gain,
-            attn_gain,
-            ffn_gain,
-            conv_weight.reshape(-1),
-            conv_bias,
-            doc_lengths.reshape(-1).astype(low),
-        ]
-    )
     shard_rows = in_proj.shape[0]
-    tail = -(-vector.shape[0] // BC)
-    vector = jnp.pad(vector, (0, tail * BC - vector.shape[0])).reshape(tail, BC)
-    small = jnp.concatenate([in_proj[:, 2 * DI : 2 * DI + BC], vector], axis=0)
-    small = gather_small(grid, small).reshape(n_dev, shard_rows + tail, BC)
-    maps_proj = small[:, :shard_rows].reshape(D, BC)
-    flat = small[:, shard_rows:].reshape(n_dev, -1)
-    cuts, at = [], 0
-    for width in (D, DI, D, D, CONV_CH * CONV, CONV_CH, n_dev * 2):
-        width //= n_dev
-        cuts.append(flat[:, at : at + width])
-        at += width
-    gain_g, gain_m, gain_a, gain_f = (cut.reshape(-1).astype(f32) for cut in cuts[:4])
-    conv_w = cuts[4].reshape(CONV_CH, CONV).astype(f32)
-    conv_b = cuts[5].reshape(CONV_CH).astype(f32)
-    lengths = cuts[6].reshape(slots, depth_fsdp[1], 2)[:, 0].astype(jnp.int32)
+    maps_and_steps = jnp.pad(in_proj[:, 2 * DI :], ((0, 0), (0, SMALL_COLS - BC - MHEADS)))
+    lines = [conv_weight[:, k] for k in range(CONV)]
+    lines += [conv_bias, global_gain, mixer_gain, attn_gain, ffn_gain, doc_lengths.reshape(-1).astype(low)]
+    lines = jnp.stack([jnp.pad(line, (0, SMALL_COLS - line.shape[0])) for line in lines])
+    vectors = jnp.concatenate(
+        [maps_and_steps, lines, jnp.zeros((SMALL_ROWS - shard_rows - lines.shape[0], SMALL_COLS), low)]
+    )
+    by_place = lambda cols: cols.reshape(shard_rows, 4, 8, HEAD_M).transpose(2, 0, 1, 3).reshape(8, shard_rows, 256)
+    cols = jnp.concatenate([by_place(in_proj[:, :DI]), by_place(in_proj[:, DI : 2 * DI])], axis=2)
+    heads_in = jnp.pad(jnp.stack([dt_bias, -jnp.exp(a_log), skip_weight]), ((0, 5), (0, 128 - MHEADS)))
+    rows2 = byte_states.reshape(patches, PATCH * D)
+    (wide, deep, patch_sum, mixed, small, all_bytes, norm8, proj8, head_w, own8, maps8, step8, core8) = forward_call(
+        grid.depth, n_dev, rows2, patch_proj, cols, vectors, out_proj, heads_in, qkv_proj, attn_out, gate_proj, up_proj, down_proj
+    )
+    lines = small[:, shard_rows : shard_rows + 10]
+    gain_g, gain_a, gain_f = (lines[:, k, : D // n_dev].reshape(-1).astype(f32) for k in (5, 7, 8))
+    gain_m = lines[:, 6, : DI // n_dev].reshape(-1).astype(f32)
+    my_places = share_at = lax.axis_index("fsdp") * patches + jnp.arange(patches, dtype=jnp.int32)
+    live = jnp.repeat((my_places < doc_lengths[0, 0] + doc_lengths[0, 1]).astype(f32), PATCH)[:, None]
+    qk, vals, attn_o = wide[:, : 2 * D], wide[:, 2 * D : 3 * D], wide[:, 3 * D : 4 * D]
+    gate_w, up_w = wide[:, 4 * D : 8 * D], wide[:, 8 * D :]
+    down_a, down_b = deep[:, : D // 2], deep[:, D // 2 :]
+    raw_mixed = mixed[:, :D]
+    mixer_r = lax.rsqrt(mixed[:, D : D + 1] / DI + EPSILON)
+    mixed_patch = patch_sum + raw_mixed * mixer_r
+
+    conv_w = lines[:, :CONV, : CONV_CH // n_dev].transpose(0, 2, 1).reshape(CONV_CH, CONV).astype(f32)
+    conv_b = lines[:, CONV, : CONV_CH // n_dev].reshape(-1).astype(f32)
+    lengths = lines[:, 9, :2].reshape(slots, depth_fsdp[1], 2)[:, 0].astype(jnp.int32)
     places = jnp.arange(slot_patches, dtype=jnp.int32)[None, :]
     first_end = lengths[:, :1]
     docs = (places >= first_end).astype(jnp.int32) + (places >= first_end + lengths[:, 1:]).astype(jnp.int32)
-    my_docs = lax.dynamic_slice(docs.reshape(-1), (me * patches,), (patches,))
-    live = jnp.repeat((my_docs < 2).astype(f32), PATCH)[:, None]
-
-    def gathered(shard, order):
-        return gather_stream(grid, shard, order).reshape(-1, shard.shape[1])
-
-    patch_bytes = byte_states.reshape(patches, n_dev, -1).transpose(1, 0, 2)
-    all_bytes = exchange(patch_bytes).reshape(n_dev * patches, -1)
     heads_of = lambda cols: cols.reshape(shard_rows, MHEADS, -1)
     own_cols = jnp.concatenate(
         [heads_of(in_proj[:, :DI]), heads_of(in_proj[:, DI : 2 * DI]), heads_of(in_proj[:, 2 * DI + BC :])],
         axis=2,
     ).transpose(1, 0, 2)
     own_proj = exchange(own_cols).reshape(D, OWN)
-
-    qk = gathered(qkv_proj[:, : 2 * D], "zxyc")
-    vals = gathered(qkv_proj[:, 2 * D :], "zyxc")
-    attn_o = gathered(attn_out, "zyxc")
-    gate_w = gathered(gate_proj, "zxyc")
-    up_w = gathered(up_proj, "zyxc")
-    down_a = gathered(down_proj[:, : D // 2], "xyzc")
-    down_b = gathered(down_proj[:, D // 2 :], "yxzc")
-
-    patch_sum = scatter_small(grid, product(all_bytes, patch_proj))
+    maps_proj = small[:, :shard_rows, :BC].reshape(D, BC)
     global_low = rms_scale(patch_sum, gain_g).astype(low)
     global_all = gather_small(grid, global_low)
     own = product(global_all, own_proj)
@@ -737,12 +1332,6 @@
     sig_m = jax.nn.sigmoid(gate_raw)
     gated = core * gate_raw * sig_m
     my_gain = mine(gain_m, HEAD_M)[None]
-    mixer_part = product((gated * my_gain).astype(low), out_proj)
-    squares = jnp.sum(gated * gated, axis=1, keepdims=True)
-    mixed = scatter_small(grid, jnp.concatenate([mixer_part, jnp.pad(squares, ((0, 0), (0, 127)))], axis=1))
-    raw_mixed = mixed[:, :D]
-    mixer_r = lax.rsqrt(mixed[:, D : D + 1] / DI + EPSILON)
-    mixed_patch = patch_sum + raw_mixed * mixer_r
 
     streams = byte_states.astype(f32) + jnp.repeat(mixed_patch, PATCH, axis=0)
     normed = rms_scale(streams, gain_a).astype(low)

time: 1120 us -> 927 us (0.83)
  waiting for transfers between devices: 465 us -> 216 us
  Pallas kernels: 0 us -> 242 us
  local copies, waits for them, and re-layouts: 249 us -> 147 us
  starting transfers between devices: 177 us -> 100 us
    ppermute x168 -> x74, waiting for transfers between devices: 447 us -> 184 us  [send(): return lax.ppermute(block, AX, self.route(dim, step))]
    pallas_call x0 -> x1, Pallas kernels: none -> 242 us  [forward_call(): pl.pallas_call(partial(forward_kernel, depth), out_shape=outs, in_specs=[...]
    dynamic_update_slice x129 -> x36, local copies, waits for them, and re-layouts: 98.5 us -> 28.9 us  [put(): lax.dynamic_update_slice(whole, part, [jnp.asarray(p, jnp.int32) for p in...]
    ppermute x168 -> x74, starting transfers between devices: 154 us -> 86.3 us  [send(): return lax.ppermute(block, AX, self.route(dim, step))]
    all_to_all x4 -> x3, waiting for transfers between devices: 17.5 us -> 31.8 us  [exchange(): return lax.all_to_all(blocks, AX, 0, 0, tiled=False)]
    another operation x20 -> x16, local copies, waits for them, and re-layouts: 13.7 us -> 1.86 us
    all_to_all x4 -> x3, starting transfers between devices: 23.3 us -> 14.2 us  [exchange(): return lax.all_to_all(blocks, AX, 0, 0, tiled=False)]
    dot_general x11 -> x9, matrix products: 36.4 us -> 27.7 us  [product(): return jnp.dot(left, right, preferred_element_type=jnp.float32)]
  transfers between devices with their start and end apart: 172 -> 77, of which waited for: 88 -> 42; matrix products, arithmetic and copies ran while one was open for 31% -> 36% of each run, Pallas kernels for 0% -> 0%
where the time goes in v2:
time: 927 us; the launch traced here: 912 us
  Pallas kernels  242 us (26%)
  waiting for transfers between devices  216 us (23%)
  local copies, waits for them, and re-layouts  147 us (16%)
  matrix products  130 us (14%)
  starting transfers between devices  100 us (11%)
  other arithmetic  69.4 us (7%)
    pallas_call x1, Pallas kernels, forward_call(): pl.pallas_call(partial(forward_kernel, depth), out_shape=outs, in_specs=[...  242 us
    ppermute x74, waiting for transfers between devices, send(): return lax.ppermute(block, AX, self.route(dim, step))  184 us
    ppermute x74, starting transfers between devices, send(): return lax.ppermute(block, AX, self.route(dim, step))  86.3 us
    dot_general x18, matrix products, weight_grad(): lax.dot_general(left, right, (((0,), (0,)), ((), ())), preferred_element_...  41.8 us
    dot_general x11, matrix products, input_grad(): lax.dot_general(grad_rows, weight, (((1,), (1,)), ((), ())), preferred_el...  38.7 us
    all_to_all x3, waiting for transfers between devices, exchange(): return lax.all_to_all(blocks, AX, 0, 0, tiled=False)  31.8 us
    dynamic_update_slice x36, local copies, waits for them, and re-layouts, put(): lax.dynamic_update_slice(whole, part, [jnp.asarray(p, jnp.int32) for p in...  28.9 us
    dot_general x9, matrix products, product(): return jnp.dot(left, right, preferred_element_type=jnp.float32)  27.7 us
  transfers between devices with their start and end apart: 77, of which 42 were waited for; matrix products, arithmetic and copies ran while one was open for 36% of the time, Pallas kernels for 0%

profile of v2, /device:TPU:8, one launch (start us, length us, event | category | flops | bytes accessed | tf_op | source)
XLA Modules:
  0.0 911.8 jit_solution(14730040938392111571)
XLA Ops:
  8.7 241.9 %global_forward.1 = (bf16[1024,12288]{1,0:T(8,128)(2,1)}, bf16[4096,1024]{1,0:T(8,128)(2,1)}, f32[32,1024]{1,0:T(8,128)}, f32[32,1152]{1,0:T(8,128)}, bf16[32,48...) custom-call(bf16[32,8192]{1,0:T(8,128)(2,1)} %reshape.700.rows_ref, ...), custom_call_target="tpu_custom_call" | custom-call | tf_op jit(solution)/shard_map/global_forward/pallas_call | solution.py:1048
  256.1 5.0 collective-permute-start.9
  264.4 4.4 fusion.20
  280.1 2.6 multiply_reduce_fusion.9
  284.5 3.7 fusion.12
  288.2 3.5 convolution_add_fusion
  291.9 5.9 fusion.3
  297.9 7.1 multiply_convert_fusion.1
  307.6 5.8 fusion.1
  313.4 6.6 multiply_reduce_fusion.1
  321.3 3.1 fusion.50
  328.4 2.6 multiply_reduce_fusion
  336.1 4.1 fusion.16
  340.8 3.4 multiply_reduce_fusion.2
  358.6 3.7 all-to-all-start
  385.2 4.9 convolution_convert_fusion.1
  390.1 3.3 convolution_convert_fusion
  393.4 3.2 reshape.751
  396.6 6.3 constant_dynamic-slice_fusion.5
  402.9 5.0 copy.379
  428.4 3.7 copy.378
  457.9 3.2 collective-permute-done.5
  469.9 2.7 collective-permute-done.4
  509.8 2.7 copy.334
  513.4 3.2 fusion.57
  523.9 2.8 maximum_select_fusion
  531.5 2.9 multiply_reduce_fusion.15
  555.7 2.8 convolution_add_fusion.1
  559.3 2.7 fusion.64
  566.9 6.3 collective-permute-done.46
  574.8 4.0 collective-permute-done.41
  579.0 5.9 collective-permute-done.47
  584.9 6.0 collective-permute-done.42
  591.0 6.5 collective-permute-done.48
  597.5 6.4 collective-permute-done.43
  604.6 5.3 collective-permute-done.49
  621.1 9.4 %collective-permute-done.63 = bf16[2,2,128,512]{3,2,0,1:T(8,128)(2,1)S(1)} collective-permute-done((bf16[2,2,128,512]{3,2,0,1:T(8,128)(2,1)S(1)}, bf16[2,2,128,512]{3,2,0,1:T(8,128)(2,1)S(1)}, u32[]{:S(2)}, u32[]{:S(2)}) %collective-permute-start.63) | collective-permute-done | bytes 524320 | tf_op jit(solution)/shard_map/ppermute | solution.py:1089
  633.4 13.5 %collective-permute-done.69 = bf16[2,2,128,512]{3,2,1,0:T(8,128)(2,1)S(1)} collective-permute-done((bf16[2,2,128,512]{3,2,1,0:T(8,128)(2,1)S(1)}, bf16[2,2,128,512]{3,2,1,0:T(8,128)(2,1)S(1)}, u32[]{:S(2)}, u32[]{:S(2)}) %collective-permute-start.69) | collective-permute-done | bytes 524320 | tf_op jit(solution)/shard_map/ppermute | solution.py:1089
  648.4 4.8 collective-permute-done.19
  654.3 6.7 collective-permute-done.17
  662.1 3.9 collective-permute-done.20
  667.4 3.5 collective-permute-done.18
  671.0 3.9 collective-permute-start.23
  685.2 5.7 collective-permute-done.70
  696.9 2.7 collective-permute-done.26
  702.0 2.7 pad_maximum_fusion
  704.7 4.0 all-to-all-start.2
  713.0 7.8 collective-permute-done.29
  723.5 6.0 collective-permute-done.28
  731.1 6.3 collective-permute-done.30
  745.8 11.2 %collective-permute-done.35 = bf16[32,2048]{1,0:T(8,128)(2,1)S(1)} collective-permute-done((bf16[32,2048]{1,0:T(8,128)(2,1)S(1)}, bf16[32,2048]{1,0:T(8,128)(2,1)S(1)}, u32[]{:S(2)}, u32[]{:S(2)}) %collective-permute-start.35) | collective-permute-done | bytes 131104 | tf_op jit(solution)/shard_map/ppermute | solution.py:1089
  768.0 2.9 collective-permute-done.66
  778.5 3.5 add_convert_fusion.1
  784.8 3.5 add_convert_fusion
  796.3 6.5 all-to-all-start.1
  810.0 31.8 %all-to-all-done.1 = bf16[32,32,256]{2,1,0:T(8,128)(2,1)} async-done(((bf16[32,32,256]{2,1,0:T(8,128)(2,1)}), bf16[32,32,256]{2,1,0:T(8,128)(2,1)}, u32[]{:S(2)}, u32[]{:S(2)}) %all-to-all-start.1) | async-done | bytes 524320 | tf_op jit(solution)/shard_map/all_to_all | solution.py:1191
  855.7 19.9 %collective-permute-done.52 = bf16[4,32,4096]{2,1,0:T(8,128)(2,1)S(1)} collective-permute-done((bf16[4,32,4096]{2,1,0:T(8,128)(2,1)S(1)}, bf16[4,32,4096]{2,1,0:T(8,128)(2,1)S(1)}, u32[]{:S(2)}, u32[]{:S(2)}) %collective-permute-start.52) | collective-permute-done | bytes 1048608 | tf_op jit(solution)/shard_map/ppermute | solution.py:1089
  875.8 2.6 collective-permute-start.53
  879.7 2.6 collective-permute-start.59
  887.0 3.0 collective-permute-done.59
  892.6 3.0 collective-permute-done.54
  898.2 3.0 collective-permute-done.60
  903.8 3.0 collective-permute-done.55
  907.7 3.1 collective-permute-done.61
  (721 shorter events, 331.2 us)
Async XLA Ops:
  256.1 177.2 %collective-permute-start.8 = (bf16[32,1024]{1,0:T(8,128)(2,1)}, bf16[32,1024]{1,0:T(8,128)(2,1)}, u32[]{:S(2)}, u32[]{:S(2)}) collective-permute-start(bf16[32,1024]{1,0:T(8,128)(2,1)} %get-tuple-element.123), channel_id=1, source_target_pairs={{0,8},{1,9},{2,10},{3,11},{4,12},{5,13},{6,14},{7,15},{8,16},{9,17... | collective-permute-start | bytes 196616 | tf_op jit(solution)/shard_map/ppermute | solution.py:1089
  256.1 179.0 %collective-permute-start.9 = (bf16[32,1024]{1,0:T(8,128)(2,1)}, bf16[32,1024]{1,0:T(8,128)(2,1)}, u32[]{:S(2)}, u32[]{:S(2)}) collective-permute-start(bf16[32,1024]{1,0:T(8,128)(2,1)} %get-tuple-element.123), channel_id=1, source_target_pairs={{0,16},{1,17},{2,18},{3,19},{4,20},{5,21},{6,22},{7,23},{8,24},{9,... | collective-permute-start | bytes 196616 | tf_op jit(solution)/shard_map/ppermute | solution.py:1089
  261.2 175.5 %collective-permute-start.10 = (bf16[32,1024]{1,0:T(8,128)(2,1)}, bf16[32,1024]{1,0:T(8,128)(2,1)}, u32[]{:S(2)}, u32[]{:S(2)}) collective-permute-start(bf16[32,1024]{1,0:T(8,128)(2,1)} %get-tuple-element.123), channel_id=1, source_target_pairs={{0,24},{1,25},{2,26},{3,27},{4,28},{5,29},{6,30},{7,31},{8,0},{9,1... | collective-permute-start | bytes 196616 | tf_op jit(solution)/shard_map/ppermute | solution.py:1089
  347.5 93.9 %collective-permute-start = (bf16[32,1152]{1,0:T(8,128)(2,1)}, bf16[32,1152]{1,0:T(8,128)(2,1)}, u32[]{:S(2)}, u32[]{:S(2)}) collective-permute-start(bf16[32,1152]{1,0:T(8,128)(2,1)} %fusion.228), channel_id=1, source_target_pairs={{0,8},{1,9},{2,10},{3,11},{4,12},{5,13},{6,14},{7,15},{8,16},{9,17... | collective-permute-start | bytes 221192 | tf_op jit(solution)/shard_map/ppermute | solution.py:1089
  349.5 95.2 %collective-permute-start.1 = (bf16[32,1152]{1,0:T(8,128)(2,1)}, bf16[32,1152]{1,0:T(8,128)(2,1)}, u32[]{:S(2)}, u32[]{:S(2)}) collective-permute-start(bf16[32,1152]{1,0:T(8,128)(2,1)} %fusion.228), channel_id=1, source_target_pairs={{0,16},{1,17},{2,18},{3,19},{4,20},{5,21},{6,22},{7,23},{8,24},{9,... | collective-permute-start | bytes 221192 | tf_op jit(solution)/shard_map/ppermute | solution.py:1089
  358.6 141.3 %all-to-all-start = ((bf16[32,32,129]{2,1,0:T(8,128)(2,1)}), bf16[32,32,129]{2,1,0:T(8,128)(2,1)}, u32[]{:S(2)}, u32[]{:S(2)}) async-start(bf16[32,32,129]{2,1,0:T(8,128)(2,1)} %maximum_bitcast_fusion), calls=%async_computation | async-start | bytes 1048576 | tf_op jit(solution)/shard_map/all_to_all | solution.py:1191
  433.3 14.4 %collective-permute-start.2 = (bf16[32,1152]{1,0:T(8,128)(2,1)}, bf16[32,1152]{1,0:T(8,128)(2,1)S(1)}, u32[]{:S(2)}, u32[]{:S(2)}) collective-permute-start(bf16[32,1152]{1,0:T(8,128)(2,1)} %fusion.228), channel_id=1, source_target_pairs={{0,24},{1,25},{2,26},{3,27},{4,28},{5,29},{6,30},{7,31},{8,0},{9,1... | collective-permute-start | bytes 221192 | tf_op jit(solution)/shard_map/ppermute | solution.py:1089
  435.2 54.4 %collective-permute-start.44 = (bf16[512,1024]{1,0:T(8,128)(2,1)}, bf16[512,1024]{1,0:T(8,128)(2,1)}, u32[]{:S(2)}, u32[]{:S(2)}) collective-permute-start(bf16[512,1024]{1,0:T(8,128)(2,1)} %convolution_convert_fusion.5), channel_id=1, source_target_pairs={{0,1},{1,0},{2,3},{3,2},{4,5},{5,4},{6,7},{7,6},{8,9},{9,8},{10,11... | collective-permute-start | bytes 3145736 | tf_op jit(solution)/shard_map/ppermute | solution.py:1089
  436.6 54.7 %collective-permute-start.38 = (bf16[512,1024]{1,0:T(8,128)(2,1)}, bf16[512,1024]{1,0:T(8,128)(2,1)}, u32[]{:S(2)}, u32[]{:S(2)}) collective-permute-start(bf16[512,1024]{1,0:T(8,128)(2,1)} %convolution_convert_fusion.6), channel_id=1, source_target_pairs={{0,1},{1,0},{2,3},{3,2},{4,5},{5,4},{6,7},{7,6},{8,9},{9,8},{10,11... | collective-permute-start | bytes 3145736 | tf_op jit(solution)/shard_map/ppermute | solution.py:1089
  441.5 12.2 %collective-permute-start.11 = (bf16[4,32,512]{2,1,0:T(8,128)(2,1)}, bf16[4,32,512]{2,1,0:T(8,128)(2,1)}, u32[]{:S(2)}, u32[]{:S(2)}) collective-permute-start(bf16[4,32,512]{2,1,0:T(8,128)(2,1)} %get-tuple-element.192), channel_id=1, source_target_pairs={{0,4},{1,5},{2,6},{3,7},{4,0},{5,1},{6,2},{7,3},{8,12},{9,13},{10,... | collective-permute-start | bytes 393224 | tf_op jit(solution)/shard_map/ppermute | solution.py:1089
  444.7 10.3 %collective-permute-start.13 = (bf16[4,32,512]{2,1,0:T(8,128)(2,1)}, bf16[4,32,512]{2,1,0:T(8,128)(2,1)S(1)}, u32[]{:S(2)}, u32[]{:S(2)}) collective-permute-start(bf16[4,32,512]{2,1,0:T(8,128)(2,1)} %get-tuple-element.191), channel_id=1, source_target_pairs={{0,2},{1,3},{2,0},{3,1},{4,6},{5,7},{6,4},{7,5},{8,10},{9,11},{10,... | collective-permute-start | bytes 393224 | tf_op jit(solution)/shard_map/ppermute | solution.py:1089
  450.2 7.6 collective-permute-start.3
  453.7 7.3 collective-permute-start.5
  455.0 9.7 %collective-permute-start.12 = (bf16[2,4,32,512]{3,2,1,0:T(8,128)(2,1)S(1)}, bf16[2,4,32,512]{3,2,1,0:T(8,128)(2,1)S(1)}, u32[]{:S(2)}, u32[]{:S(2)}) collective-permute-start(bf16[2,4,32,512]{3,2,1,0:T(8,128)(2,1)S(1)} %pad_maximum_fusion.8), channel_id=1, source_target_pairs={{0,2},{1,3},{2,0},{3,1},{4,6},{5,7},{6,4},{7,5},{8,10},{9,11},{10,... | collective-permute-start | bytes 786440 | tf_op jit(solution)/shard_map/ppermute | solution.py:1089
  457.7 156.7 %collective-permute-start.32 = (bf16[512,2048]{1,0:T(8,128)(2,1)}, bf16[512,2048]{1,0:T(8,128)(2,1)}, u32[]{:S(2)}, u32[]{:S(2)}) collective-permute-start(bf16[512,2048]{1,0:T(8,128)(2,1)} %convolution_convert_fusion.4), channel_id=1, source_target_pairs={{0,1},{1,0},{2,3},{3,2},{4,5},{5,4},{6,7},{7,6},{8,9},{9,8},{10,11... | collective-permute-start | bytes 6291464 | tf_op jit(solution)/shard_map/ppermute | solution.py:1089
  461.0 6.4 collective-permute-start.14
  464.8 7.9 collective-permute-start.4
  467.4 13.5 %collective-permute-start.6 = (bf16[2,4,32,576]{3,2,1,0:T(8,128)(2,1)}, bf16[2,4,32,576]{3,2,1,0:T(8,128)(2,1)}, u32[]{:S(2)}, u32[]{:S(2)}) collective-permute-start(bf16[2,4,32,576]{3,2,1,0:T(8,128)(2,1)} %pad_maximum_fusion.5), channel_id=1, source_target_pairs={{0,4},{1,5},{2,6},{3,7},{4,0},{5,1},{6,2},{7,3},{8,12},{9,13},{10,... | collective-permute-start | bytes 884744 | tf_op jit(solution)/shard_map/ppermute | solution.py:1089
  472.6 24.8 %collective-permute-start.15 = (bf16[4,2,2,32,1024]{4,3,2,1,0:T(8,128)(2,1)S(1)}, bf16[4,2,2,32,1024]{4,3,2,1,0:T(8,128)(2,1)}, u32[]{:S(2)}, u32[]{:S(2)}) collective-permute-start(bf16[4,2,2,32,1024]{4,3,2,1,0:T(8,128)(2,1)S(1)} %fusion.205), channel_id=1, source_target_pairs={{0,1},{1,0},{2,3},{3,2},{4,5},{5,4},{6,7},{7,6},{8,9},{9,8},{10,11... | collective-permute-start | bytes 3145736 | tf_op jit(solution)/shard_map/ppermute | solution.py:1089
  480.9 297.6 %collective-permute-start.50 = (bf16[512,4096]{1,0:T(8,128)(2,1)}, bf16[512,4096]{1,0:T(8,128)(2,1)}, u32[]{:S(2)}, u32[]{:S(2)}) collective-permute-start(bf16[512,4096]{1,0:T(8,128)(2,1)} %convolution_convert_fusion.1), channel_id=1, source_target_pairs={{0,1},{1,0},{2,3},{3,2},{4,5},{5,4},{6,7},{7,6},{8,9},{9,8},{10,11... | collective-permute-start | bytes 12582920 | tf_op jit(solution)/shard_map/ppermute | solution.py:1089
  489.6 33.4 %collective-permute-start.7 = (bf16[4,2,2,32,1152]{4,3,2,1,0:T(8,128)(2,1)}, bf16[4,2,2,32,1152]{4,3,2,1,0:T(8,128)(2,1)}, u32[]{:S(2)}, u32[]{:S(2)}) collective-permute-start(bf16[4,2,2,32,1152]{4,3,2,1,0:T(8,128)(2,1)} %dynamic_update_slice.128), channel_id=1, source_target_pairs={{0,1},{1,0},{2,3},{3,2},{4,5},{5,4},{6,7},{7,6},{8,9},{9,8},{10,11... | collective-permute-start | bytes 3538952 | tf_op jit(solution)/shard_map/ppermute | solution.py:1089
  495.1 21.5 %collective-permute-start.39 = (bf16[4,2,32,1024]{3,2,0,1:T(8,128)(2,1)}, bf16[4,2,32,1024]{3,2,0,1:T(8,128)(2,1)}, u32[]{:S(2)}, u32[]{:S(2)}) collective-permute-start(bf16[4,2,32,1024]{3,2,0,1:T(8,128)(2,1)} %bitcast.668), channel_id=1, source_target_pairs={{0,4},{1,5},{2,6},{3,7},{4,0},{5,1},{6,2},{7,3},{8,12},{9,13},{10,... | collective-permute-start | bytes 1572872 | tf_op jit(solution)/shard_map/ppermute | solution.py:1089
  497.5 23.5 %collective-permute-start.45 = (bf16[4,2,32,1024]{3,2,0,1:T(8,128)(2,1)}, bf16[4,2,32,1024]{3,2,0,1:T(8,128)(2,1)}, u32[]{:S(2)}, u32[]{:S(2)}) collective-permute-start(bf16[4,2,32,1024]{3,2,0,1:T(8,128)(2,1)} %bitcast.667), channel_id=1, source_target_pairs={{0,4},{1,5},{2,6},{3,7},{4,0},{5,1},{6,2},{7,3},{8,12},{9,13},{10,... | collective-permute-start | bytes 1572872 | tf_op jit(solution)/shard_map/ppermute | solution.py:1089
  516.7 100.9 %collective-permute-start.68 = (bf16[2048,512]{1,0:T(8,128)(2,1)}, bf16[2048,512]{1,0:T(8,128)(2,1)}, u32[]{:S(2)}, u32[]{:S(2)}) collective-permute-start(bf16[2048,512]{1,0:T(8,128)(2,1)} %convolution_convert_fusion.2), channel_id=1, source_target_pairs={{0,1},{1,0},{2,3},{3,2},{4,5},{5,4},{6,7},{7,6},{8,9},{9,8},{10,11... | collective-permute-start | bytes 6291464 | tf_op jit(solution)/shard_map/ppermute | solution.py:1089
  521.0 89.5 %collective-permute-start.62 = (bf16[2048,512]{1,0:T(8,128)(2,1)}, bf16[2048,512]{1,0:T(8,128)(2,1)}, u32[]{:S(2)}, u32[]{:S(2)}) collective-permute-start(bf16[2048,512]{1,0:T(8,128)(2,1)} %convolution_convert_fusion.3), channel_id=1, source_target_pairs={{0,1},{1,0},{2,3},{3,2},{4,5},{5,4},{6,7},{7,6},{8,9},{9,8},{10,11... | collective-permute-start | bytes 6291464 | tf_op jit(solution)/shard_map/ppermute | solution.py:1089
  523.0 41.6 %collective-permute-start.40 = (bf16[4,32,1024]{2,1,0:T(8,128)(2,1)}, bf16[4,32,1024]{2,1,0:T(8,128)(2,1)}, u32[]{:S(2)}, u32[]{:S(2)}) collective-permute-start(bf16[4,32,1024]{2,1,0:T(8,128)(2,1)} %fusion.128), channel_id=1, source_target_pairs={{0,2},{1,3},{2,0},{3,1},{4,6},{5,7},{6,4},{7,5},{8,10},{9,11},{10,... | collective-permute-start | bytes 786440 | tf_op jit(solution)/shard_map/ppermute | solution.py:1089
  564.7 8.5 collective-permute-start.46
  591.0 6.5 collective-permute-start.48
  597.5 6.4 collective-permute-start.43
  609.9 174.7 %collective-permute-start.56 = (bf16[512,4096]{1,0:T(8,128)(2,1)}, bf16[512,4096]{1,0:T(8,128)(2,1)}, u32[]{:S(2)}, u32[]{:S(2)}) collective-permute-start(bf16[512,4096]{1,0:T(8,128)(2,1)} %convolution_convert_fusion), channel_id=1, source_target_pairs={{0,1},{1,0},{2,3},{3,2},{4,5},{5,4},{6,7},{7,6},{8,9},{9,8},{10,11... | collective-permute-start | bytes 12582920 | tf_op jit(solution)/shard_map/ppermute | solution.py:1089
  610.5 20.1 %collective-permute-start.16 = (bf16[4,2,2,32,1024]{4,3,0,2,1:T(8,128)(2,1)S(1)}, bf16[4,2,2,32,1024]{4,3,0,2,1:T(8,128)(2,1)S(1)}, u32[]{:S(2)}, u32[]{:S(2)}) collective-permute-start(bf16[4,2,2,32,1024]{4,3,0,2,1:T(8,128)(2,1)S(1)} %copy-done.59), channel_id=1, source_target_pairs={{0,1},{1,0},{2,3},{3,2},{4,5},{5,4},{6,7},{7,6},{8,9},{9,8},{10,11... | collective-permute-start | bytes 3145736 | tf_op jit(solution)/shard_map/ppermute | solution.py:1089
  614.5 16.0 %collective-permute-start.63 = (bf16[2,2,128,512]{3,2,0,1:T(8,128)(2,1)S(1)}, bf16[2,2,128,512]{3,2,0,1:T(8,128)(2,1)S(1)}, u32[]{:S(2)}, u32[]{:S(2)}) collective-permute-start(bf16[2,2,128,512]{3,2,0,1:T(8,128)(2,1)S(1)} %bitcast.736), channel_id=1, source_target_pairs={{0,8},{1,9},{2,10},{3,11},{4,12},{5,13},{6,14},{7,15},{8,16},{9,17... | collective-permute-start | bytes 1572872 | tf_op jit(solution)/shard_map/ppermute | solution.py:1089
  617.5 57.4 %collective-permute-start.33 = (bf16[4,2,32,2048]{3,2,0,1:T(8,128)(2,1)S(1)}, bf16[4,2,32,2048]{3,2,0,1:T(8,128)(2,1)S(1)}, u32[]{:S(2)}, u32[]{:S(2)}) collective-permute-start(bf16[4,2,32,2048]{3,2,0,1:T(8,128)(2,1)S(1)} %bitcast.725), channel_id=1, source_target_pairs={{0,2},{1,3},{2,0},{3,1},{4,6},{5,7},{6,4},{7,5},{8,10},{9,11},{10,... | collective-permute-start | bytes 3145736 | tf_op jit(solution)/shard_map/ppermute | solution.py:1089
  630.5 16.4 %collective-permute-start.69 = (bf16[2,2,128,512]{3,2,1,0:T(8,128)(2,1)S(1)}, bf16[2,2,128,512]{3,2,1,0:T(8,128)(2,1)S(1)}, u32[]{:S(2)}, u32[]{:S(2)}) collective-permute-start(bf16[2,2,128,512]{3,2,1,0:T(8,128)(2,1)S(1)} %dynamic-slice_bitcast_fusion), channel_id=1, source_target_pairs={{0,8},{1,9},{2,10},{3,11},{4,12},{5,13},{6,14},{7,15},{8,16},{9,17... | collective-permute-start | bytes 1572872 | tf_op jit(solution)/shard_map/ppermute | solution.py:1089
  630.6 45.5 %collective-permute-start.64 = (bf16[2,2,128,512]{3,2,0,1:T(8,128)(2,1)S(1)}, bf16[2,2,128,512]{3,2,0,1:T(8,128)(2,1)S(1)}, u32[]{:S(2)}, u32[]{:S(2)}) collective-permute-start(bf16[2,2,128,512]{3,2,0,1:T(8,128)(2,1)S(1)} %fusion.70), channel_id=1, source_target_pairs={{0,8},{1,9},{2,10},{3,11},{4,12},{5,13},{6,14},{7,15},{8,16},{9,17... | collective-permute-start | bytes 1572872 | tf_op jit(solution)/shard_map/ppermute | solution.py:1089
  646.8 6.4 collective-permute-start.19
  653.2 7.8 collective-permute-start.17
  671.0 8.7 collective-permute-start.23
  679.7 11.2 %collective-permute-start.70 = (bf16[2,2,128,512]{3,2,1,0:T(8,128)(2,1)S(1)}, bf16[2,2,128,512]{3,2,1,0:T(8,128)(2,1)S(1)}, u32[]{:S(2)}, u32[]{:S(2)}) collective-permute-start(bf16[2,2,128,512]{3,2,1,0:T(8,128)(2,1)S(1)} %fusion.68), channel_id=1, source_target_pairs={{0,8},{1,9},{2,10},{3,11},{4,12},{5,13},{6,14},{7,15},{8,16},{9,17... | collective-permute-start | bytes 1572872 | tf_op jit(solution)/shard_map/ppermute | solution.py:1089
  680.9 59.0 %collective-permute-start.34 = (bf16[4,32,2048]{2,1,0:T(8,128)(2,1)}, bf16[4,32,2048]{2,1,0:T(8,128)(2,1)}, u32[]{:S(2)}, u32[]{:S(2)}) collective-permute-start(bf16[4,32,2048]{2,1,0:T(8,128)(2,1)} %fusion.81), channel_id=1, source_target_pairs={{0,4},{1,5},{2,6},{3,7},{4,0},{5,1},{6,2},{7,3},{8,12},{9,13},{10,... | collective-permute-start | bytes 1572872 | tf_op jit(solution)/shard_map/ppermute | solution.py:1089
  682.7 11.2 %collective-permute-start.24 = (bf16[32,1024]{1,0:T(8,128)(2,1)S(1)}, bf16[32,1024]{1,0:T(8,128)(2,1)S(1)}, u32[]{:S(2)}, u32[]{:S(2)}) collective-permute-start(bf16[32,1024]{1,0:T(8,128)(2,1)S(1)} %get-tuple-element.116), channel_id=1, source_target_pairs={{0,8},{1,9},{2,10},{3,11},{4,12},{5,13},{6,14},{7,15},{8,16},{9,17... | collective-permute-start | bytes 196616 | tf_op jit(solution)/shard_map/ppermute | solution.py:1089
  700.6 9.7 %collective-permute-start.27 = (bf16[4,32,512]{2,1,0:T(8,128)(2,1)}, bf16[4,32,512]{2,1,0:T(8,128)(2,1)S(1)}, u32[]{:S(2)}, u32[]{:S(2)}) collective-permute-start(bf16[4,32,512]{2,1,0:T(8,128)(2,1)} %get-tuple-element.188), channel_id=1, source_target_pairs={{0,4},{1,5},{2,6},{3,7},{4,0},{5,1},{6,2},{7,3},{8,12},{9,13},{10,... | collective-permute-start | bytes 393224 | tf_op jit(solution)/shard_map/ppermute | solution.py:1089
  704.7 91.6 %all-to-all-start.2 = ((bf16[32,32,403]{2,1,0:T(8,128)(2,1)}), bf16[32,32,403]{2,1,0:T(8,128)(2,1)S(1)}, u32[]{:S(2)}, u32[]{:S(2)}) async-start(bf16[32,32,403]{2,1,0:T(8,128)(2,1)} %pad_maximum_fusion), calls=%async_computation.2 | async-start | bytes 2097152 | tf_op jit(solution)/shard_map/all_to_all | solution.py:1191
  708.7 12.1 %collective-permute-start.29 = (bf16[4,32,512]{2,1,0:T(8,128)(2,1)}, bf16[4,32,512]{2,1,0:T(8,128)(2,1)S(1)}, u32[]{:S(2)}, u32[]{:S(2)}) collective-permute-start(bf16[4,32,512]{2,1,0:T(8,128)(2,1)} %get-tuple-element.187), channel_id=1, source_target_pairs={{0,2},{1,3},{2,0},{3,1},{4,6},{5,7},{6,4},{7,5},{8,10},{9,11},{10,... | collective-permute-start | bytes 393224 | tf_op jit(solution)/shard_map/ppermute | solution.py:1089
  711.3 18.2 %collective-permute-start.28 = (bf16[2,4,32,512]{3,2,1,0:T(8,128)(2,1)S(1)}, bf16[2,4,32,512]{3,2,1,0:T(8,128)(2,1)S(1)}, u32[]{:S(2)}, u32[]{:S(2)}) collective-permute-start(bf16[2,4,32,512]{3,2,1,0:T(8,128)(2,1)S(1)} %pad_maximum_fusion.10), channel_id=1, source_target_pairs={{0,2},{1,3},{2,0},{3,1},{4,6},{5,7},{6,4},{7,5},{8,10},{9,11},{10,... | collective-permute-start | bytes 786440 | tf_op jit(solution)/shard_map/ppermute | solution.py:1089
  720.9 22.3 %collective-permute-start.71 = (bf16[2,2,128,512]{3,2,1,0:T(8,128)(2,1)}, bf16[2,2,128,512]{3,2,1,0:T(8,128)(2,1)S(1)}, u32[]{:S(2)}, u32[]{:S(2)}) collective-permute-start(bf16[2,2,128,512]{3,2,1,0:T(8,128)(2,1)} %fusion.69), channel_id=1, source_target_pairs={{0,8},{1,9},{2,10},{3,11},{4,12},{5,13},{6,14},{7,15},{8,16},{9,17... | collective-permute-start | bytes 1572872 | tf_op jit(solution)/shard_map/ppermute | solution.py:1089
  729.5 7.8 collective-permute-start.30
  737.4 21.3 %collective-permute-start.65 = (bf16[2,2,128,512]{3,2,0,1:T(8,128)(2,1)S(1)}, bf16[2,2,128,512]{3,2,0,1:T(8,128)(2,1)S(1)}, u32[]{:S(2)}, u32[]{:S(2)}) collective-permute-start(bf16[2,2,128,512]{3,2,0,1:T(8,128)(2,1)S(1)} %copy-done.66), channel_id=1, source_target_pairs={{0,8},{1,9},{2,10},{3,11},{4,12},{5,13},{6,14},{7,15},{8,16},{9,17... | collective-permute-start | bytes 1572872 | tf_op jit(solution)/shard_map/ppermute | solution.py:1089
  739.9 51.7 %collective-permute-start.31 = (bf16[4,2,2,32,1024]{4,3,2,1,0:T(8,128)(2,1)S(1)}, bf16[4,2,2,32,1024]{4,3,2,1,0:T(8,128)(2,1)S(1)}, u32[]{:S(2)}, u32[]{:S(2)}) collective-permute-start(bf16[4,2,2,32,1024]{4,3,2,1,0:T(8,128)(2,1)S(1)} %fusion.201), channel_id=1, source_target_pairs={{0,1},{1,0},{2,3},{3,2},{4,5},{5,4},{6,7},{7,6},{8,9},{9,8},{10,11... | collective-permute-start | bytes 3145736 | tf_op jit(solution)/shard_map/ppermute | solution.py:1089
  743.2 13.8 %collective-permute-start.35 = (bf16[32,2048]{1,0:T(8,128)(2,1)S(1)}, bf16[32,2048]{1,0:T(8,128)(2,1)S(1)}, u32[]{:S(2)}, u32[]{:S(2)}) collective-permute-start(bf16[32,2048]{1,0:T(8,128)(2,1)S(1)} %fusion.186), channel_id=1, source_target_pairs={{0,8},{1,9},{2,10},{3,11},{4,12},{5,13},{6,14},{7,15},{8,16},{9,17... | collective-permute-start | bytes 393224 | tf_op jit(solution)/shard_map/ppermute | solution.py:1089
  757.0 8.5 collective-permute-start.72
  763.9 7.1 collective-permute-start.66
  765.5 7.1 collective-permute-start.37
  784.0 64.6 %collective-permute-start.51 = (bf16[4,2,32,4096]{3,2,0,1:T(8,128)(2,1)}, bf16[4,2,32,4096]{3,2,0,1:T(8,128)(2,1)}, u32[]{:S(2)}, u32[]{:S(2)}) collective-permute-start(bf16[4,2,32,4096]{3,2,0,1:T(8,128)(2,1)} %bitcast.664), channel_id=1, source_target_pairs={{0,2},{1,3},{2,0},{3,1},{4,6},{5,7},{6,4},{7,5},{8,10},{9,11},{10,... | collective-permute-start | bytes 6291464 | tf_op jit(solution)/shard_map/ppermute | solution.py:1089
  791.5 59.7 %collective-permute-start.57 = (bf16[4,2,32,4096]{3,2,0,1:T(8,128)(2,1)}, bf16[4,2,32,4096]{3,2,0,1:T(8,128)(2,1)}, u32[]{:S(2)}, u32[]{:S(2)}) collective-permute-start(bf16[4,2,32,4096]{3,2,0,1:T(8,128)(2,1)} %bitcast.663), channel_id=1, source_target_pairs={{0,4},{1,5},{2,6},{3,7},{4,0},{5,1},{6,2},{7,3},{8,12},{9,13},{10,... | collective-permute-start | bytes 6291464 | tf_op jit(solution)/shard_map/ppermute | solution.py:1089
  796.3 45.5 %all-to-all-start.1 = ((bf16[32,32,256]{2,1,0:T(8,128)(2,1)}), bf16[32,32,256]{2,1,0:T(8,128)(2,1)}, u32[]{:S(2)}, u32[]{:S(2)}) async-start(bf16[32,32,256]{2,1,0:T(8,128)(2,1)} %bitcast.735), calls=%async_computation.1 | async-start | bytes 1048576 | tf_op jit(solution)/shard_map/all_to_all | solution.py:1191
  851.0 24.6 %collective-permute-start.52 = (bf16[4,32,4096]{2,1,0:T(8,128)(2,1)S(1)}, bf16[4,32,4096]{2,1,0:T(8,128)(2,1)S(1)}, u32[]{:S(2)}, u32[]{:S(2)}) collective-permute-start(bf16[4,32,4096]{2,1,0:T(8,128)(2,1)S(1)} %fusion.62), channel_id=1, source_target_pairs={{0,4},{1,5},{2,6},{3,7},{4,0},{5,1},{6,2},{7,3},{8,12},{9,13},{10,... | collective-permute-start | bytes 3145736 | tf_op jit(solution)/shard_map/ppermute | solution.py:1089
  854.8 24.6 %collective-permute-start.58 = (bf16[4,32,4096]{2,1,0:T(8,128)(2,1)S(1)}, bf16[4,32,4096]{2,1,0:T(8,128)(2,1)S(1)}, u32[]{:S(2)}, u32[]{:S(2)}) collective-permute-start(bf16[4,32,4096]{2,1,0:T(8,128)(2,1)S(1)} %fusion.63), channel_id=1, source_target_pairs={{0,2},{1,3},{2,0},{3,1},{4,6},{5,7},{6,4},{7,5},{8,10},{9,11},{10,... | collective-permute-start | bytes 3145736 | tf_op jit(solution)/shard_map/ppermute | solution.py:1089
  875.8 8.5 collective-permute-start.53
  879.7 10.3 %collective-permute-start.59 = (bf16[32,4096]{1,0:T(8,128)(2,1)S(1)}, bf16[32,4096]{1,0:T(8,128)(2,1)S(1)}, u32[]{:S(2)}, u32[]{:S(2)}) collective-permute-start(bf16[32,4096]{1,0:T(8,128)(2,1)S(1)} %fusion.131), channel_id=1, source_target_pairs={{0,8},{1,9},{2,10},{3,11},{4,12},{5,13},{6,14},{7,15},{8,16},{9,17... | collective-permute-start | bytes 786440 | tf_op jit(solution)/shard_map/ppermute | solution.py:1089
  884.4 11.2 %collective-permute-start.54 = (bf16[32,4096]{1,0:T(8,128)(2,1)S(1)}, bf16[32,4096]{1,0:T(8,128)(2,1)S(1)}, u32[]{:S(2)}, u32[]{:S(2)}) collective-permute-start(bf16[32,4096]{1,0:T(8,128)(2,1)S(1)} %fusion.92), channel_id=1, source_target_pairs={{0,8},{1,9},{2,10},{3,11},{4,12},{5,13},{6,14},{7,15},{8,16},{9,17... | collective-permute-start | bytes 786440 | tf_op jit(solution)/shard_map/ppermute | solution.py:1089
  890.1 11.2 %collective-permute-start.60 = (bf16[32,4096]{1,0:T(8,128)(2,1)S(1)}, bf16[32,4096]{1,0:T(8,128)(2,1)S(1)}, u32[]{:S(2)}, u32[]{:S(2)}) collective-permute-start(bf16[32,4096]{1,0:T(8,128)(2,1)S(1)} %fusion.90), channel_id=1, source_target_pairs={{0,8},{1,9},{2,10},{3,11},{4,12},{5,13},{6,14},{7,15},{8,16},{9,17... | collective-permute-start | bytes 786440 | tf_op jit(solution)/shard_map/ppermute | solution.py:1089
  895.7 11.2 %collective-permute-start.55 = (bf16[32,4096]{1,0:T(8,128)(2,1)S(1)}, bf16[32,4096]{1,0:T(8,128)(2,1)S(1)}, u32[]{:S(2)}, u32[]{:S(2)}) collective-permute-start(bf16[32,4096]{1,0:T(8,128)(2,1)S(1)} %fusion.93), channel_id=1, source_target_pairs={{0,8},{1,9},{2,10},{3,11},{4,12},{5,13},{6,14},{7,15},{8,16},{9,17... | collective-permute-start | bytes 786440 | tf_op jit(solution)/shard_map/ppermute | solution.py:1089
  901.3 9.5 %collective-permute-start.61 = (bf16[32,4096]{1,0:T(8,128)(2,1)S(1)}, bf16[32,4096]{1,0:T(8,128)(2,1)S(1)}, u32[]{:S(2)}, u32[]{:S(2)}) collective-permute-start(bf16[32,4096]{1,0:T(8,128)(2,1)S(1)} %fusion.91), channel_id=1, source_target_pairs={{0,8},{1,9},{2,10},{3,11},{4,12},{5,13},{6,14},{7,15},{8,16},{9,17... | collective-permute-start | bytes 786440 | tf_op jit(solution)/shard_map/ppermute | solution.py:1089
  (143 other events, 1443.5 us)

commit v3 on v2

--- a/solution.py
+++ b/solution.py
@@ -1058,164 +1058,465 @@
     )(rows2, patch_proj, cols, vectors, out_proj, heads, qkv, attn, gate, up, down)
 
 
-AX = ("dp", "fsdp")
+PARTS = ((0, 3072), (3072, 1024), (4096, 4096), (8192, 4096))
+STEP = 1024
+
+
+def add_to(dst, sources, width):
+    def one(i, carry):
+        at = pl.ds(pl.multiple_of(i * STEP, STEP), STEP)
+        total = sources[0](at).astype(jnp.float32)
+        for source in sources[1:]:
+            total = total + source(at).astype(jnp.float32)
+        dst(at, total)
+        return carry
+
+    lax.fori_loop(0, width // STEP, one, 0)
+
+
+def big_scatter(wires, spot, grads, bufs, outs, local):
+    f32, low = jnp.float32, jnp.bfloat16
+    held_w, held_d, stage_w, stage_d, near_w, near_d, last_w, last_d, ring_w, ring_d = bufs
+    half, deep = WIDE // 2, held_d.shape[2]
+    xn, yn, cn, zn = spot.flip(2)[0], spot.flip(1)[0], spot.sibling(), spot.above(1)
+    here, xp, yp, xy = spot.plane, spot.flip(2)[1], spot.flip(1)[1], spot.flip(3)[1]
+    T = [spot.column[k % spot.depth] for k in range(1, spot.depth + 1)]
+    core, fetch, near, last, ring = {}, {}, {}, {}, {}
+    A, B = pl.ds(0, half), pl.ds(half, half)
+    DA, DB = pl.ds(0, deep // 2), pl.ds(deep // 2, deep // 2)
+
+    def load(k):
+        fetch[k] = []
+        for i, ref in enumerate(grads):
+            dst = stage_w.at[:, :, pl.ds(*PARTS[i])] if i < 4 else stage_d
+            copy = pltpu.make_async_copy(ref.at[T[k], :, spot.c], dst, local.at[k * 5 + i])
+            copy.start()
+            fetch[k].append(copy)
+
+    def open_core(k):
+        core[k] = []
+        for i, ref in enumerate(grads):
+            dst = held_w.at[T[k], :, :, pl.ds(*PARTS[i])] if i < 4 else held_d.at[T[k]]
+            core[k].append(wires.copy(ref.at[T[k], :, 1 - spot.c], dst, cn))
+
+    def first(k):
+        t = T[k]
+        got(core[k])
+        for copy in fetch[k]:
+            copy.wait()
+        for plane in range(4):
+
+            def put_w(at, total, plane=plane):
+                held_w[t, plane, :, at] = total.astype(low)
+
+            add_to(put_w, [lambda at, p=plane: held_w[t, p, :, at], lambda at, p=plane: stage_w[p, :, at]], WIDE)
+            held_d[t, plane] = (held_d[t, plane].astype(f32) + stage_d[plane].astype(f32)).astype(low)
+        if k + 1 < spot.depth:
+            load(k + 1)
+        near[k] = []
+        for x in range(2):
+            src = x * 2 + (1 - spot.y)
+            near[k].append(wires.copy(held_w.at[t, src, :, A], near_w.at[k, x, :, A], yn))
+            near[k].append(wires.copy(held_d.at[t, src, DA], near_d.at[k, x, DA], yn))
+        for y in range(2):
+            src = (1 - spot.x) * 2 + y
+            near[k].append(wires.copy(held_w.at[t, src, :, B], near_w.at[k, y, :, B], xn))
+            near[k].append(wires.copy(held_d.at[t, src, DB], near_d.at[k, y, DB], xn))
+
+    def second(k):
+        t = T[k]
+        got(near[k])
+        for other in range(2):
+            pa, pb = other * 2 + spot.y, spot.x * 2 + other
+
+            def put_a(at, total, pa=pa):
+                held_w[t, pa, :, at] = total.astype(low)
+
+            def put_b(at, total, pb=pb):
+                held_w[t, pb, :, pl.ds(pl.multiple_of(at.start + half, STEP), STEP)] = total.astype(low)
+
+            shifted_by = lambda at: pl.ds(pl.multiple_of(at.start + half, STEP), STEP)
+            add_to(put_a, [lambda at, p=pa: held_w[t, p, :, at], lambda at, o=other: near_w[k, o, :, at]], half)
+            add_to(
+                put_b,
+                [
+                    lambda at, p=pb: held_w[t, p, :, shifted_by(at)],
+                    lambda at, o=other: near_w[k, o, :, shifted_by(at)],
+                ],
+                half,
+            )
+            held_d[t, pa, DA] = (held_d[t, pa, DA].astype(f32) + near_d[k, other, DA].astype(f32)).astype(low)
+            held_d[t, pb, DB] = (held_d[t, pb, DB].astype(f32) + near_d[k, other, DB].astype(f32)).astype(low)
+        last[k] = [
+            wires.copy(held_w.at[t, xp, :, A], last_w.at[k, :, A], xn),
+            wires.copy(held_d.at[t, xp, DA], last_d.at[k, DA], xn),
+            wires.copy(held_w.at[t, yp, :, B], last_w.at[k, :, B], yn),
+            wires.copy(held_d.at[t, yp, DB], last_d.at[k, DB], yn),
+        ]
+
+    def third(k):
+        t = T[k]
+        got(last[k])
+        if k:
+            got(ring[k - 1])
+        terms = [lambda at: held_w[t, here, :, at], lambda at: last_w[k, :, at]]
+        if k:
+            terms.append(lambda at: ring_w[k - 1, :, at])
+        down = held_d[t, here].astype(f32) + last_d[k].astype(f32)
+        if k:
+            down = down + ring_d[k - 1].astype(f32)
+        if k < spot.depth - 1:
+
+            def put_on(at, total):
+                held_w[t, here, :, at] = total.astype(low)
+
+            add_to(put_on, terms, WIDE)
+            held_d[t, here] = down.astype(low)
+            ring[k] = [
+                wires.copy(held_w.at[t, here], ring_w.at[k], zn),
+                wires.copy(held_d.at[t, here], ring_d.at[k], zn),
+            ]
+        else:
+            for out, (begin, width) in zip(outs, PARTS):
+
+                def put_out(at, total, out=out):
+                    out[:, at] = total
+
+                add_to(
+                    put_out,
+                    [
+                        lambda at, f=f, b=begin: f(pl.ds(pl.multiple_of(at.start + b, STEP), STEP))
+                        for f in terms
+                    ],
+                    width,
+                )
+            outs[4][...] = down
+
+    load(0)
+    for k in range(spot.depth):
+        open_core(k)
+    yield
+    steps = [(first, 0)]
+    n = spot.depth
+    for k in range(1, n + 2):
+        for step, lag in ((first, 0), (second, 1), (third, 2)):
+            if 0 <= k - lag < n:
+                steps.append((step, k - lag))
+    for step, k in steps:
+        step(k)
+        yield
+
+
+class Back:
+    def __init__(self, mix, own, core, ext, d_patch, gains, head_w, heads, taps):
+        f32, low = jnp.float32, jnp.bfloat16
+        count = mix.count
+        dt_row, rate_row, skip_row = heads[0:1], heads[1:2], heads[2:3]
+        r = ext[:, 0:1] + ext[:, 2:3]
+        along = ext[:, 1:2] + ext[:, 3:4]
+        raw = own[:, :256]
+        sig = sigmoid(raw)
+        gated = core * raw * sig
+        back = flat_dot(d_patch, head_w, ((1,), (1,)))
+        self.norm = (gated * r * gains).astype(low)
+        self.gain = jnp.sum(back * gated * r, axis=0, keepdims=True)
+        d_gated = r * gains * back - gated * (r * r * r * along * (1.0 / DI))
+        d_core = d_gated * raw * sig
+        d_gate = d_gated * core * sig * (1.0 + raw * (1.0 - sig))
+        lane = lanes((1, 128), 1)
+        graph = jnp.zeros((count, count), f32)
+        d_inputs = []
+        direct = jnp.zeros((count, 128), f32)
+        flow = jnp.zeros((count, 128), f32)
+        d_skip = jnp.zeros((1, 128), f32)
+        for i in range(4):
+            cut = slice(i * HEAD_M, (i + 1) * HEAD_M)
+            inputs, grad = mix.inputs[:, cut], d_core[:, cut]
+            decay, step = mix.decay(i), mix.row(mix.step_t, i)
+            kept = decay * mix.inner
+            skip = pick_lane(skip_row, mix.head(i))
+            d_mixing = flat_dot(grad.astype(low), inputs.astype(low), ((1,), (1,)))
+            d_inputs.append(
+                flat_dot((kept * step).astype(low), grad.astype(low), ((0,), (0,))) + skip * grad
+            )
+            graph = graph + decay * step * d_mixing
+            turn = kept * d_mixing
+            arrive = jnp.sum(turn.T, axis=1, keepdims=True)
+            leave = jnp.sum(turn * step, axis=1, keepdims=True)
+            here = lane == mix.head(i)
+            direct = direct + jnp.where(here, arrive, 0.0)
+            flow = flow + jnp.where(here, leave - mix.col(mix.step, i) * arrive, 0.0)
+            d_skip = d_skip + jnp.where(here, jnp.sum(grad * inputs, keepdims=True).reshape(1, 1), 0.0)
+        tail = exact_dot(mix.upper, flow)
+        mine = own_lanes(lane, mix)
+        d_step = jnp.where(mine, direct + rate_row * tail, 0.0)
+        d_raw = d_step * sigmoid(mix.raw)
+        self.skip = d_skip
+        self.rate = jnp.sum(rate_row * mix.step * jnp.where(mine, tail, 0.0), axis=0, keepdims=True)
+        self.bias = jnp.sum(d_raw, axis=0, keepdims=True)
+        low_graph = graph.astype(low)
+        d_out_map = flat_dot(low_graph, mix.in_map)
+        d_in_map = flat_dot(low_graph, mix.out_map, ((0,), (0,)))
+        d_act = jnp.concatenate(d_inputs + [d_in_map, d_out_map], axis=1)
+        d_conv = d_act * (mix.sig * (1.0 + mix.conv * (1.0 - mix.sig)))
+        d_channels = jnp.zeros_like(d_conv)
+        self.taps = [None] * CONV + [jnp.sum(d_conv, axis=0, keepdims=True)]
+        for s in range(CONV):
+            kept = d_conv * mix.slot.same[s]
+            d_channels = d_channels + taps[CONV - 1 - s] * shift(kept, -s)
+            self.taps[CONV - 1 - s] = jnp.sum(kept * shift(mix.channels, s), axis=0, keepdims=True)
+        self.rows = jnp.concatenate([d_gate, d_channels, d_raw], axis=1).astype(low)
+
+
+def own_lanes(lane, mix):
+    mine = lane == mix.head(0)
+    for i in range(1, 4):
+        mine = mine | (lane == mix.head(i))
+    return mine
+
+
+COLS = 512 + 256 + 128
+
+
+def backward_kernel(
+    depth,
+    mix_ref,
+    direct_ref,
+    sum_ref,
+    gains_ref,
+    small_ref,
+    bytes_ref,
+    norm_ref,
+    proj_ref,
+    head_w_ref,
+    own_ref,
+    maps_ref,
+    step_ref,
+    core_ref,
+    patch_ref,
+    heads_ref,
+    g_qkv,
+    g_attn,
+    g_gate,
+    g_up,
+    g_down,
+    o_qkv,
+    o_attn,
+    o_gate,
+    o_up,
+    o_down,
+    o_patch,
+    o_rows,
+    o_head,
+    o_cols,
+    o_maps,
+    all_ref,
+    mix_all,
+    rows_all,
+    head_sum,
+    head_low,
+    head_far,
+    col_send,
+    col_recv,
+    back_send,
+    parts8,
+    pair8,
+    near8,
+    held_w,
+    held_d,
+    stage_w,
+    stage_d,
+    near_w,
+    near_d,
+    last_w,
+    last_d,
+    ring_w,
+    ring_d,
+    send,
+    recv,
+    swap_send,
+    swap_recv,
+    local,
+):
+    f32, low = jnp.float32, jnp.bfloat16
+    spot = Spot(depth)
+    count = 128
+    wires = Wires(send, recv)
+    mix_all[spot.q] = mix_ref[...]
+    greet(spot)
+    plane = spread_plane(wires, spot, mix_all)
+    next(plane)
+    big = big_scatter(
+        wires,
+        spot,
+        (g_qkv, g_attn, g_gate, g_up, g_down),
+        (held_w, held_d, stage_w, stage_d, near_w, near_d, last_w, last_d, ring_w, ring_d),
+        (o_qkv, o_attn, o_gate, o_up, o_down),
+        local,
+    )
+    next(big)
+    next(plane)
+    taps = tap_rows(spot, small_ref)
+    heads = heads_ref[...]
+    dt_row, rate_row = heads[0:1], heads[1:2]
+    gains = jnp.concatenate(
+        [small_ref[spot.q + 8 * i, TILE : TILE + 16, 0:HEAD_M][6:7].astype(f32) for i in range(4)], axis=1
+    )
+    gain = gain_row(small_ref[:, TILE + 5, 0:128])
+    next(big)
+    run(plane)
+    sums = None
+    for x in range(2):
+        at = pl.ds(x * count, count)
+        slot = Slot(spot, small_ref, x, count)
+        mix = Mixed(spot, slot, own_ref[at], maps_ref[at], step_ref[at], taps, dt_row, rate_row)
+        d_patch = mix_all[pl.ds(x * 4, 4), :, pl.ds(0, D)].reshape(count, D)
+        ext = mix_all[pl.ds(x * 4, 4), :, pl.ds(D, 128)].reshape(count, 128).astype(f32)
+        back = Back(
+            mix, own_ref[at], core_ref[at], ext, d_patch, gains, head_w_ref[...].reshape(256, D), heads, taps
+        )
+        rows_all[at] = back.rows
+        head = flat_dot(back.norm, d_patch, ((0,), (0,)))
+        head_sum[...] = head if x == 0 else head_sum[...] + head
+        new = [*back.taps, back.gain, back.bias, back.rate, back.skip]
+        sums = new if sums is None else [a + b for a, b in zip(sums, new)]
+        grad = flat_dot(back.rows[:, :512], proj_ref[...], ((1,), (1,)))
+        grad = grad + flat_dot(
+            back.rows[:, 512:], small_ref[:, :TILE, :].reshape(D, SMALL_COLS), ((1,), (1,))
+        )
+        parts8[pl.ds(x * 2, 2)] = grad.astype(low).reshape(2, 2, TILE, D)
+        next(big)
+    total8 = sum_plane(wires, spot, parts8, pair8, near8)
+    next(total8)
+    head_low[...] = head_sum[...].astype(low).reshape(depth, HEAD_M, D)
+    head_ring = [
+        wires.copy(head_low.at[(spot.z + k) % depth], head_far.at[k - 1], spot.above(k)) for k in range(1, depth)
+    ]
+    next(total8)
+    norm = norm_ref[...].reshape(2 * count, D)
+    rows = rows_all[...]
+    for b in range(4):
+        block = flat_dot(norm[:, b * 256 : (b + 1) * 256], rows, ((0,), (0,)))
+        col_send[pl.ds(b * 8, 8)] = block.astype(low).reshape(8, TILE, COLS)
+    swap_cols = Swap(
+        spot, swap_send.at[0], swap_recv.at[0], lambda to: col_send.at[to], lambda me: col_recv.at[me]
+    )
+    grad_norm = next(total8)
+    patch_sum = sum_ref[...]
+    scale = lax.rsqrt(jnp.mean(patch_sum * patch_sum, axis=1, keepdims=True) + EPSILON)
+    along = jnp.mean(grad_norm * gain * patch_sum, axis=1, keepdims=True)
+    d_sum = direct_ref[...] + scale * gain * grad_norm - patch_sum * (scale * scale * scale * along)
+    gain_sum = jnp.sum(grad_norm * patch_sum * scale, axis=0, keepdims=True)
+    wide = lambda row: jnp.concatenate([row, jnp.zeros((1, D - row.shape[1]), f32)], axis=1)
+    lines = [wide(row) for row in sums[: CONV + 1]]
+    lines += [wide(jnp.concatenate(sums[CONV + 1 :], axis=1)), gains_ref[0:1], gains_ref[1:2], gain_sum]
+    lines += [jnp.zeros((16 - len(lines), D), f32)]
+    all_ref[spot.me] = jnp.concatenate([d_sum, *lines], axis=0).astype(low)
+    spread = spread_all(wires, spot, all_ref)
+    next(spread)
+    swap_cols.start()
+    col_recv[spot.me] = col_send[spot.me]
+    next(big)
+    next(spread)
+    next(big)
+    next(spread)
+    run(spread)
+    d_all = all_ref[:, :TILE].reshape(-1, D)
+    for b in range(4):
+        back_send[pl.ds(b * 8, 8)] = (
+            flat_dot(d_all[b * 256 : (b + 1) * 256], patch_ref[...], ((1,), (1,))).astype(low).reshape(8, TILE, 256)
+        )
+    swap_rows = Swap(
+        spot,
+        swap_send.at[1],
+        swap_recv.at[1],
+        lambda to: back_send.at[to],
+        lambda me: o_rows.at[:, pl.ds(pl.multiple_of(me * 256, 256), 256)],
+    )
+    swap_rows.start()
+    o_rows[:, pl.ds(pl.multiple_of(spot.me * 256, 256), 256)] = back_send[spot.me]
+    o_patch[...] = flat_dot(bytes_ref[...], d_all, ((0,), (0,)))
+    got(head_ring)
+    total = head_low[spot.z].astype(f32)
+    for k in range(depth - 1):
+        total = total + head_far[k].astype(f32)
+    o_head[...] = total
+    next(big)
+    swap_cols.arrive()
+    for q in range(8):
+        total = col_recv[q, :, :512].astype(f32)
+        for t in range(1, depth):
+            total = total + col_recv[t * 8 + q, :, :512].astype(f32)
+        o_cols[q] = total
+    total = jnp.zeros((TILE, COLS - 512), f32)
+    for e in range(spot.count):
+        total = total + col_recv[e, :, 512:].astype(f32)
+    o_maps[...] = total
+    run(big)
+    swap_rows.arrive()
+    wires.drain()
+    swap_cols.leave()
+    swap_rows.leave()
+
+
+def backward_call(depth, n_dev, mix, direct, patch_sum, gains, saved, patch_proj, heads, grads):
+    f32, low = jnp.float32, jnp.bfloat16
+    vmem = pl.BlockSpec(memory_space=pltpu.VMEM)
+    anywhere = pl.BlockSpec(memory_space=pl.ANY)
+    shape = jax.ShapeDtypeStruct
+    deep = grads[4].shape[0] // n_dev
+    cut = [g.reshape(depth, 4, 2, g.shape[0] // n_dev, g.shape[1]) for g in grads]
+    outs = [shape((TILE, width), f32) for _, width in PARTS] + [
+        shape((deep, D), f32),
+        shape((256, D), f32),
+        shape((TILE, PATCH * D), low),
+        shape((HEAD_M, D), f32),
+        shape((8, TILE, 512), f32),
+        shape((TILE, COLS - 512), f32),
+        shape((n_dev, SMALL_ROWS, D), low),
+    ]
+    scratch = [
+        pltpu.VMEM((8, TILE, EXT), low),
+        pltpu.VMEM((8 * TILE, COLS), low),
+        pltpu.VMEM((256, D), f32),
+        pltpu.VMEM((depth, HEAD_M, D), low),
+        pltpu.VMEM((depth - 1, HEAD_M, D), low),
+        pltpu.VMEM((n_dev, TILE, COLS), low),
+        pltpu.VMEM((n_dev, TILE, COLS), low),
+        pltpu.VMEM((n_dev, TILE, 256), low),
+        pltpu.VMEM((4, 2, TILE, D), low),
+        pltpu.VMEM((4, TILE, D), low),
+        pltpu.VMEM((3, TILE, D), low),
+        pltpu.VMEM((depth, 4, TILE, WIDE), low),
+        pltpu.VMEM((depth, 4, deep, D), low),
+        pltpu.VMEM((4, TILE, WIDE), low),
+        pltpu.VMEM((4, deep, D), low),
+        pltpu.VMEM((depth, 2, TILE, WIDE), low),
+        pltpu.VMEM((depth, 2, deep, D), low),
+        pltpu.VMEM((depth, TILE, WIDE), low),
+        pltpu.VMEM((depth, deep, D), low),
+        pltpu.VMEM((depth - 1, TILE, WIDE), low),
+        pltpu.VMEM((depth - 1, deep, D), low),
+        pltpu.SemaphoreType.DMA((N_WIRES,)),
+        pltpu.SemaphoreType.DMA((N_WIRES,)),
+        pltpu.SemaphoreType.DMA((2, n_dev)),
+        pltpu.SemaphoreType.DMA((2, n_dev)),
+        pltpu.SemaphoreType.DMA((5 * depth,)),
+    ]
+    return pl.pallas_call(
+        partial(backward_kernel, depth),
+        out_shape=outs,
+        in_specs=[vmem] * 15 + [anywhere] * 5,
+        out_specs=[vmem] * 11,
+        scratch_shapes=scratch,
+        compiler_params=pltpu.CompilerParams(
+            collective_id=1, has_side_effects=True, vmem_limit_bytes=62 * 2**20
+        ),
+        name="global_backward",
+    )(mix, direct, patch_sum, gains, *saved, patch_proj, heads, *cut)
+
+
 BC = 2 * STATE
-OWN = 2 * HEAD_M + 1
-
-
-class Grid:
-    def __init__(self, dp, fsdp):
-        self.depth, self.count = dp // 2, dp * fsdp
-        dp_at, fs_at = lax.axis_index("dp"), lax.axis_index("fsdp")
-        self.z, self.x, self.y, self.c = dp_at // 2, dp_at % 2, fs_at // 2, fs_at % 2
-        self.at = {"z": self.z, "x": self.x, "y": self.y, "c": self.c}
-
-    def route(self, dim, step=1):
-        pairs = []
-        for i in range(self.count):
-            z, x, y, c = i // 8, i // 4 % 2, i // 2 % 2, i % 2
-            if dim == "z":
-                z = (z + step) % self.depth
-            elif dim == "x":
-                x = 1 - x
-            elif dim == "y":
-                y = 1 - y
-            else:
-                c = 1 - c
-            pairs.append((i, z * 8 + x * 4 + y * 2 + c))
-        return pairs
-
-    def send(self, block, dim, step=1):
-        return lax.ppermute(block, AX, self.route(dim, step))
-
-
-def put(whole, part, place):
-    return lax.dynamic_update_slice(whole, part, [jnp.asarray(p, jnp.int32) for p in place])
-
-
-def gather_stream(grid, own, order):
-    rows, n = own.shape
-    pieces = [(own[None], {})]
-    zs = 1
-    for dim in order:
-        if dim == "z":
-            stacked = jnp.stack([p for p, _ in pieces], axis=0)
-            blocks = [stacked]
-            for _ in range(grid.depth - 1):
-                blocks.append(grid.send(blocks[-1], "z"))
-            whole = jnp.zeros((len(pieces), grid.depth, rows, n), own.dtype)
-            for k, block in enumerate(blocks):
-                whole = put(whole, block, (0, (grid.z - k) % grid.depth, 0, 0))
-            pieces = [(whole[i], at) for i, (_, at) in enumerate(pieces)]
-        else:
-            pieces = pieces + [(grid.send(p, dim), {**at, dim: True}) for p, at in pieces]
-    out = jnp.zeros((grid.depth, 2, 2, 2, rows, n), own.dtype)
-    for piece, at in pieces:
-        place = [1 - grid.at[d] if d in at else grid.at[d] for d in "xyc"]
-        out = put(out, piece[:, None, None, None], (0, *place, 0, 0))
-    return out.reshape(grid.count, rows, n)
-
-
-def pick(part, where, axis):
-    return lax.dynamic_index_in_dim(part, where, axis, keepdims=False)
-
-
-def scatter_stream(grid, part, order):
-    low = jnp.bfloat16
-    dims = ["z", "x", "y"]
-    for dim in order:
-        axis = dims.index(dim)
-        here = grid.at[dim]
-        if dim == "z":
-            total = None
-            for k in range(1, grid.depth + 1):
-                mine = pick(part, (here - k) % grid.depth, axis).astype(jnp.float32)
-                total = mine if total is None else mine + total.astype(jnp.float32)
-                if k < grid.depth:
-                    total = grid.send(total.astype(low), "z")
-            part = total
-        else:
-            arrived = grid.send(pick(part, 1 - here, axis).astype(low), dim)
-            part = pick(part, here, axis).astype(jnp.float32) + arrived.astype(jnp.float32)
-        dims.pop(axis)
-    return part
-
-
-def gather_small(grid, own):
-    rows, n = own.shape
-    column = jnp.zeros((grid.depth, rows, n), own.dtype)
-    for k in range(grid.depth):
-        block = own if k == 0 else grid.send(own, "z", k)
-        column = put(column, block[None], ((grid.z - k) % grid.depth, 0, 0))
-    half = n // 2
-    plane = jnp.zeros((grid.depth, 2, 2, rows, n), own.dtype)
-    for first, second, at in (("x", "y", 0), ("y", "x", half)):
-        mine = column[:, :, at : at + half]
-        both = jnp.stack([mine, grid.send(mine, first)])
-        far = grid.send(both, second)
-        for i in range(2):
-            for j, block in enumerate((both[i], far[i])):
-                place = {first: grid.at[first] ^ i, second: grid.at[second] ^ j}
-                plane = put(plane, block[:, None, None], (0, place["x"], place["y"], 0, at))
-    other = grid.send(plane, "c")
-    pair = jnp.where(grid.c == 0, jnp.stack([plane, other], 3), jnp.stack([other, plane], 3))
-    return pair.reshape(grid.count * rows, n)
-
-
-def scatter_small(grid, part):
-    low = jnp.bfloat16
-    n = part.shape[1]
-    part = part.reshape(grid.depth, 2, 2, 2, -1, n)
-    arrived = grid.send(pick(part, 1 - grid.c, 3).astype(low), "c")
-    part = pick(part, grid.c, 3) + arrived.astype(jnp.float32)
-    half = n // 2
-    sums = []
-    for order, at in (("yx", 0), ("xy", half)):
-        piece = part[..., at : at + half]
-        dims = ["z", "x", "y"]
-        for dim in order:
-            axis = dims.index(dim)
-            arrived = grid.send(pick(piece, 1 - grid.at[dim], axis).astype(low), dim)
-            piece = pick(piece, grid.at[dim], axis) + arrived.astype(jnp.float32)
-            dims.pop(axis)
-        sums.append(piece)
-    column = jnp.concatenate(sums, axis=-1)
-    total = pick(column, grid.z, 0)
-    for k in range(1, grid.depth):
-        block = pick(column, (grid.z + k) % grid.depth, 0).astype(low)
-        total = total + grid.send(block, "z", k).astype(jnp.float32)
-    return total
-
-
-def exchange(blocks):
-    return lax.all_to_all(blocks, AX, 0, 0, tiled=False)
-
-
-def causal_taps(channels, weight, bias, docs):
-    slots, count = docs.shape
-    padded = jnp.pad(channels, ((0, 0), (CONV - 1, 0), (0, 0)))
-    padded_docs = jnp.pad(docs, ((0, 0), (CONV - 1, 0)), constant_values=-1)
-    total = bias[None, None, :]
-    for k in range(CONV):
-        same = (padded_docs[:, k : k + count] == docs).astype(jnp.float32)
-        total = total + padded[:, k : k + count] * weight[:, k][None, None, :] * same[:, :, None]
-    return total
-
-
-def head_core(channels, maps, step_raw, conv_w, conv_b, maps_w, maps_b, dt_bias, a_log, skip, docs):
-    count = docs.shape[1]
-    inputs = jax.nn.silu(causal_taps(channels, conv_w, conv_b, docs))
-    both = jax.nn.silu(causal_taps(maps, maps_w, maps_b, docs))
-    in_map, out_map = both[..., :STATE], both[..., STATE:]
-    step_size = jax.nn.softplus(step_raw + dt_bias)
-    lower = jnp.tril(jnp.ones((count, count), jnp.float32))
-    cumulative = jnp.dot(step_size * -jnp.exp(a_log), lower.T, precision=HIGHEST)
-    keep = (lower > 0)[None] & (docs[:, :, None] == docs[:, None, :])
-    spread = cumulative[:, :, None] - cumulative[:, None, :]
-    decay = jnp.where(keep, jnp.exp(jnp.where(keep, spread, 0.0)), 0.0)
-    inner = jnp.einsum("gtn,gsn->gts", out_map, in_map, precision=HIGHEST)
-    mixing = decay * inner * step_size[:, None, :]
-    return jnp.einsum("gts,gsp->gtp", mixing, inputs, precision=HIGHEST) + skip * inputs
 
 
 def split_heads(rows_by_cols):
@@ -1260,13 +1561,10 @@
     down_proj,
 ):
     f32, low = jnp.float32, jnp.bfloat16
-    grid = Grid(*depth_fsdp)
-    n_dev = grid.count
+    depth, n_dev = depth_fsdp[0] // 2, depth_fsdp[0] * depth_fsdp[1]
     me = lax.axis_index("dp") * depth_fsdp[1] + lax.axis_index("fsdp")
     rows = byte_states.shape[0]
     patches = rows // PATCH
-    slots = depth_fsdp[0]
-    slot_patches = patches * depth_fsdp[1]
 
     shard_rows = in_proj.shape[0]
     maps_and_steps = jnp.pad(in_proj[:, 2 * DI :], ((0, 0), (0, SMALL_COLS - BC - MHEADS)))
@@ -1281,12 +1579,12 @@
     heads_in = jnp.pad(jnp.stack([dt_bias, -jnp.exp(a_log), skip_weight]), ((0, 5), (0, 128 - MHEADS)))
     rows2 = byte_states.reshape(patches, PATCH * D)
     (wide, deep, patch_sum, mixed, small, all_bytes, norm8, proj8, head_w, own8, maps8, step8, core8) = forward_call(
-        grid.depth, n_dev, rows2, patch_proj, cols, vectors, out_proj, heads_in, qkv_proj, attn_out, gate_proj, up_proj, down_proj
+        depth, n_dev, rows2, patch_proj, cols, vectors, out_proj, heads_in, qkv_proj, attn_out, gate_proj, up_proj, down_proj
     )
     lines = small[:, shard_rows : shard_rows + 10]
     gain_g, gain_a, gain_f = (lines[:, k, : D // n_dev].reshape(-1).astype(f32) for k in (5, 7, 8))
     gain_m = lines[:, 6, : DI // n_dev].reshape(-1).astype(f32)
-    my_places = share_at = lax.axis_index("fsdp") * patches + jnp.arange(patches, dtype=jnp.int32)
+    my_places = lax.axis_index("fsdp") * patches + jnp.arange(patches, dtype=jnp.int32)
     live = jnp.repeat((my_places < doc_lengths[0, 0] + doc_lengths[0, 1]).astype(f32), PATCH)[:, None]
     qk, vals, attn_o = wide[:, : 2 * D], wide[:, 2 * D : 3 * D], wide[:, 3 * D : 4 * D]
     gate_w, up_w = wide[:, 4 * D : 8 * D], wide[:, 8 * D :]
@@ -1294,44 +1592,6 @@
     raw_mixed = mixed[:, :D]
     mixer_r = lax.rsqrt(mixed[:, D : D + 1] / DI + EPSILON)
     mixed_patch = patch_sum + raw_mixed * mixer_r
-
-    conv_w = lines[:, :CONV, : CONV_CH // n_dev].transpose(0, 2, 1).reshape(CONV_CH, CONV).astype(f32)
-    conv_b = lines[:, CONV, : CONV_CH // n_dev].reshape(-1).astype(f32)
-    lengths = lines[:, 9, :2].reshape(slots, depth_fsdp[1], 2)[:, 0].astype(jnp.int32)
-    places = jnp.arange(slot_patches, dtype=jnp.int32)[None, :]
-    first_end = lengths[:, :1]
-    docs = (places >= first_end).astype(jnp.int32) + (places >= first_end + lengths[:, 1:]).astype(jnp.int32)
-    heads_of = lambda cols: cols.reshape(shard_rows, MHEADS, -1)
-    own_cols = jnp.concatenate(
-        [heads_of(in_proj[:, :DI]), heads_of(in_proj[:, DI : 2 * DI]), heads_of(in_proj[:, 2 * DI + BC :])],
-        axis=2,
-    ).transpose(1, 0, 2)
-    own_proj = exchange(own_cols).reshape(D, OWN)
-    maps_proj = small[:, :shard_rows, :BC].reshape(D, BC)
-    global_low = rms_scale(patch_sum, gain_g).astype(low)
-    global_all = gather_small(grid, global_low)
-    own = product(global_all, own_proj)
-    maps = product(global_all, maps_proj)
-    by_slot = lambda cols: cols.reshape(slots, slot_patches, -1)
-    gate_raw = own[:, :HEAD_M]
-    mine = lambda vec, width: lax.dynamic_slice_in_dim(vec, me * width, width, 0)
-    core_args = (
-        by_slot(own[:, HEAD_M : 2 * HEAD_M]),
-        by_slot(maps),
-        by_slot(own[:, 2 * HEAD_M :])[..., 0],
-        mine(conv_w, HEAD_M),
-        mine(conv_b, HEAD_M),
-        conv_w[DI:],
-        conv_b[DI:],
-        mine(dt_bias, 1),
-        mine(a_log, 1),
-        mine(skip_weight, 1),
-    )
-    core, core_back = jax.vjp(partial(head_core, docs=docs), *core_args)
-    core = core.reshape(-1, HEAD_M)
-    sig_m = jax.nn.sigmoid(gate_raw)
-    gated = core * gate_raw * sig_m
-    my_gain = mine(gain_m, HEAD_M)[None]
 
     streams = byte_states.astype(f32) + jnp.repeat(mixed_patch, PATCH, axis=0)
     normed = rms_scale(streams, gain_a).astype(low)
@@ -1352,34 +1612,23 @@
     ffn_out = jnp.concatenate([product(hidden, down_a), product(hidden, down_b)], axis=1)
     block_out = (live * (attended + ffn_out)).astype(low)
 
-    def plane_of(act, which):
-        cols = act.reshape(rows, n_dev // 2, 2, -1)
-        return pick(cols, which, 2).reshape(rows, -1)
-
-    def scattered(act, grad, order):
-        there = weight_grad(plane_of(act, 1 - grid.c), grad).astype(low)
-        arrived = grid.send(there, "c")
-        part = (weight_grad(plane_of(act, grid.c), grad) + arrived.astype(f32)).astype(low)
-        part = part.reshape(grid.depth, 2, 2, -1, grad.shape[1])
-        return scatter_stream(grid, part, order)
+    def scattered(act, grad):
+        return weight_grad(act, grad).astype(low)
 
     grad_block = live * out_grad.astype(f32)
     down_low = grad_block.astype(low)
-    grad_down = jnp.concatenate(
-        [scattered(hidden, down_low[:, : D // 2], "zyx"), scattered(hidden, down_low[:, D // 2 :], "zxy")],
-        axis=1,
-    )
+    grad_down = scattered(hidden, down_low)
     grad_hidden = input_grad(down_low[:, : D // 2], down_a) + input_grad(down_low[:, D // 2 :], down_b)
     grad_gate_low = (grad_hidden * upward * sigma * (1.0 + gate * (1.0 - sigma))).astype(low)
     grad_up_low = (grad_hidden * gate * sigma).astype(low)
-    grad_gate = scattered(ffn_low, grad_gate_low, "yxz")
-    grad_up = scattered(ffn_low, grad_up_low, "xyz")
+    grad_gate = scattered(ffn_low, grad_gate_low)
+    grad_up = scattered(ffn_low, grad_up_low)
     grad_ffn_in = input_grad(grad_gate_low, gate_w) + input_grad(grad_up_low, up_w)
     _, norm_back = jax.vjp(rms_scale, attended, gain_f)
     grad_attended_norm, grad_gain_f = norm_back(grad_ffn_in)
     grad_attended = grad_block + grad_attended_norm
     attn_grad_low = grad_attended.astype(low)
-    grad_attn_out = scattered(mixed_heads, attn_grad_low, "xyz")
+    grad_attn_out = scattered(mixed_heads, attn_grad_low)
     grad_mixed = split_heads(input_grad(attn_grad_low, attn_o).astype(low))
     grad_values = dot_f32("hbij,hbid->hbjd", attn_low, grad_mixed)
     grad_weights = dot_f32("hbid,hbjd->hbij", grad_mixed, value_rows)
@@ -1391,9 +1640,7 @@
     grad_keys = dot_f32("hbij,hbid->hbjd", scores_low, queries) * scale
     grad_qk = jnp.concatenate([join_heads(grad_queries.astype(low)), join_heads(grad_keys.astype(low))], axis=1)
     grad_v = join_heads(grad_values.astype(low))
-    grad_qkv = jnp.concatenate(
-        [scattered(normed, grad_qk, "yxz"), scattered(normed, grad_v, "xyz")], axis=1
-    )
+    grad_qkv = scattered(normed, jnp.concatenate([grad_qk, grad_v], axis=1))
     grad_normed = input_grad(grad_qk, qk) + input_grad(grad_v, vals)
     _, norm_back = jax.vjp(rms_scale, streams, gain_a)
     grad_streams_norm, grad_gain_a = norm_back(grad_normed)
@@ -1406,85 +1653,57 @@
     pair_high = pair.astype(low)
     pair_rest = (pair - pair_high.astype(f32)).astype(low)
     extra = jnp.pad(jnp.concatenate([pair_high, pair_rest], axis=1), ((0, 0), (0, 124)))
-    mix_all = gather_small(grid, jnp.concatenate([mix_low, extra], axis=1))
-    extra = mix_all[:, D : D + 4].astype(f32)
-    r_all, along_all = extra[:, 0:1] + extra[:, 2:3], extra[:, 1:2] + extra[:, 3:4]
-    mix_all = mix_all[:, :D]
-    grad_out_proj = weight_grad((gated * r_all * my_gain).astype(low), mix_all)
-    back_m = input_grad(mix_all, out_proj)
-    grad_gain_m = jnp.sum(back_m * gated * r_all, axis=0)
-    grad_gated = r_all * my_gain * back_m - gated * (r_all * r_all * r_all * along_all / DI)
-    grad_core = grad_gated * gate_raw * sig_m
-    grad_gate_raw = grad_gated * core * sig_m * (1.0 + gate_raw * (1.0 - sig_m))
-    (d_chan, d_maps, d_step, d_cw, d_cb, d_mw, d_mb, d_dt, d_alog, d_skip) = core_back(by_slot(grad_core))
-    d_own = jnp.concatenate(
-        [grad_gate_raw, d_chan.reshape(-1, HEAD_M), d_step.reshape(-1, 1)], axis=1
-    ).astype(low)
-    d_maps = d_maps.reshape(-1, BC).astype(low)
-    grad_norm = scatter_small(grid, input_grad(d_own, own_proj) + input_grad(d_maps, maps_proj))
-    grad_own_cols = weight_grad(global_all, d_own)
-    grad_maps_cols = weight_grad(global_all, d_maps)
-    _, norm_back = jax.vjp(rms_scale, patch_sum, gain_g)
-    grad_sum_norm, grad_gain_g = norm_back(grad_norm)
-    sum_low = (grad_patch_mix + grad_sum_norm).astype(low)
-    sum_all = gather_small(grid, sum_low)
-    grad_patch_proj = weight_grad(all_bytes, sum_all)
-    back_bytes = input_grad(sum_all, patch_proj).astype(low).reshape(n_dev, patches, -1)
-    back_bytes = exchange(back_bytes).transpose(1, 0, 2).reshape(rows, D)
-    grad_states = grad_streams + back_bytes.astype(f32)
-
-    taps = jnp.zeros((CONV_CH, CONV + 1), f32)
-    taps = put(taps, jnp.concatenate([d_cw, d_cb[:, None]], axis=1), (me * HEAD_M, 0))
-    taps = put(taps, jnp.concatenate([d_mw, d_mb[:, None]], axis=1), (DI, 0))
-    sums = [taps.reshape(n_dev, -1)]
-    sums += [g.reshape(n_dev, -1) for g in (grad_gain_g, grad_gain_a, grad_gain_f)]
-    heads = jnp.zeros((3, MHEADS), f32)
-    heads = put(heads, jnp.stack([d_dt, d_alog, d_skip]), (0, me)).reshape(1, -1)
-    sums += [jnp.broadcast_to(heads, (n_dev, 3 * MHEADS))]
-    sums = jnp.concatenate(sums, axis=1)
-    width = sums.shape[1]
-    extra_cols = -(-width // shard_rows)
-    sums = jnp.pad(sums, ((0, 0), (0, extra_cols * shard_rows - width))).reshape(n_dev, shard_rows, extra_cols)
-    parcel = jnp.concatenate(
-        [
-            grad_own_cols.reshape(n_dev, shard_rows, OWN),
-            grad_maps_cols.reshape(n_dev, shard_rows, BC),
-            sums,
-        ],
-        axis=2,
-    ).astype(low)
-    parcel = exchange(parcel).astype(f32)
-    side = lambda a, b: parcel[:, :, a:b].transpose(1, 0, 2).reshape(shard_rows, -1)
-    summed = jnp.sum(parcel[:, :, OWN:], axis=0)
+    gains = jnp.pad(jnp.stack([grad_gain_a, grad_gain_f]), ((0, 6), (0, 0)))
+    saved = (small, all_bytes, norm8, proj8, head_w, own8, maps8, step8, core8)
+    (g_qkv, g_attn, g_gate, g_up, g_down, g_patch, back_rows, g_out, g_cols, g_maps, everyone) = backward_call(
+        depth,
+        n_dev,
+        jnp.concatenate([mix_low, extra], axis=1),
+        grad_patch_mix,
+        patch_sum,
+        gains,
+        saved,
+        patch_proj,
+        heads_in,
+        (grad_qkv, grad_attn_out, grad_gate, grad_up, grad_down),
+    )
+    grad_states = grad_streams + back_rows.reshape(rows, D).astype(f32)
+
+    lines = everyone[:, shard_rows : shard_rows + 9].astype(f32)
+    sums = jnp.sum(lines, axis=0)
+    own_part = lambda row: lax.dynamic_slice_in_dim(row, me * (D // n_dev), D // n_dev, 0)
+    by_plane = jnp.sum(lines.reshape(depth, 8, 9, D), axis=0)
+    by_head = lambda rows_of: rows_of.reshape(8, -1, 4, HEAD_M).transpose(1, 2, 0, 3).reshape(-1, DI)
+    taps = jnp.concatenate([by_head(by_plane[:, : CONV + 1, :256]), sums[: CONV + 1, 256:512]], axis=1)
+    share = CONV_CH // n_dev
+    taps = lax.dynamic_slice_in_dim(taps, me * share, share, 1)
+    gain_m_sum = by_head(by_plane[:, CONV + 1 : CONV + 2, :256])[0]
+    gain_m_sum = lax.dynamic_slice_in_dim(gain_m_sum, me * HEAD_M, HEAD_M, 0)
+    head_line = sums[CONV + 1]
+    back_cols = lambda cols: cols.reshape(8, shard_rows, 4, HEAD_M).transpose(1, 2, 0, 3).reshape(shard_rows, DI)
     grad_in_proj = jnp.concatenate(
-        [side(0, HEAD_M), side(HEAD_M, 2 * HEAD_M), summed[:, :BC], side(2 * HEAD_M, OWN)], axis=1
-    )
-    flat = summed[:, BC:].reshape(-1)
-    taps = flat[: CONV_CH * (CONV + 1) // n_dev].reshape(-1, CONV + 1)
-    at = CONV_CH * (CONV + 1) // n_dev
-    grad_gain_g, grad_gain_a, grad_gain_f = (flat[at + i * D // n_dev : at + (i + 1) * D // n_dev] for i in range(3))
-    at += 3 * D // n_dev
-    heads = flat[at : at + 3 * MHEADS].reshape(3, MHEADS)
+        [back_cols(g_cols[..., :256]), back_cols(g_cols[..., 256:]), g_maps[:, : BC + MHEADS]], axis=1
+    )
     return (
         block_out,
         grad_states,
-        grad_patch_proj,
-        grad_gain_g,
+        g_patch,
+        own_part(sums[CONV + 4]),
         grad_in_proj,
-        taps[:, :CONV],
-        taps[:, CONV],
-        heads[0],
-        heads[1],
-        heads[2],
-        grad_gain_m,
-        grad_out_proj,
-        grad_gain_a,
-        grad_qkv,
-        grad_attn_out,
-        grad_gain_f,
-        grad_gate,
-        grad_up,
-        grad_down,
+        taps[:CONV].T,
+        taps[CONV],
+        head_line[256 : 256 + MHEADS],
+        head_line[384 : 384 + MHEADS],
+        head_line[512 : 512 + MHEADS],
+        gain_m_sum,
+        g_out,
+        own_part(sums[CONV + 2]),
+        g_qkv,
+        g_attn,
+        own_part(sums[CONV + 3]),
+        g_gate,
+        g_up,
+        g_down,
     )
 
 

time: 927 us -> 641 us (0.69)
  the two profiles are of different devices: /device:TPU:8 before, /device:TPU:0 now
where the time goes in v3:
time: 641 us; the launch traced here: 630 us
  Pallas kernels  482 us (75%)
  matrix products  84.2 us (13%)
  local copies, waits for them, and re-layouts  42.5 us (7%)
  other arithmetic  18.5 us (3%)
    pallas_call x1, Pallas kernels, forward_call(): pl.pallas_call(partial(forward_kernel, depth), out_shape=outs, in_specs=[...  245 us
    pallas_call x1, Pallas kernels, backward_call(): pl.pallas_call(partial(backward_kernel, depth), out_shape=outs, in_specs=...  237 us
    dot_general x7, matrix products, product(): return jnp.dot(left, right, preferred_element_type=jnp.float32)  26.4 us
    dot_general x5, matrix products, weight_grad(): lax.dot_general(left, right, (((0,), (0,)), ((), ())), preferred_element_...  24.2 us
    dot_general x7, matrix products, input_grad(): lax.dot_general(grad_rows, weight, (((1,), (1,)), ((), ())), preferred_el...  23.9 us

profile of v3, /device:TPU:0, one launch (start us, length us, event | category | flops | bytes accessed | tf_op | source)
XLA Modules:
  0.0 630.2 jit_solution(2155773547661396678)
XLA Ops:
  0.7 0.7 negate_bitcast_fusion
  1.4 0.7 convert_bitcast_fusion
  5.5 1.3 fusion.123
  8.1 0.8 slice_bitcast_fusion.5
  9.0 1.3 select_maximum_fusion.1.heads_ref
  10.5 0.7 slice.131
  11.3 1.9 concatenate.32.vec_ref
  13.2 1.0 fusion.121
  15.3 0.7 pad_maximum_fusion.1.cols_ref
  16.2 1.0 reshape.268.rows_ref
  17.2 245.4 %global_forward.1 = (bf16[1024,12288]{1,0:T(8,128)(2,1)}, bf16[4096,1024]{1,0:T(8,128)(2,1)}, f32[32,1024]{1,0:T(8,128)}, f32[32,1152]{1,0:T(8,128)}, bf16[32,48...) custom-call(bf16[32,8192]{1,0:T(8,128)(2,1)} %reshape.268.rows_ref, ...), custom_call_target="tpu_custom_call" | custom-call | tf_op jit(solution)/shard_map/global_forward/pallas_call | solution.py:1048
  262.6 0.8 add_rsqrt_fusion
  263.5 1.0 convert_reduce_fusion
  264.7 1.1 multiply_add_fusion
  266.0 2.4 fusion.48
  268.5 0.9 reshape.276
  269.5 3.5 fusion.20
  273.0 0.9 fusion.119
  274.5 0.9 copy.103
  275.4 2.2 reshape.302
  277.6 1.6 copy.105
  279.2 3.3 fusion.124
  282.5 2.0 fusion.55
  285.1 2.6 multiply_reduce_fusion.5
  287.9 7.8 %fusion.3 = f32[256,4096]{1,0:T(8,128)} fusion(bf16[256,1024]{1,0:T(8,128)(2,1)S(1)} %multiply_convert_fusion.4, bf16[1024,12288]{1,0:T(8,128)(2,1)} %get-tuple-element.46), kind=kOutput, calls=%fused_computation.6 | convolution fusion | flops 2147483648 | bytes 13107200 | tf_op jit(solution)/shard_map/dot_general | solution.py:79
  295.7 1.3 fusion.12
  297.0 1.4 convolution_add_fusion
  298.3 7.6 %multiply_convert_fusion.1 = (bf16[256,4096]{1,0:T(8,128)(2,1)S(1)}, bf16[256,4096]{1,0:T(8,128)(2,1)S(1)}, bf16[256,4096]{1,0:T(8,128)(2,1)S(1)}) fusion(f32[256,4096]{1,0:T(8,128)S(1)} %convolution_add_fusion, f32[256,4096]{1,0:T(8,128)} %fusion.3, bf16[256,1024]{1,0:T(8,128)(2,1)S(1)} %multiply_convert_fusion.4, bf16[1024,12288]{1,0:T(8,128)(2,1)} %get-tuple-element.46), kind=kOutput, calls=%fused_computation.15 | convolution fusion | flops 2164260864 | bytes 23592960 | tf_op jit(solution)/shard_map/dot_general | solution.py:79
  306.0 1.2 fusion.10
  307.3 1.2 fusion.14
  308.5 5.7 fusion.1
  314.3 6.0 multiply_reduce_fusion.1
  320.3 1.2 fusion.58
  321.5 3.1 fusion.51
  324.7 1.2 copy.110
  325.9 0.9 reshape.278
  326.8 2.6 fusion.54
  330.0 0.9 copy.169
  332.6 0.8 fusion.57
  334.4 0.7 copy.116
  335.3 3.9 fusion.16
  339.2 2.6 multiply_reduce_fusion.2
  342.4 1.6 bitcast_reduce_fusion
  344.9 2.1 convolution_convert_fusion.4
  347.0 4.7 convolution_convert_fusion.3
  351.7 5.7 convolution_convert_fusion
  357.4 5.7 convolution_convert_fusion.2
  363.1 6.0 convolution_convert_fusion.1
  369.1 236.5 %global_backward.1 = (f32[32,3072]{1,0:T(8,128)}, f32[32,1024]{1,0:T(8,128)}, f32[32,4096]{1,0:T(8,128)}, f32[32,4096]{1,0:T(8,128)}, f32[128,1024]{1,0:T(8,128)...) custom-call(bf16[32,1152]{1,0:T(8,128)(2,1)} %fusion.100.mix_ref, ...), custom_call_target="tpu_custom_call" | custom-call | tf_op jit(solution)/shard_map/global_backward/pallas_call | solution.py:1506
  605.6 1.4 fusion.86
  607.0 1.5 slice_convert_fusion
  608.5 1.0 reduce_sum.125
  610.1 0.9 slice_reduce_fusion
  611.0 0.8 slice.170
  615.7 1.2 reshape.300
  617.0 1.1 add.149
  619.7 1.6 pad_maximum_fusion
  621.3 1.0 copy.179
  622.3 1.7 copy.180
  623.9 0.7 copy.181
  624.7 1.6 copy.182
  626.3 1.9 copy.183
  628.1 0.8 copy.184
  628.9 0.8 copy.185
  (148 shorter events, 17.8 us)
Async XLA Ops:
  0.7 15.5 %copy-start = (bf16[256,1024]{1,0:T(8,128)(2,1)S(1)}, bf16[256,1024]{1,0:T(8,128)(2,1)}, u32[]{:S(2)}) copy-start(bf16[256,1024]{1,0:T(8,128)(2,1)} %param.20) | copy-start | bytes 1572868
  0.7 15.4 %copy-start.4 = (bf16[256,1024]{1,0:T(8,128)(2,1)S(1)}, bf16[256,1024]{1,0:T(8,128)(2,1)}, u32[]{:S(2)}) copy-start(bf16[256,1024]{1,0:T(8,128)(2,1)} %param.22) | copy-start | bytes 1572868
  275.4 7.1 %copy-start.8 = (bf16[2,128,16,64]{1,3,0,2:T(8,128)(2,1)}, bf16[2,128,16,64]{1,3,0,2:T(8,128)(2,1)S(1)}, u32[]{:S(2)}) copy-start(bf16[2,128,16,64]{1,3,0,2:T(8,128)(2,1)S(1)} %copy.103) | copy-start | bytes 1572868
  279.2 3.3 copy-start.21
  285.0 2.6 copy-start.5
  287.7 8.0 %slice-start = ((s8[8388608]{0:T(1024)(128)(4,1)}), s8[4194304]{0:T(1024)(128)(4,1)S(1)}, s32[]{:S(2)}) async-start(s8[8388608]{0:T(1024)(128)(4,1)} %bitcast.174), calls=%async_computation | async-start | bytes 8388608
  287.9 7.8 %slice-start.1 = ((s8[8388608]{0:T(1024)(128)(4,1)}), s8[4194304]{0:T(1024)(128)(4,1)S(1)}, s32[]{:S(2)}) async-start(s8[8388608]{0:T(1024)(128)(4,1)} %bitcast.174), calls=%async_computation.1 | async-start | bytes 8388608
  306.0 1.3 copy-start.2
  306.0 2.6 copy-start.11
  306.0 8.3 %copy-start.13 = (bf16[256,4096]{1,0:T(8,128)(2,1)}, bf16[256,4096]{1,0:T(8,128)(2,1)S(1)}, u32[]{:S(2)}) copy-start(bf16[256,4096]{1,0:T(8,128)(2,1)S(1)} %get-tuple-element.77) | copy-start | bytes 6291460
  326.8 4.1 copy-start.7
  326.8 4.1 copy-start.22
  326.8 4.1 copy-start.24
  331.5 1.0 copy-start.9
  331.5 1.9 copy-start.10
  335.2 3.9 copy-start.25
  335.3 3.9 copy-start.27
  341.7 2.2 copy-start.17
  341.7 3.1 copy-start.6
  343.9 7.8 %copy-start.15 = (f32[32,1024]{1,0:T(8,128)}, f32[32,1024]{1,0:T(8,128)S(1)}, u32[]{:S(2)}) copy-start(f32[32,1024]{1,0:T(8,128)S(1)} %get-tuple-element.75.direct_ref) | copy-start | bytes 393220
  344.2 2.8 copy-start.23
  344.2 2.8 copy-start.26
  344.2 2.8 copy-start.28
  347.0 4.7 copy-start.3
  351.7 5.7 copy-start.14
  357.4 5.7 copy-start.12
  608.5 8.5 %copy-start.1 = (f32[256,1024]{1,0:T(8,128)S(1)}, f32[256,1024]{1,0:T(8,128)}, u32[]{:S(2)}) copy-start(f32[256,1024]{1,0:T(8,128)} %get-tuple-element.76) | copy-start | bytes 3145732
  609.6 8.5 %copy-start.20 = (f32[8,32,512]{2,1,0:T(8,128)S(1)}, f32[8,32,512]{2,1,0:T(8,128)}, u32[]{:S(2)}) copy-start(f32[8,32,512]{2,1,0:T(8,128)} %get-tuple-element.59) | copy-start | bytes 1572868
  618.1 3.2 copy-start.16
  618.9 5.1 copy-start.29
  619.5 8.7 %copy-start.19 = (f32[32,4096]{1,0:T(8,128)S(1)}, f32[32,4096]{1,0:T(8,128)}, u32[]{:S(2)}) copy-start(f32[32,4096]{1,0:T(8,128)} %get-tuple-element.148) | copy-start | bytes 1572868
  621.3 7.6 %copy-start.18 = (f32[128,1024]{1,0:T(8,128)S(1)}, f32[128,1024]{1,0:T(8,128)}, u32[]{:S(2)}) copy-start(f32[128,1024]{1,0:T(8,128)} %get-tuple-element.149) | copy-start | bytes 1572868

commit v4 on v3

--- a/solution.py
+++ b/solution.py
@@ -747,6 +747,16 @@
     yield
 
 
+def ticker(steps, plan):
+    counts = iter(plan)
+
+    def tick():
+        for _ in range(next(counts)):
+            next(steps, None)
+
+    return tick
+
+
 def run(steps):
     for _ in steps:
         pass
@@ -853,6 +863,8 @@
 
 
 N_WIRES = 256
+PLAN_F = (1, 1, 1, 0, 1, 1, 1, 1, 1, 1, 0, 1, 0, 1, 0)
+PLAN_B = (1, 1, 1, 1, 1, 1, 1, 0, 1, 1, 0, 1, 1, 1, 0, 0, 0, 0, 1)
 
 
 def forward_kernel(
@@ -929,7 +941,8 @@
     small = spread_all(wires, spot, small_ref)
     next(small)
     head_w = [wires.copy(out_ref, head_w_ref.at[spot.z], spot.above(k)) for k in range(1, depth)]
-    next(big)
+    tick = ticker(big, PLAN_F)
+    tick()
     own_rows = []
     at = 0
     for i, ref in enumerate((qkv, attn, gate, up)):
@@ -942,19 +955,24 @@
     )
     for copy in own_rows:
         copy.start()
+    tick()
     swap_bytes.arrive()
 
     for b in range(4):
         block = flat_dot(bytes_ref[pl.ds(b * 256, 256)], patch_ref[...]).astype(low)
         parts[pl.ds(b * 4, 4)] = block.reshape(4, 2, TILE, D)
+    tick()
     total = sum_all(wires, spot, parts, pair, near, column, far, sum_ref)
     next(total)
     next(small)
+    tick()
     next(total)
-    next(big)
+    tick()
     next(total)
     next(small)
+    tick()
     next(total)
+    tick()
     run(small)
     patch_sum = sum_ref[...]
     scale = lax.rsqrt(jnp.mean(patch_sum * patch_sum, axis=1, keepdims=True) + EPSILON)
@@ -962,17 +980,20 @@
     norm_ref[spot.q] = (patch_sum * scale * gain).astype(low)
     plane = spread_plane(wires, spot, norm_ref)
     next(plane)
+    tick()
     next(plane)
+    tick()
     swap_proj.arrive()
     taps = tap_rows(spot, small_ref)
     run(plane)
-    next(big)
+    tick()
 
     norm = norm_ref[...].reshape(2 * count, D)
     own_ref[...] = flat_dot(norm, proj_ref[...])
     maps_ref[...] = flat_dot(norm, small_ref[:, :TILE, 0:256].reshape(D, 256))
     step_ref[...] = flat_dot(norm, small_ref[:, :TILE, 256:384].reshape(D, 128))
     dt_row, rate_row, skip_row = heads_ref[0:1], heads_ref[1:2], heads_ref[2:3]
+    tick()
     got(head_w)
     gains = jnp.concatenate(
         [small_ref[spot.q + 8 * i, TILE : TILE + 16, 0:HEAD_M][6:7].astype(f32) for i in range(4)], axis=1
@@ -998,8 +1019,10 @@
         parts8[pl.ds(x * 2, 2), :, :, pl.ds(D, 128)] = (
             jnp.broadcast_to(squares, (count, 128)).astype(low).reshape(2, 2, TILE, 128)
         )
+        tick()
     for total in sum_plane(wires, spot, parts8, pair8, near8):
-        pass
+        if total is None:
+            tick()
     mixed_ref[...] = total
     for copy in own_rows:
         copy.wait()
@@ -1354,8 +1377,10 @@
         (o_qkv, o_attn, o_gate, o_up, o_down),
         local,
     )
-    next(big)
+    tick = ticker(big, PLAN_B)
+    tick()
     next(plane)
+    tick()
     taps = tap_rows(spot, small_ref)
     heads = heads_ref[...]
     dt_row, rate_row = heads[0:1], heads[1:2]
@@ -1363,8 +1388,8 @@
         [small_ref[spot.q + 8 * i, TILE : TILE + 16, 0:HEAD_M][6:7].astype(f32) for i in range(4)], axis=1
     )
     gain = gain_row(small_ref[:, TILE + 5, 0:128])
-    next(big)
     run(plane)
+    tick()
     sums = None
     for x in range(2):
         at = pl.ds(x * count, count)
@@ -1376,6 +1401,7 @@
             mix, own_ref[at], core_ref[at], ext, d_patch, gains, head_w_ref[...].reshape(256, D), heads, taps
         )
         rows_all[at] = back.rows
+        tick()
         head = flat_dot(back.norm, d_patch, ((0,), (0,)))
         head_sum[...] = head if x == 0 else head_sum[...] + head
         new = [*back.taps, back.gain, back.bias, back.rate, back.skip]
@@ -1385,14 +1411,16 @@
             back.rows[:, 512:], small_ref[:, :TILE, :].reshape(D, SMALL_COLS), ((1,), (1,))
         )
         parts8[pl.ds(x * 2, 2)] = grad.astype(low).reshape(2, 2, TILE, D)
-        next(big)
+        tick()
     total8 = sum_plane(wires, spot, parts8, pair8, near8)
     next(total8)
+    tick()
     head_low[...] = head_sum[...].astype(low).reshape(depth, HEAD_M, D)
     head_ring = [
         wires.copy(head_low.at[(spot.z + k) % depth], head_far.at[k - 1], spot.above(k)) for k in range(1, depth)
     ]
     next(total8)
+    tick()
     norm = norm_ref[...].reshape(2 * count, D)
     rows = rows_all[...]
     for b in range(4):
@@ -1401,7 +1429,9 @@
     swap_cols = Swap(
         spot, swap_send.at[0], swap_recv.at[0], lambda to: col_send.at[to], lambda me: col_recv.at[me]
     )
+    tick()
     grad_norm = next(total8)
+    tick()
     patch_sum = sum_ref[...]
     scale = lax.rsqrt(jnp.mean(patch_sum * patch_sum, axis=1, keepdims=True) + EPSILON)
     along = jnp.mean(grad_norm * gain * patch_sum, axis=1, keepdims=True)
@@ -1416,11 +1446,13 @@
     next(spread)
     swap_cols.start()
     col_recv[spot.me] = col_send[spot.me]
-    next(big)
+    tick()
     next(spread)
-    next(big)
+    tick()
     next(spread)
+    tick()
     run(spread)
+    tick()
     d_all = all_ref[:, :TILE].reshape(-1, D)
     for b in range(4):
         back_send[pl.ds(b * 8, 8)] = (
@@ -1434,14 +1466,16 @@
         lambda me: o_rows.at[:, pl.ds(pl.multiple_of(me * 256, 256), 256)],
     )
     swap_rows.start()
+    tick()
     o_rows[:, pl.ds(pl.multiple_of(spot.me * 256, 256), 256)] = back_send[spot.me]
     o_patch[...] = flat_dot(bytes_ref[...], d_all, ((0,), (0,)))
+    tick()
     got(head_ring)
     total = head_low[spot.z].astype(f32)
     for k in range(depth - 1):
         total = total + head_far[k].astype(f32)
     o_head[...] = total
-    next(big)
+    tick()
     swap_cols.arrive()
     for q in range(8):
         total = col_recv[q, :, :512].astype(f32)
@@ -1452,6 +1486,7 @@
     for e in range(spot.count):
         total = total + col_recv[e, :, 512:].astype(f32)
     o_maps[...] = total
+    tick()
     run(big)
     swap_rows.arrive()
     wires.drain()
@@ -1516,25 +1551,275 @@
     )(mix, direct, patch_sum, gains, *saved, patch_proj, heads, *cut)
 
 
+def patch_pairs(count):
+    i, j = lanes((count, count), 0), lanes((count, count), 1)
+    return (i >= j) & ((i >> 3) == (j >> 3))
+
+
+def rms_back(value, gain, grad):
+    scale = lax.rsqrt(jnp.mean(value * value, axis=1, keepdims=True) + EPSILON)
+    along = jnp.mean(grad * gain * value, axis=1, keepdims=True)
+    d_value = scale * gain * grad - value * (scale * scale * scale * along)
+    return d_value, jnp.sum(grad * value * scale, axis=0, keepdims=True)
+
+
+def halves_of(block):
+    left = lanes(block.shape, 1) < HEAD
+    return left, [jnp.where(left, block, 0), jnp.where(left, 0, block)]
+
+
+def local_kernel(
+    lengths,
+    bytes_ref,
+    grad_ref,
+    sum_ref,
+    mixed_ref,
+    small_ref,
+    wide,
+    deep,
+    o_block,
+    o_streams,
+    o_mix,
+    o_direct,
+    o_gains,
+    g_qkv,
+    g_attn,
+    g_gate,
+    g_up,
+    g_down,
+    attn_w,
+    ffn_w,
+    g_buf,
+    streams,
+    normed,
+    qkv,
+    weights,
+    heads,
+    attended,
+    ffn_low,
+    ffn_t,
+    total,
+    d_ffn,
+    d_down,
+    load_sem,
+    ffn_sem,
+    g_sem,
+):
+    f32, low = jnp.float32, jnp.bfloat16
+    rows = bytes_ref.shape[0]
+    scale = HEAD ** (-0.5)
+    load = pltpu.make_async_copy(wide.at[:, pl.ds(0, 4 * D)], attn_w, load_sem.at[0])
+    load.start()
+
+    def ffn_loads(j, slot):
+        at = lambda base: pl.ds(pl.multiple_of(base + j * D, D), D)
+        return [
+            pltpu.make_async_copy(wide.at[:, at(4 * D)], ffn_w.at[slot, 0], ffn_sem.at[slot, 0]),
+            pltpu.make_async_copy(wide.at[:, at(8 * D)], ffn_w.at[slot, 1], ffn_sem.at[slot, 1]),
+            pltpu.make_async_copy(deep.at[at(0)], ffn_w.at[slot, 2], ffn_sem.at[slot, 2]),
+        ]
+
+    for copy in ffn_loads(0, 0):
+        copy.start()
+    gain_a = gain_row(small_ref[:, TILE + 7, 0:128])
+    gain_f = gain_row(small_ref[:, TILE + 8, 0:128])
+    place = lax.axis_index("fsdp") * (rows // PATCH) + (lanes((rows, 1), 0) >> 3)
+    live = (place < lengths[0, 0] + lengths[0, 1]).astype(f32)
+    raw = mixed_ref[:, pl.ds(0, D)]
+    mixer_r = lax.rsqrt(mixed_ref[:, pl.ds(D, 128)] * (1.0 / DI) + EPSILON)[:, 0:1]
+    patch = sum_ref[...] + raw * mixer_r
+    patch = jnp.broadcast_to(patch[:, None, :], (rows // PATCH, PATCH, D)).reshape(rows, D)
+    streams[...] = bytes_ref[...].astype(f32) + patch
+    normed[...] = rms_scale(streams[...], gain_a).astype(low)
+    d_down[...] = (live * grad_ref[...].astype(f32)).astype(low)
+    load.wait()
+    for i in range(3):
+        at = pl.ds(i * D, D)
+        qkv[:, at] = flat_dot(normed[...], attn_w[:, at]).astype(low)
+    pairs = patch_pairs(128)
+
+    def blocks(p, b):
+        row = pl.ds(b * 128, 128)
+        return row, [pl.ds(pl.multiple_of(base + p * 128, 128), 128) for base in (0, D, 2 * D)]
+
+    def attend(p, carry):
+        for b in range(rows // 128):
+            row, (qa, ka, va) = blocks(p, b)
+            k, v = qkv[row, ka], qkv[row, va]
+            left, queries = halves_of(qkv[row, qa])
+            outs = []
+            for h in range(2):
+                scores = flat_dot(queries[h], k, ((1,), (1,))) * scale
+                scores = jnp.where(pairs, scores, -1e30)
+                e = jnp.exp(scores - jnp.max(scores, axis=1, keepdims=True))
+                w = e / jnp.sum(e, axis=1, keepdims=True)
+                weights[p, b, h] = w
+                outs.append(flat_dot(w.astype(low), v))
+            heads[row, qa] = jnp.where(left, outs[0], outs[1]).astype(low)
+        return carry
+
+    lax.fori_loop(0, D // 128, attend, 0)
+    attended[...] = streams[...] + flat_dot(heads[...], attn_w[:, pl.ds(3 * D, D)])
+    ffn_low[...] = rms_scale(attended[...], gain_f).astype(low)
+    ffn_t[...] = ffn_low[...].astype(f32).T.astype(low)
+    total[...] = attended[...]
+    d_ffn[...] = jnp.zeros_like(d_ffn)
+    n_ffn = deep.shape[0] // D
+
+    def stores(j):
+        at = pl.ds(pl.multiple_of(j * D, D), D)
+        return [
+            pltpu.make_async_copy(g_buf.at[0], g_gate.at[:, at], g_sem.at[0]),
+            pltpu.make_async_copy(g_buf.at[1], g_up.at[:, at], g_sem.at[1]),
+            pltpu.make_async_copy(g_buf.at[2], g_down.at[at], g_sem.at[2]),
+        ]
+
+    def feed(j, carry):
+        slot = lax.rem(j, 2)
+        for copy in ffn_loads(j, slot):
+            copy.wait()
+
+        @pl.when(j + 1 < n_ffn)
+        def _():
+            for copy in ffn_loads(j + 1, 1 - slot):
+                copy.start()
+
+        gate = flat_dot(ffn_low[...], ffn_w[slot, 0])
+        upward = flat_dot(ffn_low[...], ffn_w[slot, 1])
+        sig = sigmoid(gate)
+        act = gate * sig
+        hidden = (act * upward).astype(low)
+        total[...] += flat_dot(hidden, ffn_w[slot, 2])
+        d_hidden = flat_dot(d_down[...], ffn_w[slot, 2], ((1,), (1,)))
+        d_gate = (d_hidden * upward * (sig + act * (1.0 - sig))).astype(low)
+        d_up = (d_hidden * act).astype(low)
+        d_ffn[...] += flat_dot(d_gate, ffn_w[slot, 0], ((1,), (1,)))
+        d_ffn[...] += flat_dot(d_up, ffn_w[slot, 1], ((1,), (1,)))
+
+        @pl.when(j > 0)
+        def _():
+            for copy in stores(j - 1):
+                copy.wait()
+
+        g_buf[0] = flat_dot(ffn_t[...], d_gate).astype(low)
+        g_buf[1] = flat_dot(ffn_t[...], d_up).astype(low)
+        g_buf[2] = flat_dot(hidden.astype(f32).T.astype(low), d_down[...]).astype(low)
+        for copy in stores(j):
+            copy.start()
+        return carry
+
+    lax.fori_loop(0, n_ffn, feed, 0)
+    o_block[...] = (live * total[...]).astype(low)
+    d_norm, gain_f_sum = rms_back(attended[...], gain_f, d_ffn[...])
+    d_attended = live * grad_ref[...].astype(f32) + d_norm
+    total[...] = d_attended
+    d_low = d_attended.astype(low)
+    for copy in stores(n_ffn - 1):
+        copy.wait()
+    d_down[...] = flat_dot(d_low, attn_w[:, pl.ds(3 * D, D)], ((1,), (1,))).astype(low)
+    g_buf[0] = flat_dot(heads[...].astype(f32).T.astype(low), d_low).astype(low)
+    last = [pltpu.make_async_copy(g_buf.at[0], g_attn, g_sem.at[0])]
+    last[0].start()
+
+    def attend_back(p, carry):
+        for b in range(rows // 128):
+            row, (qa, ka, va) = blocks(p, b)
+            q, k, v = qkv[row, qa], qkv[row, ka], qkv[row, va]
+            grad = d_down[row, qa]
+            left, grads = halves_of(grad)
+            dq, dk, dv = [], [], []
+            for h in range(2):
+                w = weights[p, b, h]
+                dv.append(flat_dot(w.T.astype(low), grad))
+                d_w = flat_dot(grads[h], v, ((1,), (1,)))
+                d_s = w * (d_w - jnp.sum(w * d_w, axis=1, keepdims=True))
+                dq.append(flat_dot(d_s.astype(low), k) * scale)
+                dk.append(flat_dot(d_s.T.astype(low), q) * scale)
+            qkv[row, qa] = jnp.where(left, dq[0], dq[1]).astype(low)
+            qkv[row, ka] = jnp.where(left, dk[0], dk[1]).astype(low)
+            qkv[row, va] = jnp.where(left, dv[0], dv[1]).astype(low)
+        return carry
+
+    lax.fori_loop(0, D // 128, attend_back, 0)
+    ffn_t[...] = normed[...].astype(f32).T.astype(low)
+    for i in range(3):
+        at = pl.ds(i * D, D)
+        if i == 2:
+            last[0].wait()
+        buf = (i + 1) % 3
+        g_buf[buf] = flat_dot(ffn_t[...], qkv[:, at]).astype(low)
+        copy = pltpu.make_async_copy(g_buf.at[buf], g_qkv.at[:, at], g_sem.at[buf])
+        copy.start()
+        last.append(copy)
+    d_ffn[...] = flat_dot(qkv[...], attn_w[:, pl.ds(0, 3 * D)], ((1,), (1,)))
+    d_norm, gain_a_sum = rms_back(streams[...], gain_a, d_ffn[...])
+    d_streams = total[...] + d_norm
+    o_streams[...] = d_streams
+    direct = jnp.sum(d_streams.reshape(rows // PATCH, PATCH, D), axis=1)
+    o_direct[...] = direct
+    mix = direct.astype(low)
+    along = jnp.sum(mix.astype(f32) * raw, axis=1, keepdims=True)
+    high_r, high_a = (v.astype(low).astype(f32) for v in (mixer_r, along))
+    lane = lanes((rows // PATCH, 128), 1)
+    ext = jnp.zeros((rows // PATCH, 128), f32)
+    for i, v in enumerate((high_r, high_a, mixer_r - high_r, along - high_a)):
+        ext = jnp.where(lane == i, v, ext)
+    o_mix[:, pl.ds(0, D)] = mix
+    o_mix[:, pl.ds(D, 128)] = ext.astype(low)
+    o_gains[...] = jnp.concatenate([gain_a_sum, gain_f_sum, jnp.zeros((6, D), f32)], axis=0)
+    for copy in last[1:]:
+        copy.wait()
+
+
+def local_call(lengths, byte_states, out_grad, patch_sum, mixed, small, wide, deep):
+    f32, low = jnp.float32, jnp.bfloat16
+    vmem = pl.BlockSpec(memory_space=pltpu.VMEM)
+    anywhere = pl.BlockSpec(memory_space=pl.ANY)
+    shape = jax.ShapeDtypeStruct
+    rows = byte_states.shape[0]
+    outs = [
+        shape((rows, D), low),
+        shape((rows, D), f32),
+        shape((rows // PATCH, EXT), low),
+        shape((rows // PATCH, D), f32),
+        shape((8, D), f32),
+        shape((D, 3 * D), low),
+        shape((D, D), low),
+        shape((D, deep.shape[0]), low),
+        shape((D, deep.shape[0]), low),
+        shape(deep.shape, low),
+    ]
+    scratch = [
+        pltpu.VMEM((D, 4 * D), low),
+        pltpu.VMEM((2, 3, D, D), low),
+        pltpu.VMEM((3, D, D), low),
+        pltpu.VMEM((rows, D), f32),
+        pltpu.VMEM((rows, D), low),
+        pltpu.VMEM((rows, 3 * D), low),
+        pltpu.VMEM((D // 128, rows // 128, 2, 128, 128), f32),
+        pltpu.VMEM((rows, D), low),
+        pltpu.VMEM((rows, D), f32),
+        pltpu.VMEM((rows, D), low),
+        pltpu.VMEM((D, rows), low),
+        pltpu.VMEM((rows, D), f32),
+        pltpu.VMEM((rows, D), f32),
+        pltpu.VMEM((rows, D), low),
+        pltpu.SemaphoreType.DMA((1,)),
+        pltpu.SemaphoreType.DMA((2, 3)),
+        pltpu.SemaphoreType.DMA((3,)),
+    ]
+    return pl.pallas_call(
+        local_kernel,
+        out_shape=outs,
+        in_specs=[pl.BlockSpec(memory_space=pltpu.SMEM)] + [vmem] * 5 + [anywhere] * 2,
+        out_specs=[vmem] * 5 + [anywhere] * 5,
+        scratch_shapes=scratch,
+        compiler_params=pltpu.CompilerParams(vmem_limit_bytes=60 * 2**20),
+        name="local_block",
+    )(lengths, byte_states, out_grad, patch_sum, mixed, small, wide, deep)
+
+
 BC = 2 * STATE
-
-
-def split_heads(rows_by_cols):
-    rows = rows_by_cols.shape[0]
-    return rows_by_cols.reshape(rows // 128, 128, -1, HEAD).transpose(2, 0, 1, 3)
-
-
-def join_heads(heads):
-    return heads.transpose(1, 2, 0, 3).reshape(heads.shape[1] * heads.shape[2], -1)
-
-
-def patch_mask():
-    places = jnp.arange(128)
-    return (places[:, None] >= places[None, :]) & (places[:, None] // PATCH == places[None, :] // PATCH)
-
-
-def dot_f32(spec, a, b):
-    return jnp.einsum(spec, a, b, preferred_element_type=jnp.float32)
 
 
 def fast_body(
@@ -1581,91 +1866,21 @@
     (wide, deep, patch_sum, mixed, small, all_bytes, norm8, proj8, head_w, own8, maps8, step8, core8) = forward_call(
         depth, n_dev, rows2, patch_proj, cols, vectors, out_proj, heads_in, qkv_proj, attn_out, gate_proj, up_proj, down_proj
     )
-    lines = small[:, shard_rows : shard_rows + 10]
-    gain_g, gain_a, gain_f = (lines[:, k, : D // n_dev].reshape(-1).astype(f32) for k in (5, 7, 8))
-    gain_m = lines[:, 6, : DI // n_dev].reshape(-1).astype(f32)
-    my_places = lax.axis_index("fsdp") * patches + jnp.arange(patches, dtype=jnp.int32)
-    live = jnp.repeat((my_places < doc_lengths[0, 0] + doc_lengths[0, 1]).astype(f32), PATCH)[:, None]
-    qk, vals, attn_o = wide[:, : 2 * D], wide[:, 2 * D : 3 * D], wide[:, 3 * D : 4 * D]
-    gate_w, up_w = wide[:, 4 * D : 8 * D], wide[:, 8 * D :]
-    down_a, down_b = deep[:, : D // 2], deep[:, D // 2 :]
-    raw_mixed = mixed[:, :D]
-    mixer_r = lax.rsqrt(mixed[:, D : D + 1] / DI + EPSILON)
-    mixed_patch = patch_sum + raw_mixed * mixer_r
-
-    streams = byte_states.astype(f32) + jnp.repeat(mixed_patch, PATCH, axis=0)
-    normed = rms_scale(streams, gain_a).astype(low)
-    queries, key_rows = jnp.split(product(normed, qk).astype(low), 2, axis=1)
-    queries, key_rows = split_heads(queries), split_heads(key_rows)
-    value_rows = split_heads(product(normed, vals).astype(low))
-    scale = HEAD ** (-0.5)
-    scores = dot_f32("hbid,hbjd->hbij", queries, key_rows) * scale
-    attn_weights = jax.nn.softmax(jnp.where(patch_mask(), scores, -1e30), axis=-1)
-    attn_low = attn_weights.astype(low)
-    mixed_heads = join_heads(dot_f32("hbij,hbjd->hbid", attn_low, value_rows).astype(low))
-    attended = streams + product(mixed_heads, attn_o)
-    ffn_low = rms_scale(attended, gain_f).astype(low)
-    gate = product(ffn_low, gate_w)
-    upward = product(ffn_low, up_w)
-    sigma = jax.nn.sigmoid(gate)
-    hidden = (gate * sigma * upward).astype(low)
-    ffn_out = jnp.concatenate([product(hidden, down_a), product(hidden, down_b)], axis=1)
-    block_out = (live * (attended + ffn_out)).astype(low)
-
-    def scattered(act, grad):
-        return weight_grad(act, grad).astype(low)
-
-    grad_block = live * out_grad.astype(f32)
-    down_low = grad_block.astype(low)
-    grad_down = scattered(hidden, down_low)
-    grad_hidden = input_grad(down_low[:, : D // 2], down_a) + input_grad(down_low[:, D // 2 :], down_b)
-    grad_gate_low = (grad_hidden * upward * sigma * (1.0 + gate * (1.0 - sigma))).astype(low)
-    grad_up_low = (grad_hidden * gate * sigma).astype(low)
-    grad_gate = scattered(ffn_low, grad_gate_low)
-    grad_up = scattered(ffn_low, grad_up_low)
-    grad_ffn_in = input_grad(grad_gate_low, gate_w) + input_grad(grad_up_low, up_w)
-    _, norm_back = jax.vjp(rms_scale, attended, gain_f)
-    grad_attended_norm, grad_gain_f = norm_back(grad_ffn_in)
-    grad_attended = grad_block + grad_attended_norm
-    attn_grad_low = grad_attended.astype(low)
-    grad_attn_out = scattered(mixed_heads, attn_grad_low)
-    grad_mixed = split_heads(input_grad(attn_grad_low, attn_o).astype(low))
-    grad_values = dot_f32("hbij,hbid->hbjd", attn_low, grad_mixed)
-    grad_weights = dot_f32("hbid,hbjd->hbij", grad_mixed, value_rows)
-    grad_scores = attn_weights * (
-        grad_weights - jnp.sum(attn_weights * grad_weights, axis=-1, keepdims=True)
-    )
-    scores_low = grad_scores.astype(low)
-    grad_queries = dot_f32("hbij,hbjd->hbid", scores_low, key_rows) * scale
-    grad_keys = dot_f32("hbij,hbid->hbjd", scores_low, queries) * scale
-    grad_qk = jnp.concatenate([join_heads(grad_queries.astype(low)), join_heads(grad_keys.astype(low))], axis=1)
-    grad_v = join_heads(grad_values.astype(low))
-    grad_qkv = scattered(normed, jnp.concatenate([grad_qk, grad_v], axis=1))
-    grad_normed = input_grad(grad_qk, qk) + input_grad(grad_v, vals)
-    _, norm_back = jax.vjp(rms_scale, streams, gain_a)
-    grad_streams_norm, grad_gain_a = norm_back(grad_normed)
-    grad_streams = grad_attended + grad_streams_norm
-
-    grad_patch_mix = grad_streams.reshape(patches, PATCH, D).sum(axis=1)
-    mix_low = grad_patch_mix.astype(low)
-    along = jnp.sum(mix_low.astype(f32) * raw_mixed, axis=1, keepdims=True)
-    pair = jnp.concatenate([mixer_r, along], axis=1)
-    pair_high = pair.astype(low)
-    pair_rest = (pair - pair_high.astype(f32)).astype(low)
-    extra = jnp.pad(jnp.concatenate([pair_high, pair_rest], axis=1), ((0, 0), (0, 124)))
-    gains = jnp.pad(jnp.stack([grad_gain_a, grad_gain_f]), ((0, 6), (0, 0)))
+    block_out, grad_streams, mix, direct, gains, *grads = local_call(
+        doc_lengths, byte_states, out_grad, patch_sum, mixed, small, wide, deep
+    )
     saved = (small, all_bytes, norm8, proj8, head_w, own8, maps8, step8, core8)
     (g_qkv, g_attn, g_gate, g_up, g_down, g_patch, back_rows, g_out, g_cols, g_maps, everyone) = backward_call(
         depth,
         n_dev,
-        jnp.concatenate([mix_low, extra], axis=1),
-        grad_patch_mix,
+        mix,
+        direct,
         patch_sum,
         gains,
         saved,
         patch_proj,
         heads_in,
-        (grad_qkv, grad_attn_out, grad_gate, grad_up, grad_down),
+        grads,
     )
     grad_states = grad_streams + back_rows.reshape(rows, D).astype(f32)
 

time: 641 us -> 552 us (0.86)
  the two profiles are of different devices: /device:TPU:0 before, /device:TPU:8 now
where the time goes in v4:
time: 552 us; the launch traced here: 541 us
  Pallas kernels  510 us (92%)
  local copies, waits for them, and re-layouts  22.4 us (4%)
  other arithmetic  7.21 us (1%)
    pallas_call x1, Pallas kernels, backward_call(): pl.pallas_call(partial(backward_kernel, depth), out_shape=outs, in_specs=...  227 us
    pallas_call x1, Pallas kernels, forward_call(): pl.pallas_call(partial(forward_kernel, depth), out_shape=outs, in_specs=[...  219 us
    pallas_call x1, Pallas kernels, local_call(): pl.pallas_call(local_kernel, out_shape=outs, in_specs=[pl.BlockSpec(memor...  64.6 us

profile of v4, /device:TPU:8, one launch (start us, length us, event | category | flops | bytes accessed | tf_op | source)
XLA Modules:
  0.0 541.4 jit_solution(12303377780837873031)
XLA Ops:
  0.7 0.0 copy-start.14
  0.7 0.0 copy-start.13
  0.7 0.0 copy-start
  0.7 0.8 slice_bitcast_fusion.5
  1.6 0.7 slice.81
  2.4 0.7 convert_bitcast_fusion
  3.1 0.7 pad.47
  3.7 0.7 pad.48
  4.4 0.7 pad.49
  5.1 0.7 pad.50
  5.7 0.7 pad.51
  6.4 1.9 concatenate.13.vec_ref
  8.3 1.0 fusion.6
  9.2 0.2 reshape.104
  9.5 0.1 copy.63
  9.6 0.2 reshape.105
  9.8 0.2 reshape.106
  10.1 0.1 copy.62
  10.2 0.2 reshape.107
  10.4 0.7 pad_maximum_fusion.1.cols_ref
  11.1 0.0 copy-done.14
  11.1 0.6 select_maximum_fusion.heads_ref
  11.7 1.0 reshape.103.rows_ref
  12.8 218.8 %global_forward.1 = (bf16[1024,12288]{1,0:T(8,128)(2,1)}, bf16[4096,1024]{1,0:T(8,128)(2,1)}, f32[32,1024]{1,0:T(8,128)}, f32[32,1152]{1,0:T(8,128)}, bf16[32,48...) custom-call(bf16[32,8192]{1,0:T(8,128)(2,1)} %reshape.103.rows_ref, ...), custom_call_target="tpu_custom_call" | custom-call | tf_op jit(solution)/shard_map/global_forward/pallas_call | solution.py:1071
  231.6 64.6 %local_block.1 = (bf16[256,1024]{1,0:T(8,128)(2,1)}, f32[256,1024]{1,0:T(8,128)}, bf16[32,1152]{1,0:T(8,128)(2,1)}, f32[32,1024]{1,0:T(8,128)}, f32[8,1024]{1,0:...) custom-call(s32[1,2]{1,0:T(1,128)} %lengths.1, ...), custom_call_target="tpu_custom_call" | custom-call | tf_op jit(solution)/shard_map/local_block/pallas_call | solution.py:1811
  296.1 227.0 %global_backward.1 = (f32[32,3072]{1,0:T(8,128)}, f32[32,1024]{1,0:T(8,128)}, f32[32,4096]{1,0:T(8,128)}, f32[32,4096]{1,0:T(8,128)}, f32[128,1024]{1,0:T(8,128)...) custom-call(bf16[32,1152]{1,0:T(8,128)(2,1)} %get-tuple-element.60.m, ...), custom_call_target="tpu_custom_call" | custom-call | tf_op jit(solution)/shard_map/global_backward/pallas_call | solution.py:1541
  523.1 1.4 fusion
  524.6 0.6 slice_bitcast_fusion.1
  525.2 1.5 slice_convert_fusion
  526.7 0.2 reduce_sum.19
  527.0 0.0 copy-start.3
  527.0 0.1 reshape.118
  527.1 0.1 reshape.119
  527.2 0.1 fusion.1
  527.3 0.6 slice_bitcast_fusion
  527.9 0.5 slice_bitcast_fusion.4
  528.5 0.2 reshape.113
  528.7 0.3 copy.55
  529.0 0.0 copy-start.1
  529.1 0.2 reshape.114
  529.2 0.2 reshape.115
  529.5 0.3 copy.56
  529.8 0.2 reshape.116
  530.0 0.8 pad_maximum_fusion
  530.8 0.6 fusion.2
  531.4 0.9 slice_reduce_fusion
  532.3 0.1 reshape.120
  532.4 0.1 squeeze_reshape.3
  532.5 0.6 dynamic_slice.24
  533.0 1.3 reshape.121
  534.3 0.0 copy-start.8
  534.4 0.0 copy-done.1
  534.4 0.0 copy-start.10
  534.4 0.0 copy-start.6
  534.4 1.1 add.41
  535.5 1.0 copy.71
  536.5 0.7 copy.72
  537.2 0.7 copy.73
  537.9 0.0 copy-done.10
  537.9 0.7 copy.74
  538.6 0.0 copy-done.6
  538.6 0.8 copy.75
  539.4 0.8 copy.76
  540.2 0.8 copy.77
  (43 shorter events, 0.2 us)
Async XLA Ops:
  0.7 10.5 %copy-start.14 = (f32[32]{0:T(128)S(1)}, f32[32]{0:T(128)}, u32[]{:S(2)}) copy-start(f32[32]{0:T(128)} %param.29) | copy-start | bytes 388
  0.7 10.5 %copy-start.13 = (f32[32]{0:T(128)S(1)}, f32[32]{0:T(128)}, u32[]{:S(2)}) copy-start(f32[32]{0:T(128)} %param.28) | copy-start | bytes 388
  0.7 10.4 %copy-start.12 = (f32[32]{0:T(128)S(1)}, f32[32]{0:T(128)}, u32[]{:S(2)}) copy-start(f32[32]{0:T(128)} %param.30) | copy-start | bytes 388
  0.7 11.1 %copy-start = (bf16[256,1024]{1,0:T(8,128)(2,1)S(1)}, bf16[256,1024]{1,0:T(8,128)(2,1)}, u32[]{:S(2)}) copy-start(bf16[256,1024]{1,0:T(8,128)(2,1)} %bytes_ref.1) | copy-start | bytes 1572868
  525.2 3.2 copy-start.7
  527.0 1.8 copy-start.3
  528.4 1.6 copy-start.11
  529.0 5.3 copy-start.1
  530.0 5.5 %copy-start.2 = (f32[256,1024]{1,0:T(8,128)S(1)}, f32[256,1024]{1,0:T(8,128)}, u32[]{:S(2)}) copy-start(f32[256,1024]{1,0:T(8,128)} %get-tuple-element.125) | copy-start | bytes 3145732
  533.0 3.4 copy-start.9
  534.3 2.8 copy-start.8
  534.4 3.6 copy-start.10
  534.4 4.2 copy-start.6
  535.5 3.9 copy-start.5
  535.5 4.7 copy-start.4

commit v5 on v3

--- a/solution.py
+++ b/solution.py
@@ -453,6 +453,11 @@
 
 MESH = pl.DeviceIdType.MESH
 WIDE = 12288
+PARTS = ((0, 3072), (3072, 1024), (4096, 4096), (8192, 4096))
+STEP = 1024
+FAR_F, FAR_B = 2048, 2048
+CUTS = (2048, 2048, 1024)
+CUTS_F = (1024, 1024, 1024)
 TILE = 32
 SMALL_ROWS, SMALL_COLS = 48, 384
 EXT = D + 128
@@ -555,6 +560,20 @@
 
     def leave(self):
         self.each(lambda copy: copy.wait_send())
+
+
+def plane_swap(wires, spot, src_at, dst_at):
+    copies = []
+    for way in range(4):
+        for other in range(2):
+            if way or other:
+                x = spot.x ^ (way >> 1)
+                y = spot.y ^ (way & 1)
+                c = spot.c ^ other
+                copies.append(
+                    wires.copy(src_at(x * 4 + y * 2 + c), dst_at(spot.q), device(spot.z, x, y, c))
+                )
+    return copies
 
 
 def block_row(t, plane, c):
@@ -668,83 +687,128 @@
 
 
 def big_gather(wires, spot, ow, od, shards):
-    half, down = WIDE // 2, od.shape[0] // spot.count
+    down = od.shape[0] // spot.count
     xn, yn, cn, zn = spot.flip(2)[0], spot.flip(1)[0], spot.sibling(), spot.above(1)
     here, xp, yp, xy = spot.plane, spot.flip(2)[1], spot.flip(1)[1], spot.flip(3)[1]
+    parts = {"C": (WIDE - FAR_F, FAR_F, None), ("A", 0): (0, 2 * D, None), ("B", 0): (2 * D, 2 * D, None)}
+    begin, side, at = 4 * D, (WIDE - FAR_F - 4 * D) // 2, 0
+    for i, width in enumerate(CUTS_F, 1):
+        last = i == len(CUTS_F)
+        parts["A", i] = (begin + at, width, (0, down // 2) if last else None)
+        parts["B", i] = (begin + side + at, width, (down // 2, down // 2) if last else None)
+        at += width
+    assert at == side
+    mine = pl.multiple_of(spot.me * TILE, TILE)
+    row = pl.multiple_of(spot.me * down, down)
 
     def refs(t, plane, part):
+        begin, width, deep = parts[part]
         r = block_row(t, plane, spot.c)
-        wide, deep = pl.multiple_of(r * TILE, TILE), pl.multiple_of(r * down, down)
-        if part == "A":
-            return [ow.at[pl.ds(wide, TILE), pl.ds(0, half)], od.at[pl.ds(deep, down // 2)]]
-        if part == "B":
-            return [
-                ow.at[pl.ds(wide, TILE), pl.ds(half, half)],
-                od.at[pl.ds(pl.multiple_of(deep + down // 2, down // 2), down // 2)],
-            ]
-        return [ow.at[pl.ds(wide, TILE)], od.at[pl.ds(deep, down)]]
+        found = [ow.at[pl.ds(pl.multiple_of(r * TILE, TILE), TILE), pl.ds(begin, width)]]
+        if deep:
+            found.append(od.at[pl.ds(pl.multiple_of(r * down + deep[0], deep[1]), deep[1])])
+        return found
 
     def go(t, plane, part, to):
         return [wires.copy(r, r, to) for r in refs(t, plane, part)]
 
-    qkv, attn, gate, up, deep = shards
-    cols, at = [], 0
-    mine = pl.multiple_of(spot.me * TILE, TILE)
-    for ref, a, b in ((qkv, 0, 3072), (attn, 0, 1024), (gate, 0, 2048), (gate, 2048, 2048), (up, 0, 4096)):
-        cols.append((ref.at[:, pl.ds(a, b)], ow.at[pl.ds(mine, TILE), pl.ds(at, b)]))
-        at += b
-    row = pl.multiple_of(spot.me * down, down)
-    deeps = [
-        (deep.at[pl.ds(h * down // 2, down // 2)], od.at[pl.ds(pl.multiple_of(row + h * (down // 2), down // 2), down // 2)])
-        for h in range(2)
-    ]
-
     def own(part, to):
-        pairs = {"A": cols[:3] + deeps[:1], "B": cols[3:] + deeps[1:], "AB": cols + deeps}[part]
+        begin, width, deep = parts[part]
+        pairs = []
+        for ref, (base, size) in zip(shards[:4], PARTS):
+            low, high = max(begin, base), min(begin + width, base + size)
+            if low < high:
+                pairs.append(
+                    (ref.at[:, pl.ds(low - base, high - low)], ow.at[pl.ds(mine, TILE), pl.ds(low, high - low)])
+                )
+        if deep:
+            pairs.append(
+                (shards[4].at[pl.ds(*deep)], od.at[pl.ds(pl.multiple_of(row + deep[0], deep[1]), deep[1])])
+            )
         return [wires.copy(a, b, to) for a, b in pairs]
 
     T = spot.column
-    core, ring, fx, fy, sx, sy = [], {}, {}, {}, {}, {}
-
-    def first(j):
+    core, ring, fx, fy, sx, sy = {i: [] for i in range(len(CUTS_F) + 2)}, {}, {}, {}, {}, {}
+
+    def arrived(j, i):
+        if (j - 1, i) in ring:
+            got(ring.pop((j - 1, i)))
+
+    def climb_on(j, i):
         send = own if j == 0 else (lambda part, to: go(T[j], here, part, to))
+        arrived(j, i)
+        ring[j, i] = send(("A", i), zn) + send(("B", i), zn)
+
+    def first(j, i):
+        send = own if j == 0 else (lambda part, to: go(T[j], here, part, to))
+        arrived(j, i)
+        fx[j, i], fy[j, i] = send(("A", i), xn), send(("B", i), yn)
+        core[i].append(send(("A", i), cn) + send(("B", i), cn))
+
+    def second(j, i):
+        send = own if j == 0 else (lambda part, to: go(T[j], here, part, to))
+        got(fx[j, i])
+        sy[j, i] = send(("A", i), yn) + go(T[j], xp, ("A", i), yn)
+        got(fy[j, i])
+        sx[j, i] = send(("B", i), xn) + go(T[j], yp, ("B", i), xn)
+        core[i].append(go(T[j], xp, ("A", i), cn) + go(T[j], yp, ("B", i), cn))
+
+    def third(j, i):
+        got(sy[j, i])
+        core[i].append(go(T[j], yp, ("A", i), cn) + go(T[j], xy, ("A", i), cn))
+        got(sx[j, i])
+        core[i].append(go(T[j], xp, ("B", i), cn) + go(T[j], xy, ("B", i), cn))
+
+    flat, climb = [], {}
+
+    def far(j):
+        if j < 0:
+            flat.extend(own("C", spot.flip(way)[0]) for way in (1, 2, 3))
+            core[len(CUTS_F) + 1].append(own("C", cn))
+            return
+        if j == 0:
+            for copies in flat:
+                got(copies)
+        else:
+            got(climb[j - 1])
         if j < spot.depth - 1:
-            ring[j] = send("AB", zn)
-        fx[j], fy[j] = send("A", xn), send("B", yn)
-        core.append(send("AB", cn))
-
-    def second(j):
-        got(fx[j])
-        sy[j] = (own("A", yn) if j == 0 else go(T[j], here, "A", yn)) + go(T[j], xp, "A", yn)
-        got(fy[j])
-        sx[j] = (own("B", xn) if j == 0 else go(T[j], here, "B", xn)) + go(T[j], yp, "B", xn)
-        core.append(go(T[j], xp, "A", cn) + go(T[j], yp, "B", cn))
-
-    def third(j):
-        got(sy[j])
-        core.append(go(T[j], yp, "A", cn) + go(T[j], xy, "A", cn))
-        got(sx[j])
-        core.append(go(T[j], xp, "B", cn) + go(T[j], xy, "B", cn))
-
-    first(0)
-    yield
-    for j in range(1, spot.depth):
-        second(j - 1)
-        yield
-        got(ring[j - 1])
-        first(j)
-        yield
-        if j >= 2:
-            third(j - 2)
-            yield
-    second(spot.depth - 1)
-    yield
-    third(spot.depth - 2)
-    third(spot.depth - 1)
-    yield
-    for copies in core:
-        got(copies)
-    yield
+            climb[j] = own("C", zn) if j == 0 else go(T[j], here, "C", zn)
+            for plane in (xp, yp, xy):
+                climb[j] += go(T[j], plane, "C", zn)
+        for plane in (xp, yp, xy) + ((here,) if j else ()):
+            core[len(CUTS_F) + 1].append(go(T[j], plane, "C", cn))
+
+    chunks, n = range(len(CUTS_F) + 1), spot.depth
+    steps = {"C%d" % j: partial(far, j) for j in range(-1, n)}
+    for i in chunks:
+        for j in range(n):
+            steps["r%d%d" % (j, i)] = partial(climb_on, j, i)
+            steps["a%d%d" % (j, i)] = partial(first, j, i)
+            steps["b%d%d" % (j, i)] = partial(second, j, i)
+            steps["c%d%d" % (j, i)] = partial(third, j, i)
+        del steps["r%d%d" % (n - 1, i)]
+
+    def close(which):
+        for part in which:
+            for copies in core.pop(part):
+                got(copies)
+
+    return steps, close
+
+
+class Ticker:
+    def __init__(self, steps, plan):
+        self.steps, self.plan = dict(steps), iter(plan)
+
+    def __call__(self):
+        for name in next(self.plan):
+            self.steps.pop(name)()
+
+    def rest(self, order):
+        for name in order:
+            if name in self.steps:
+                self.steps.pop(name)()
+        assert not self.steps
 
 
 def run(steps):
@@ -852,7 +916,323 @@
     return jnp.sum(jnp.where(lanes(row.shape, 1) == lane, row, 0.0), axis=1, keepdims=True)
 
 
-N_WIRES = 256
+def patch_pairs(count):
+    i, j = lanes((count, count), 0), lanes((count, count), 1)
+    return (i >= j) & ((i >> 3) == (j >> 3))
+
+
+def rms_back(value, gain, grad):
+    scale = lax.rsqrt(jnp.mean(value * value, axis=1, keepdims=True) + EPSILON)
+    along = jnp.mean(grad * gain * value, axis=1, keepdims=True)
+    d_value = scale * gain * grad - value * (scale * scale * scale * along)
+    return d_value, jnp.sum(grad * value * scale, axis=0, keepdims=True)
+
+
+def halves_of(block):
+    left = lanes(block.shape, 1) < HEAD
+    return left, [jnp.where(left, block, 0), jnp.where(left, 0, block)]
+
+
+def local_block(
+    tick,
+    ready,
+    whole,
+    lengths,
+    bytes_ref,
+    grad_ref,
+    sum_ref,
+    mixed_ref,
+    small_ref,
+    wide,
+    deep,
+    o_block,
+    o_streams,
+    o_mix,
+    o_direct,
+    o_gains,
+    g_qkv,
+    g_attn,
+    g_gate,
+    g_up,
+    g_down,
+    attn_w,
+    ffn_w,
+    g_buf,
+    streams,
+    normed,
+    qkv,
+    weights,
+    heads,
+    attended,
+    ffn_low,
+    ffn_t,
+    total,
+    d_ffn,
+    d_down,
+    load_sem,
+    ffn_sem,
+    g_sem,
+):
+    f32, low = jnp.float32, jnp.bfloat16
+    rows = bytes_ref.shape[0]
+    scale = HEAD ** (-0.5)
+    ready()
+    load = pltpu.make_async_copy(wide.at[:, pl.ds(0, 4 * D)], attn_w, load_sem.at[0])
+    load.start()
+
+    def ffn_loads(j, slot):
+        at = lambda base: pl.ds(pl.multiple_of(base + j * D, D), D)
+        return [
+            pltpu.make_async_copy(wide.at[:, at(4 * D)], ffn_w.at[slot, 0], ffn_sem.at[slot, 0]),
+            pltpu.make_async_copy(wide.at[:, at(8 * D)], ffn_w.at[slot, 1], ffn_sem.at[slot, 1]),
+            pltpu.make_async_copy(deep.at[at(0)], ffn_w.at[slot, 2], ffn_sem.at[slot, 2]),
+        ]
+
+    gain_a = gain_row(small_ref[:, TILE + 7, 0:128])
+    gain_f = gain_row(small_ref[:, TILE + 8, 0:128])
+    place = lax.axis_index("fsdp") * (rows // PATCH) + (lanes((rows, 1), 0) >> 3)
+    live = (place < lengths[0, 0] + lengths[0, 1]).astype(f32)
+    raw = mixed_ref[:, pl.ds(0, D)]
+    mixer_r = lax.rsqrt(mixed_ref[:, pl.ds(D, 128)] * (1.0 / DI) + EPSILON)[:, 0:1]
+    patch = sum_ref[...] + raw * mixer_r
+    patch = jnp.broadcast_to(patch[:, None, :], (rows // PATCH, PATCH, D)).reshape(rows, D)
+    streams[...] = bytes_ref[...].astype(f32) + patch
+    normed[...] = rms_scale(streams[...], gain_a).astype(low)
+    d_down[...] = (live * grad_ref[...].astype(f32)).astype(low)
+    load.wait()
+    for i in range(3):
+        at = pl.ds(i * D, D)
+        qkv[:, at] = flat_dot(normed[...], attn_w[:, at]).astype(low)
+        tick()
+    pairs = patch_pairs(128)
+
+    def blocks(p, b):
+        row = pl.ds(b * 128, 128)
+        return row, [pl.ds(pl.multiple_of(base + p * 128, 128), 128) for base in (0, D, 2 * D)]
+
+    def attend(p, carry):
+        for b in range(rows // 128):
+            row, (qa, ka, va) = blocks(p, b)
+            k, v = qkv[row, ka], qkv[row, va]
+            left, queries = halves_of(qkv[row, qa])
+            outs = []
+            for h in range(2):
+                scores = flat_dot(queries[h], k, ((1,), (1,))) * scale
+                scores = jnp.where(pairs, scores, -1e30)
+                e = jnp.exp(scores - jnp.max(scores, axis=1, keepdims=True))
+                w = e / jnp.sum(e, axis=1, keepdims=True)
+                weights[p, b, h] = w
+                outs.append(flat_dot(w.astype(low), v))
+            heads[row, qa] = jnp.where(left, outs[0], outs[1]).astype(low)
+        return carry
+
+    for begin in range(0, D // 128, 2):
+        lax.fori_loop(begin, begin + 2, attend, 0)
+        tick()
+    attended[...] = streams[...] + flat_dot(heads[...], attn_w[:, pl.ds(3 * D, D)])
+    ffn_low[...] = rms_scale(attended[...], gain_f).astype(low)
+    whole()
+    for copy in ffn_loads(0, 0):
+        copy.start()
+    ffn_t[...] = ffn_low[...].astype(f32).T.astype(low)
+    total[...] = attended[...]
+    d_ffn[...] = jnp.zeros_like(d_ffn)
+    n_ffn = deep.shape[0] // D
+
+    def stores(j):
+        at = pl.ds(pl.multiple_of(j * D, D), D)
+        return [
+            pltpu.make_async_copy(g_buf.at[0], g_gate.at[:, at], g_sem.at[0]),
+            pltpu.make_async_copy(g_buf.at[1], g_up.at[:, at], g_sem.at[1]),
+            pltpu.make_async_copy(g_buf.at[2], g_down.at[at], g_sem.at[2]),
+        ]
+
+    def feed(j, carry):
+        slot = lax.rem(j, 2)
+        for copy in ffn_loads(j, slot):
+            copy.wait()
+
+        @pl.when(j + 1 < n_ffn)
+        def _():
+            for copy in ffn_loads(j + 1, 1 - slot):
+                copy.start()
+
+        gate = flat_dot(ffn_low[...], ffn_w[slot, 0])
+        upward = flat_dot(ffn_low[...], ffn_w[slot, 1])
+        sig = sigmoid(gate)
+        act = gate * sig
+        hidden = (act * upward).astype(low)
+        total[...] += flat_dot(hidden, ffn_w[slot, 2])
+        d_hidden = flat_dot(d_down[...], ffn_w[slot, 2], ((1,), (1,)))
+        d_gate = (d_hidden * upward * (sig + act * (1.0 - sig))).astype(low)
+        d_up = (d_hidden * act).astype(low)
+        d_ffn[...] += flat_dot(d_gate, ffn_w[slot, 0], ((1,), (1,)))
+        d_ffn[...] += flat_dot(d_up, ffn_w[slot, 1], ((1,), (1,)))
+
+        @pl.when(j > 0)
+        def _():
+            for copy in stores(j - 1):
+                copy.wait()
+
+        g_buf[0] = flat_dot(ffn_t[...], d_gate).astype(low)
+        g_buf[1] = flat_dot(ffn_t[...], d_up).astype(low)
+        g_buf[2] = flat_dot(hidden.astype(f32).T.astype(low), d_down[...]).astype(low)
+        for copy in stores(j):
+            copy.start()
+        return carry
+
+    lax.fori_loop(0, n_ffn, feed, 0)
+    o_block[...] = (live * total[...]).astype(low)
+    d_norm, gain_f_sum = rms_back(attended[...], gain_f, d_ffn[...])
+    d_attended = live * grad_ref[...].astype(f32) + d_norm
+    total[...] = d_attended
+    d_low = d_attended.astype(low)
+    for copy in stores(n_ffn - 1):
+        copy.wait()
+    d_down[...] = flat_dot(d_low, attn_w[:, pl.ds(3 * D, D)], ((1,), (1,))).astype(low)
+    g_buf[0] = flat_dot(heads[...].astype(f32).T.astype(low), d_low).astype(low)
+    last = [pltpu.make_async_copy(g_buf.at[0], g_attn, g_sem.at[0])]
+    last[0].start()
+
+    def attend_back(p, carry):
+        for b in range(rows // 128):
+            row, (qa, ka, va) = blocks(p, b)
+            q, k, v = qkv[row, qa], qkv[row, ka], qkv[row, va]
+            grad = d_down[row, qa]
+            left, grads = halves_of(grad)
+            dq, dk, dv = [], [], []
+            for h in range(2):
+                w = weights[p, b, h]
+                dv.append(flat_dot(w.T.astype(low), grad))
+                d_w = flat_dot(grads[h], v, ((1,), (1,)))
+                d_s = w * (d_w - jnp.sum(w * d_w, axis=1, keepdims=True))
+                dq.append(flat_dot(d_s.astype(low), k) * scale)
+                dk.append(flat_dot(d_s.T.astype(low), q) * scale)
+            qkv[row, qa] = jnp.where(left, dq[0], dq[1]).astype(low)
+            qkv[row, ka] = jnp.where(left, dk[0], dk[1]).astype(low)
+            qkv[row, va] = jnp.where(left, dv[0], dv[1]).astype(low)
+        return carry
+
+    lax.fori_loop(0, D // 128, attend_back, 0)
+    ffn_t[...] = normed[...].astype(f32).T.astype(low)
+    for i in range(3):
+        at = pl.ds(i * D, D)
+        if i == 2:
+            last[0].wait()
+        buf = (i + 1) % 3
+        g_buf[buf] = flat_dot(ffn_t[...], qkv[:, at]).astype(low)
+        copy = pltpu.make_async_copy(g_buf.at[buf], g_qkv.at[:, at], g_sem.at[buf])
+        copy.start()
+        last.append(copy)
+    d_ffn[...] = flat_dot(qkv[...], attn_w[:, pl.ds(0, 3 * D)], ((1,), (1,)))
+    d_norm, gain_a_sum = rms_back(streams[...], gain_a, d_ffn[...])
+    d_streams = total[...] + d_norm
+    o_streams[...] = d_streams
+    direct = jnp.sum(d_streams.reshape(rows // PATCH, PATCH, D), axis=1)
+    o_direct[...] = direct
+    mix = direct.astype(low)
+    along = jnp.sum(mix.astype(f32) * raw, axis=1, keepdims=True)
+    high_r, high_a = (v.astype(low).astype(f32) for v in (mixer_r, along))
+    lane = lanes((rows // PATCH, 128), 1)
+    ext = jnp.zeros((rows // PATCH, 128), f32)
+    for i, v in enumerate((high_r, high_a, mixer_r - high_r, along - high_a)):
+        ext = jnp.where(lane == i, v, ext)
+    o_mix[:, pl.ds(0, D)] = mix
+    o_mix[:, pl.ds(D, 128)] = ext.astype(low)
+    o_gains[...] = jnp.concatenate([gain_a_sum, gain_f_sum, jnp.zeros((6, D), f32)], axis=0)
+    for copy in last[1:]:
+        copy.wait()
+
+
+N_WIRES = 512
+PLAN_F = (
+    ("C-1", "r00", "a00"),
+    (),
+    (),
+    (),
+    ("b00", "a01"),
+    ("r10", "a10", "r01"),
+    (),
+    ("b10", "a02", "r20"),
+    ("c00",),
+    ("a20", "b01"),
+    ("b20", "r02", "r03", "a03"),
+    ("c10",),
+    ("b02",),
+    ("a30",),
+    ("r11", "a11"),
+    ("C0",),
+    ("b30",),
+    ("c20",),
+    ("r12", "a12"),
+    ("b03",),
+    ("r13", "a13"),
+    (),
+    ("c30", "b11", "b12"),
+    ("r21", "a21"),
+    ("b13", "r22", "a22"),
+    ("C1", "c01", "c02"),
+    ("r23", "a23", "b21"),
+    ("b22", "c03", "c11"),
+    ("a31", "b23", "c12"),
+    ("C2", "a32", "c13"),
+)
+REST_F = (
+    "b31",
+    "a33",
+    "b32",
+    "b33",
+    "C3",
+    "c21",
+    "c22",
+    "c23",
+    "c31",
+    "c32",
+    "c33",
+)
+PLAN_B = (
+    (),
+    (),
+    ("a00",),
+    ("a01", "a02"),
+    ("C0",),
+    ("a10",),
+    (),
+    ("C1",),
+    ("a11",),
+    ("b00",),
+    ("a20",),
+    ("C2",),
+    ("c00",),
+    (),
+    (),
+    (),
+    ("b01", "a12"),
+    (),
+    (),
+    ("b02",),
+    ("b10", "a21"),
+    (),
+    (),
+    ("a22", "c01", "b11", "c10"),
+    ("a30", "b12", "c02"),
+    ("a31", "b20"),
+    ("c11", "a32", "b21", "C3"),
+)
+REST_B = (
+    "c12",
+    "b22",
+    "c20",
+    "b30",
+    "c21",
+    "b31",
+    "c22",
+    "b32",
+    "C4",
+    "c30",
+    "c31",
+    "c32",
+)
 
 
 def forward_kernel(
@@ -863,6 +1243,9 @@
     vec_ref,
     out_ref,
     heads_ref,
+    lengths,
+    states_ref,
+    grad_ref,
     qkv,
     attn,
     gate,
@@ -870,8 +1253,17 @@
     down,
     ow,
     od,
+    o_block,
+    o_streams,
+    o_mix,
+    o_direct,
+    o_gains,
+    g_qkv,
+    g_attn,
+    g_gate,
+    g_up,
+    g_down,
     sum_ref,
-    mixed_ref,
     small_ref,
     bytes_ref,
     norm_ref,
@@ -881,6 +1273,24 @@
     maps_ref,
     step_ref,
     core_ref,
+    mixed_ref,
+    attn_w,
+    ffn_w,
+    g_buf,
+    streams,
+    normed,
+    qkv_low,
+    weights,
+    mixed_heads,
+    attended,
+    ffn_low,
+    ffn_t,
+    total_ref,
+    d_ffn,
+    d_down,
+    load_sem,
+    ffn_sem,
+    g_sem,
     parts,
     pair,
     near,
@@ -911,25 +1321,23 @@
 
     swap_bytes = Swap(
         spot,
-        swap_send.at[0],
-        swap_recv.at[0],
+        swap_send,
+        swap_recv,
         lanes_of,
         lambda me: bytes_ref.at[pl.ds(pl.multiple_of(me * TILE, TILE), TILE)],
     )
     swap_bytes.start()
-    big = big_gather(wires, spot, ow, od, (qkv, attn, gate, up, down))
-    swap_proj = Swap(
+    steps, close = big_gather(wires, spot, ow, od, (qkv, attn, gate, up, down))
+    near_proj = plane_swap(
+        wires,
         spot,
-        swap_send.at[1],
-        swap_recv.at[1],
-        lambda to: cols_ref.at[to % 8],
-        lambda me: proj_ref.at[pl.ds(pl.multiple_of(me * TILE, TILE), TILE)],
-    )
-    swap_proj.start()
+        lambda q: cols_ref.at[q],
+        lambda q: proj_ref.at[pl.ds(pl.multiple_of((spot.z * 8 + q) * TILE, TILE), TILE)],
+    )
     small = spread_all(wires, spot, small_ref)
     next(small)
-    head_w = [wires.copy(out_ref, head_w_ref.at[spot.z], spot.above(k)) for k in range(1, depth)]
-    next(big)
+    tick = Ticker(steps, PLAN_F)
+    tick()
     own_rows = []
     at = 0
     for i, ref in enumerate((qkv, attn, gate, up)):
@@ -942,19 +1350,28 @@
     )
     for copy in own_rows:
         copy.start()
+    tick()
     swap_bytes.arrive()
+    got(near_proj)
+    layer = proj_ref.at[pl.ds(pl.multiple_of(spot.z * 8 * TILE, 8 * TILE), 8 * TILE)]
+    far_proj = [wires.copy(layer, layer, spot.above(k)) for k in range(1, depth)]
 
     for b in range(4):
         block = flat_dot(bytes_ref[pl.ds(b * 256, 256)], patch_ref[...]).astype(low)
         parts[pl.ds(b * 4, 4)] = block.reshape(4, 2, TILE, D)
+    tick()
     total = sum_all(wires, spot, parts, pair, near, column, far, sum_ref)
     next(total)
     next(small)
+    tick()
     next(total)
-    next(big)
+    tick()
     next(total)
     next(small)
+    tick()
+    head_w = [wires.copy(out_ref, head_w_ref.at[spot.z], spot.above(k)) for k in range(1, depth)]
     next(total)
+    tick()
     run(small)
     patch_sum = sum_ref[...]
     scale = lax.rsqrt(jnp.mean(patch_sum * patch_sum, axis=1, keepdims=True) + EPSILON)
@@ -962,17 +1379,20 @@
     norm_ref[spot.q] = (patch_sum * scale * gain).astype(low)
     plane = spread_plane(wires, spot, norm_ref)
     next(plane)
+    tick()
     next(plane)
-    swap_proj.arrive()
+    tick()
+    got(far_proj)
     taps = tap_rows(spot, small_ref)
     run(plane)
-    next(big)
+    tick()
 
     norm = norm_ref[...].reshape(2 * count, D)
     own_ref[...] = flat_dot(norm, proj_ref[...])
     maps_ref[...] = flat_dot(norm, small_ref[:, :TILE, 0:256].reshape(D, 256))
     step_ref[...] = flat_dot(norm, small_ref[:, :TILE, 256:384].reshape(D, 128))
     dt_row, rate_row, skip_row = heads_ref[0:1], heads_ref[1:2], heads_ref[2:3]
+    tick()
     got(head_w)
     gains = jnp.concatenate(
         [small_ref[spot.q + 8 * i, TILE : TILE + 16, 0:HEAD_M][6:7].astype(f32) for i in range(4)], axis=1
@@ -984,6 +1404,7 @@
         mix = Mixed(spot, slot, own, maps, step_ref[at], taps, dt_row, rate_row)
         outs = []
         for i in range(4):
+            tick()
             inputs = mix.inputs[:, i * HEAD_M : (i + 1) * HEAD_M]
             mixing = (mix.decay(i) * mix.inner * mix.row(mix.step_t, i)).astype(low)
             skip = pick_lane(skip_row, mix.head(i))
@@ -998,28 +1419,104 @@
         parts8[pl.ds(x * 2, 2), :, :, pl.ds(D, 128)] = (
             jnp.broadcast_to(squares, (count, 128)).astype(low).reshape(2, 2, TILE, 128)
         )
+        tick()
     for total in sum_plane(wires, spot, parts8, pair8, near8):
-        pass
+        if total is None:
+            tick()
     mixed_ref[...] = total
-    for copy in own_rows:
-        copy.wait()
-    run(big)
+
+    def ready():
+        for copy in own_rows:
+            copy.wait()
+        close([0])
+
+    def whole():
+        tick.rest(REST_F)
+        close(range(1, len(CUTS_F) + 2))
+
+    local_block(
+        tick,
+        ready,
+        whole,
+        lengths,
+        states_ref,
+        grad_ref,
+        sum_ref,
+        mixed_ref,
+        small_ref,
+        ow,
+        od,
+        o_block,
+        o_streams,
+        o_mix,
+        o_direct,
+        o_gains,
+        g_qkv,
+        g_attn,
+        g_gate,
+        g_up,
+        g_down,
+        attn_w,
+        ffn_w,
+        g_buf,
+        streams,
+        normed,
+        qkv_low,
+        weights,
+        mixed_heads,
+        attended,
+        ffn_low,
+        ffn_t,
+        total_ref,
+        d_ffn,
+        d_down,
+        load_sem,
+        ffn_sem,
+        g_sem,
+    )
     wires.drain()
     swap_bytes.leave()
-    swap_proj.leave()
-
-
-def forward_call(depth, n_dev, rows2, patch_proj, cols, vectors, out_proj, heads, qkv, attn, gate, up, down):
+
+
+def forward_call(
+    depth,
+    n_dev,
+    rows2,
+    patch_proj,
+    cols,
+    vectors,
+    out_proj,
+    heads,
+    lengths,
+    byte_states,
+    out_grad,
+    qkv,
+    attn,
+    gate,
+    up,
+    down,
+):
     f32, low = jnp.float32, jnp.bfloat16
     vmem = pl.BlockSpec(memory_space=pltpu.VMEM)
     anywhere = pl.BlockSpec(memory_space=pl.ANY)
+    smem = pl.BlockSpec(memory_space=pltpu.SMEM)
     shape = jax.ShapeDtypeStruct
     plane_patches = 8 * TILE
+    rows, hidden = byte_states.shape[0], down.shape[0] * n_dev
     outs = [
         shape((D, WIDE), low),
-        shape((down.shape[0] * n_dev, D), low),
+        shape((hidden, D), low),
+        shape((rows, D), low),
+        shape((rows, D), f32),
+        shape((rows // PATCH, EXT), low),
+        shape((rows // PATCH, D), f32),
+        shape((8, D), f32),
+        shape((D, 3 * D), low),
+        shape((D, D), low),
+        shape((D, hidden), low),
+        shape((D, hidden), low),
+        shape((hidden, D), low),
         shape((TILE, D), f32),
-        shape((TILE, EXT), f32),
         shape((n_dev, SMALL_ROWS, SMALL_COLS), low),
         shape((n_dev * TILE, 256), low),
         shape((8, TILE, D), low),
@@ -1031,6 +1528,24 @@
         shape((plane_patches, 256), f32),
     ]
     scratch = [
+        pltpu.VMEM((TILE, EXT), f32),
+        pltpu.VMEM((D, 4 * D), low),
+        pltpu.VMEM((2, 3, D, D), low),
+        pltpu.VMEM((3, D, D), low),
+        pltpu.VMEM((rows, D), f32),
+        pltpu.VMEM((rows, D), low),
+        pltpu.VMEM((rows, 3 * D), low),
+        pltpu.VMEM((D // 128, rows // 128, 2, 128, 128), f32),
+        pltpu.VMEM((rows, D), low),
+        pltpu.VMEM((rows, D), f32),
+        pltpu.VMEM((rows, D), low),
+        pltpu.VMEM((D, rows), low),
+        pltpu.VMEM((rows, D), f32),
+        pltpu.VMEM((rows, D), f32),
+        pltpu.VMEM((rows, D), low),
+        pltpu.SemaphoreType.DMA((1,)),
+        pltpu.SemaphoreType.DMA((2, 3)),
+        pltpu.SemaphoreType.DMA((3,)),
         pltpu.VMEM((16, 2, TILE, D), low),
         pltpu.VMEM((16, TILE, D), low),
         pltpu.VMEM((3, depth, TILE, D), low),
@@ -1041,25 +1556,23 @@
         pltpu.VMEM((3, TILE, EXT), low),
         pltpu.SemaphoreType.DMA((N_WIRES,)),
         pltpu.SemaphoreType.DMA((N_WIRES,)),
-        pltpu.SemaphoreType.DMA((2, n_dev)),
-        pltpu.SemaphoreType.DMA((2, n_dev)),
+        pltpu.SemaphoreType.DMA((n_dev,)),
+        pltpu.SemaphoreType.DMA((n_dev,)),
         pltpu.SemaphoreType.DMA((5,)),
     ]
-    return pl.pallas_call(
+    found = pl.pallas_call(
         partial(forward_kernel, depth),
         out_shape=outs,
-        in_specs=[vmem] * 6 + [anywhere] * 5,
-        out_specs=[anywhere] * 2 + [vmem] * 11,
+        in_specs=[vmem] * 6 + [smem] + [vmem] * 2 + [anywhere] * 5,
+        out_specs=[anywhere] * 2 + [vmem] * 5 + [anywhere] * 5 + [vmem] * 10,
         scratch_shapes=scratch,
         compiler_params=pltpu.CompilerParams(
-            collective_id=0, has_side_effects=True, vmem_limit_bytes=56 * 2**20
+            collective_id=0, has_side_effects=True, vmem_limit_bytes=62 * 2**20
         ),
         name="global_forward",
-    )(rows2, patch_proj, cols, vectors, out_proj, heads, qkv, attn, gate, up, down)
-
-
-PARTS = ((0, 3072), (3072, 1024), (4096, 4096), (8192, 4096))
-STEP = 1024
+    )(rows2, patch_proj, cols, vectors, out_proj, heads, lengths, byte_states, out_grad, qkv, attn, gate, up, down)
+    block, streams, mix, direct, gains, *rest = found[2:]
+    return (block, streams, mix, direct, gains), rest[:5], rest[5], rest[6:]
 
 
 def add_to(dst, sources, width):
@@ -1076,13 +1589,15 @@
 
 def big_scatter(wires, spot, grads, bufs, outs, local):
     f32, low = jnp.float32, jnp.bfloat16
-    held_w, held_d, stage_w, stage_d, near_w, near_d, last_w, last_d, ring_w, ring_d = bufs
-    half, deep = WIDE // 2, held_d.shape[2]
+    held_w, held_d, stage_w, stage_d, near_w, near_d, last_w, last_d, ring_w, ring_d, climb_c, flat_c = bufs
+    half, deep = (WIDE - FAR_B) // 2, held_d.shape[2]
     xn, yn, cn, zn = spot.flip(2)[0], spot.flip(1)[0], spot.sibling(), spot.above(1)
     here, xp, yp, xy = spot.plane, spot.flip(2)[1], spot.flip(1)[1], spot.flip(3)[1]
     T = [spot.column[k % spot.depth] for k in range(1, spot.depth + 1)]
     core, fetch, near, last, ring = {}, {}, {}, {}, {}
-    A, B = pl.ds(0, half), pl.ds(half, half)
+    A, B, C = pl.ds(0, half), pl.ds(half, half), pl.ds(2 * half, FAR_B)
+    AB = pl.ds(0, 2 * half)
+    climb, flat = {}, []
     DA, DB = pl.ds(0, deep // 2), pl.ds(deep // 2, deep // 2)
 
     def load(k):
@@ -1099,7 +1614,7 @@
             dst = held_w.at[T[k], :, :, pl.ds(*PARTS[i])] if i < 4 else held_d.at[T[k]]
             core[k].append(wires.copy(ref.at[T[k], :, 1 - spot.c], dst, cn))
 
-    def first(k):
+    def join(k):
         t = T[k]
         got(core[k])
         for copy in fetch[k]:
@@ -1113,102 +1628,164 @@
             held_d[t, plane] = (held_d[t, plane].astype(f32) + stage_d[plane].astype(f32)).astype(low)
         if k + 1 < spot.depth:
             load(k + 1)
-        near[k] = []
+
+    parts, at = [], 0
+    for i, width in enumerate(CUTS):
+        end = i == len(CUTS) - 1
+        width = half - at if end else width
+        parts.append((at, width, end))
+        at += width
+
+    def spans(i):
+        at, width, end = parts[i]
+        found = [(pl.ds(at, width), pl.ds(half + at, width))]
+        return found, end
+
+    def near_sends(k, i):
+        t = T[k]
+        [(a, b)], end = spans(i)
+        sends = []
         for x in range(2):
             src = x * 2 + (1 - spot.y)
-            near[k].append(wires.copy(held_w.at[t, src, :, A], near_w.at[k, x, :, A], yn))
-            near[k].append(wires.copy(held_d.at[t, src, DA], near_d.at[k, x, DA], yn))
+            sends.append(wires.copy(held_w.at[t, src, :, a], near_w.at[k, x, :, a], yn))
+            if end:
+                sends.append(wires.copy(held_d.at[t, src, DA], near_d.at[k, x, DA], yn))
         for y in range(2):
             src = (1 - spot.x) * 2 + y
-            near[k].append(wires.copy(held_w.at[t, src, :, B], near_w.at[k, y, :, B], xn))
-            near[k].append(wires.copy(held_d.at[t, src, DB], near_d.at[k, y, DB], xn))
-
-    def second(k):
+            sends.append(wires.copy(held_w.at[t, src, :, b], near_w.at[k, y, :, b], xn))
+            if end:
+                sends.append(wires.copy(held_d.at[t, src, DB], near_d.at[k, y, DB], xn))
+        near[k, i] = sends
+
+    def first(k, i):
+        if i == 0:
+            join(k)
+        near_sends(k, i)
+
+    def second(k, i):
         t = T[k]
-        got(near[k])
+        got(near[k, i])
+        at, width, end = parts[i]
         for other in range(2):
-            pa, pb = other * 2 + spot.y, spot.x * 2 + other
-
-            def put_a(at, total, pa=pa):
-                held_w[t, pa, :, at] = total.astype(low)
-
-            def put_b(at, total, pb=pb):
-                held_w[t, pb, :, pl.ds(pl.multiple_of(at.start + half, STEP), STEP)] = total.astype(low)
-
-            shifted_by = lambda at: pl.ds(pl.multiple_of(at.start + half, STEP), STEP)
-            add_to(put_a, [lambda at, p=pa: held_w[t, p, :, at], lambda at, o=other: near_w[k, o, :, at]], half)
-            add_to(
-                put_b,
-                [
-                    lambda at, p=pb: held_w[t, p, :, shifted_by(at)],
-                    lambda at, o=other: near_w[k, o, :, shifted_by(at)],
-                ],
-                half,
-            )
-            held_d[t, pa, DA] = (held_d[t, pa, DA].astype(f32) + near_d[k, other, DA].astype(f32)).astype(low)
-            held_d[t, pb, DB] = (held_d[t, pb, DB].astype(f32) + near_d[k, other, DB].astype(f32)).astype(low)
-        last[k] = [
-            wires.copy(held_w.at[t, xp, :, A], last_w.at[k, :, A], xn),
-            wires.copy(held_d.at[t, xp, DA], last_d.at[k, DA], xn),
-            wires.copy(held_w.at[t, yp, :, B], last_w.at[k, :, B], yn),
-            wires.copy(held_d.at[t, yp, DB], last_d.at[k, DB], yn),
-        ]
-
-    def third(k):
-        t = T[k]
-        got(last[k])
-        if k:
-            got(ring[k - 1])
-        terms = [lambda at: held_w[t, here, :, at], lambda at: last_w[k, :, at]]
-        if k:
-            terms.append(lambda at: ring_w[k - 1, :, at])
-        down = held_d[t, here].astype(f32) + last_d[k].astype(f32)
-        if k:
-            down = down + ring_d[k - 1].astype(f32)
-        if k < spot.depth - 1:
-
-            def put_on(at, total):
-                held_w[t, here, :, at] = total.astype(low)
-
-            add_to(put_on, terms, WIDE)
-            held_d[t, here] = down.astype(low)
-            ring[k] = [
-                wires.copy(held_w.at[t, here], ring_w.at[k], zn),
-                wires.copy(held_d.at[t, here], ring_d.at[k], zn),
-            ]
-        else:
-            for out, (begin, width) in zip(outs, PARTS):
-
-                def put_out(at, total, out=out):
-                    out[:, at] = total
+            for plane, base in ((other * 2 + spot.y, at), (spot.x * 2 + other, half + at)):
+                moved = lambda c, base=base: pl.ds(pl.multiple_of(c.start + base, STEP), STEP)
+
+                def put(c, total, plane=plane, moved=moved):
+                    held_w[t, plane, :, moved(c)] = total.astype(low)
 
                 add_to(
-                    put_out,
+                    put,
                     [
-                        lambda at, f=f, b=begin: f(pl.ds(pl.multiple_of(at.start + b, STEP), STEP))
-                        for f in terms
+                        lambda c, p=plane, m=moved: held_w[t, p, :, m(c)],
+                        lambda c, o=other, m=moved: near_w[k, o, :, m(c)],
                     ],
                     width,
                 )
-            outs[4][...] = down
+            if end:
+                pa, pb = other * 2 + spot.y, spot.x * 2 + other
+                held_d[t, pa, DA] = (held_d[t, pa, DA].astype(f32) + near_d[k, other, DA].astype(f32)).astype(low)
+                held_d[t, pb, DB] = (held_d[t, pb, DB].astype(f32) + near_d[k, other, DB].astype(f32)).astype(low)
+        [(a, b)], _ = spans(i)
+        sends = [
+            wires.copy(held_w.at[t, xp, :, a], last_w.at[k, :, a], xn),
+            wires.copy(held_w.at[t, yp, :, b], last_w.at[k, :, b], yn),
+        ]
+        if end:
+            sends.append(wires.copy(held_d.at[t, xp, DA], last_d.at[k, DA], xn))
+            sends.append(wires.copy(held_d.at[t, yp, DB], last_d.at[k, DB], yn))
+        last[k, i] = sends
+
+    def finish(terms, begin, end):
+        for out, (base, size) in zip(outs, PARTS):
+            a, b = max(begin, base), min(end, base + size)
+
+            def put_out(at, total, out=out, shift_by=a - base):
+                out[:, pl.ds(pl.multiple_of(at.start + shift_by, STEP), STEP)] = total
+
+            if a < b:
+                moved = [
+                    lambda at, f=f, a=a: f(pl.ds(pl.multiple_of(at.start + a, STEP), STEP)) for f in terms
+                ]
+                add_to(put_out, moved, b - a)
+
+    def far(k):
+        t = T[k]
+        if k:
+            got(climb[k - 1])
+            for plane in range(4):
+                base = lambda at: pl.ds(pl.multiple_of(at.start + 2 * half, STEP), STEP)
+
+                def put_far(at, total, plane=plane):
+                    held_w[t, plane, :, base(at)] = total.astype(low)
+
+                terms = [
+                    lambda at, p=plane: held_w[t, p, :, base(at)],
+                    lambda at, p=plane: climb_c[k - 1, p, :, at],
+                ]
+                add_to(put_far, terms, FAR_B)
+        if k < spot.depth - 1:
+            climb[k] = [wires.copy(held_w.at[t, :, :, C], climb_c.at[k], zn)]
+        else:
+            for way in (1, 2, 3):
+                to, plane = spot.flip(way)
+                flat.append(wires.copy(held_w.at[t, plane, :, C], flat_c.at[way - 1], to))
+
+    def far_end():
+        got(flat)
+        terms = [lambda at: held_w[T[-1], here, :, at]]
+        for way in range(3):
+            terms.append(
+                lambda at, w=way: flat_c[w, :, pl.ds(pl.multiple_of(at.start - 2 * half, STEP), STEP)]
+            )
+        finish(terms, 2 * half, WIDE)
+
+    def third(k, i):
+        t = T[k]
+        got(last[k, i])
+        if k:
+            got(ring[k - 1, i])
+        at, width, end = parts[i]
+        [(a, b)], _ = spans(i)
+        terms = [lambda c: held_w[t, here, :, c], lambda c: last_w[k, :, c]]
+        if k:
+            terms.append(lambda c: ring_w[k - 1, :, c])
+        if end:
+            down = held_d[t, here].astype(f32) + last_d[k].astype(f32)
+            if k:
+                down = down + ring_d[k - 1].astype(f32)
+        if k == spot.depth - 1:
+            finish(terms, at, at + width)
+            finish(terms, half + at, half + at + width)
+            if end:
+                outs[4][...] = down
+            return
+        for base in (at, half + at):
+            moved = lambda c, base=base: pl.ds(pl.multiple_of(c.start + base, STEP), STEP)
+
+            def put_on(c, total, moved=moved):
+                held_w[t, here, :, moved(c)] = total.astype(low)
+
+            add_to(put_on, [lambda c, f=f, m=moved: f(m(c)) for f in terms], width)
+        ring[k, i] = [wires.copy(held_w.at[t, here, :, c], ring_w.at[k, :, c], zn) for c in (a, b)]
+        if end:
+            held_d[t, here] = down.astype(low)
+            ring[k, i].append(wires.copy(held_d.at[t, here], ring_d.at[k], zn))
 
     load(0)
     for k in range(spot.depth):
         open_core(k)
-    yield
-    steps = [(first, 0)]
-    n = spot.depth
-    for k in range(1, n + 2):
-        for step, lag in ((first, 0), (second, 1), (third, 2)):
-            if 0 <= k - lag < n:
-                steps.append((step, k - lag))
-    for step, k in steps:
-        step(k)
-        yield
+    steps = {"C%d" % k: partial(far, k) for k in range(spot.depth)}
+    steps["C%d" % spot.depth] = far_end
+    for i in range(len(CUTS)):
+        for k in range(spot.depth):
+            steps["a%d%d" % (k, i)] = partial(first, k, i)
+            steps["b%d%d" % (k, i)] = partial(second, k, i)
+            steps["c%d%d" % (k, i)] = partial(third, k, i)
+    return steps
 
 
 class Back:
-    def __init__(self, mix, own, core, ext, d_patch, gains, head_w, heads, taps):
+    def __init__(self, mix, own, core, ext, d_patch, gains, head_w, heads, taps, tick):
         f32, low = jnp.float32, jnp.bfloat16
         count = mix.count
         dt_row, rate_row, skip_row = heads[0:1], heads[1:2], heads[2:3]
@@ -1230,6 +1807,7 @@
         flow = jnp.zeros((count, 128), f32)
         d_skip = jnp.zeros((1, 128), f32)
         for i in range(4):
+            tick()
             cut = slice(i * HEAD_M, (i + 1) * HEAD_M)
             inputs, grad = mix.inputs[:, cut], d_core[:, cut]
             decay, step = mix.decay(i), mix.row(mix.step_t, i)
@@ -1318,6 +1896,8 @@
     head_far,
     col_send,
     col_recv,
+    col_far,
+    col_sum,
     back_send,
     parts8,
     pair8,
@@ -1332,6 +1912,8 @@
     last_d,
     ring_w,
     ring_d,
+    climb_c,
+    flat_c,
     send,
     recv,
     swap_send,
@@ -1346,16 +1928,18 @@
     greet(spot)
     plane = spread_plane(wires, spot, mix_all)
     next(plane)
-    big = big_scatter(
+    steps = big_scatter(
         wires,
         spot,
         (g_qkv, g_attn, g_gate, g_up, g_down),
-        (held_w, held_d, stage_w, stage_d, near_w, near_d, last_w, last_d, ring_w, ring_d),
+        (held_w, held_d, stage_w, stage_d, near_w, near_d, last_w, last_d, ring_w, ring_d, climb_c, flat_c),
         (o_qkv, o_attn, o_gate, o_up, o_down),
         local,
     )
-    next(big)
+    tick = Ticker(steps, PLAN_B)
+    tick()
     next(plane)
+    tick()
     taps = tap_rows(spot, small_ref)
     heads = heads_ref[...]
     dt_row, rate_row = heads[0:1], heads[1:2]
@@ -1363,8 +1947,8 @@
         [small_ref[spot.q + 8 * i, TILE : TILE + 16, 0:HEAD_M][6:7].astype(f32) for i in range(4)], axis=1
     )
     gain = gain_row(small_ref[:, TILE + 5, 0:128])
-    next(big)
     run(plane)
+    tick()
     sums = None
     for x in range(2):
         at = pl.ds(x * count, count)
@@ -1373,9 +1957,10 @@
         d_patch = mix_all[pl.ds(x * 4, 4), :, pl.ds(0, D)].reshape(count, D)
         ext = mix_all[pl.ds(x * 4, 4), :, pl.ds(D, 128)].reshape(count, 128).astype(f32)
         back = Back(
-            mix, own_ref[at], core_ref[at], ext, d_patch, gains, head_w_ref[...].reshape(256, D), heads, taps
+            mix, own_ref[at], core_ref[at], ext, d_patch, gains, head_w_ref[...].reshape(256, D), heads, taps, tick
         )
         rows_all[at] = back.rows
+        tick()
         head = flat_dot(back.norm, d_patch, ((0,), (0,)))
         head_sum[...] = head if x == 0 else head_sum[...] + head
         new = [*back.taps, back.gain, back.bias, back.rate, back.skip]
@@ -1385,23 +1970,21 @@
             back.rows[:, 512:], small_ref[:, :TILE, :].reshape(D, SMALL_COLS), ((1,), (1,))
         )
         parts8[pl.ds(x * 2, 2)] = grad.astype(low).reshape(2, 2, TILE, D)
-        next(big)
+        tick()
     total8 = sum_plane(wires, spot, parts8, pair8, near8)
     next(total8)
+    tick()
     head_low[...] = head_sum[...].astype(low).reshape(depth, HEAD_M, D)
-    head_ring = [
-        wires.copy(head_low.at[(spot.z + k) % depth], head_far.at[k - 1], spot.above(k)) for k in range(1, depth)
-    ]
     next(total8)
+    tick()
     norm = norm_ref[...].reshape(2 * count, D)
     rows = rows_all[...]
     for b in range(4):
         block = flat_dot(norm[:, b * 256 : (b + 1) * 256], rows, ((0,), (0,)))
         col_send[pl.ds(b * 8, 8)] = block.astype(low).reshape(8, TILE, COLS)
-    swap_cols = Swap(
-        spot, swap_send.at[0], swap_recv.at[0], lambda to: col_send.at[to], lambda me: col_recv.at[me]
-    )
+    tick()
     grad_norm = next(total8)
+    tick()
     patch_sum = sum_ref[...]
     scale = lax.rsqrt(jnp.mean(patch_sum * patch_sum, axis=1, keepdims=True) + EPSILON)
     along = jnp.mean(grad_norm * gain * patch_sum, axis=1, keepdims=True)
@@ -1414,13 +1997,20 @@
     all_ref[spot.me] = jnp.concatenate([d_sum, *lines], axis=0).astype(low)
     spread = spread_all(wires, spot, all_ref)
     next(spread)
-    swap_cols.start()
-    col_recv[spot.me] = col_send[spot.me]
-    next(big)
+    col_ring = [
+        wires.copy(col_send.at[pl.ds(((spot.z + k) % depth) * 8, 8)], col_far.at[k - 1], spot.above(k))
+        for k in range(1, depth)
+    ]
+    head_ring = [
+        wires.copy(head_low.at[(spot.z + k) % depth], head_far.at[k - 1], spot.above(k)) for k in range(1, depth)
+    ]
+    tick()
     next(spread)
-    next(big)
+    tick()
     next(spread)
+    tick()
     run(spread)
+    tick()
     d_all = all_ref[:, :TILE].reshape(-1, D)
     for b in range(4):
         back_send[pl.ds(b * 8, 8)] = (
@@ -1428,34 +2018,40 @@
         )
     swap_rows = Swap(
         spot,
-        swap_send.at[1],
-        swap_recv.at[1],
+        swap_send,
+        swap_recv,
         lambda to: back_send.at[to],
         lambda me: o_rows.at[:, pl.ds(pl.multiple_of(me * 256, 256), 256)],
     )
     swap_rows.start()
+    got(col_ring)
+    for q in range(8):
+        total = col_send[spot.z * 8 + q].astype(f32)
+        for k in range(depth - 1):
+            total = total + col_far[k, q].astype(f32)
+        col_sum[q] = total.astype(low)
+    col_plane = plane_swap(wires, spot, lambda q: col_sum.at[q], lambda q: col_recv.at[q])
+    col_recv[spot.q] = col_sum[spot.q]
+    tick()
     o_rows[:, pl.ds(pl.multiple_of(spot.me * 256, 256), 256)] = back_send[spot.me]
     o_patch[...] = flat_dot(bytes_ref[...], d_all, ((0,), (0,)))
+    tick()
     got(head_ring)
     total = head_low[spot.z].astype(f32)
     for k in range(depth - 1):
         total = total + head_far[k].astype(f32)
     o_head[...] = total
-    next(big)
-    swap_cols.arrive()
+    tick()
+    got(col_plane)
+    total = jnp.zeros((TILE, COLS - 512), f32)
     for q in range(8):
-        total = col_recv[q, :, :512].astype(f32)
-        for t in range(1, depth):
-            total = total + col_recv[t * 8 + q, :, :512].astype(f32)
-        o_cols[q] = total
-    total = jnp.zeros((TILE, COLS - 512), f32)
-    for e in range(spot.count):
-        total = total + col_recv[e, :, 512:].astype(f32)
+        o_cols[q] = col_recv[q, :, :512].astype(f32)
+        total = total + col_recv[q, :, 512:].astype(f32)
     o_maps[...] = total
-    run(big)
+    tick()
+    tick.rest(REST_B)
     swap_rows.arrive()
     wires.drain()
-    swap_cols.leave()
     swap_rows.leave()
 
 
@@ -1482,7 +2078,9 @@
         pltpu.VMEM((depth, HEAD_M, D), low),
         pltpu.VMEM((depth - 1, HEAD_M, D), low),
         pltpu.VMEM((n_dev, TILE, COLS), low),
-        pltpu.VMEM((n_dev, TILE, COLS), low),
+        pltpu.VMEM((8, TILE, COLS), low),
+        pltpu.VMEM((depth - 1, 8, TILE, COLS), low),
+        pltpu.VMEM((8, TILE, COLS), low),
         pltpu.VMEM((n_dev, TILE, 256), low),
         pltpu.VMEM((4, 2, TILE, D), low),
         pltpu.VMEM((4, TILE, D), low),
@@ -1491,16 +2089,18 @@
         pltpu.VMEM((depth, 4, deep, D), low),
         pltpu.VMEM((4, TILE, WIDE), low),
         pltpu.VMEM((4, deep, D), low),
-        pltpu.VMEM((depth, 2, TILE, WIDE), low),
+        pltpu.VMEM((depth, 2, TILE, WIDE - FAR_B), low),
         pltpu.VMEM((depth, 2, deep, D), low),
-        pltpu.VMEM((depth, TILE, WIDE), low),
+        pltpu.VMEM((depth, TILE, WIDE - FAR_B), low),
         pltpu.VMEM((depth, deep, D), low),
-        pltpu.VMEM((depth - 1, TILE, WIDE), low),
+        pltpu.VMEM((depth - 1, TILE, WIDE - FAR_B), low),
         pltpu.VMEM((depth - 1, deep, D), low),
+        pltpu.VMEM((depth - 1, 4, TILE, FAR_B), low),
+        pltpu.VMEM((3, TILE, FAR_B), low),
         pltpu.SemaphoreType.DMA((N_WIRES,)),
         pltpu.SemaphoreType.DMA((N_WIRES,)),
-        pltpu.SemaphoreType.DMA((2, n_dev)),
-        pltpu.SemaphoreType.DMA((2, n_dev)),
+        pltpu.SemaphoreType.DMA((n_dev,)),
+        pltpu.SemaphoreType.DMA((n_dev,)),
         pltpu.SemaphoreType.DMA((5 * depth,)),
     ]
     return pl.pallas_call(
@@ -1517,24 +2117,6 @@
 
 
 BC = 2 * STATE
-
-
-def split_heads(rows_by_cols):
-    rows = rows_by_cols.shape[0]
-    return rows_by_cols.reshape(rows // 128, 128, -1, HEAD).transpose(2, 0, 1, 3)
-
-
-def join_heads(heads):
-    return heads.transpose(1, 2, 0, 3).reshape(heads.shape[1] * heads.shape[2], -1)
-
-
-def patch_mask():
-    places = jnp.arange(128)
-    return (places[:, None] >= places[None, :]) & (places[:, None] // PATCH == places[None, :] // PATCH)
-
-
-def dot_f32(spec, a, b):
-    return jnp.einsum(spec, a, b, preferred_element_type=jnp.float32)
 
 
 def fast_body(
@@ -1578,94 +2160,35 @@
     cols = jnp.concatenate([by_place(in_proj[:, :DI]), by_place(in_proj[:, DI : 2 * DI])], axis=2)
     heads_in = jnp.pad(jnp.stack([dt_bias, -jnp.exp(a_log), skip_weight]), ((0, 5), (0, 128 - MHEADS)))
     rows2 = byte_states.reshape(patches, PATCH * D)
-    (wide, deep, patch_sum, mixed, small, all_bytes, norm8, proj8, head_w, own8, maps8, step8, core8) = forward_call(
-        depth, n_dev, rows2, patch_proj, cols, vectors, out_proj, heads_in, qkv_proj, attn_out, gate_proj, up_proj, down_proj
-    )
-    lines = small[:, shard_rows : shard_rows + 10]
-    gain_g, gain_a, gain_f = (lines[:, k, : D // n_dev].reshape(-1).astype(f32) for k in (5, 7, 8))
-    gain_m = lines[:, 6, : DI // n_dev].reshape(-1).astype(f32)
-    my_places = lax.axis_index("fsdp") * patches + jnp.arange(patches, dtype=jnp.int32)
-    live = jnp.repeat((my_places < doc_lengths[0, 0] + doc_lengths[0, 1]).astype(f32), PATCH)[:, None]
-    qk, vals, attn_o = wide[:, : 2 * D], wide[:, 2 * D : 3 * D], wide[:, 3 * D : 4 * D]
-    gate_w, up_w = wide[:, 4 * D : 8 * D], wide[:, 8 * D :]
-    down_a, down_b = deep[:, : D // 2], deep[:, D // 2 :]
-    raw_mixed = mixed[:, :D]
-    mixer_r = lax.rsqrt(mixed[:, D : D + 1] / DI + EPSILON)
-    mixed_patch = patch_sum + raw_mixed * mixer_r
-
-    streams = byte_states.astype(f32) + jnp.repeat(mixed_patch, PATCH, axis=0)
-    normed = rms_scale(streams, gain_a).astype(low)
-    queries, key_rows = jnp.split(product(normed, qk).astype(low), 2, axis=1)
-    queries, key_rows = split_heads(queries), split_heads(key_rows)
-    value_rows = split_heads(product(normed, vals).astype(low))
-    scale = HEAD ** (-0.5)
-    scores = dot_f32("hbid,hbjd->hbij", queries, key_rows) * scale
-    attn_weights = jax.nn.softmax(jnp.where(patch_mask(), scores, -1e30), axis=-1)
-    attn_low = attn_weights.astype(low)
-    mixed_heads = join_heads(dot_f32("hbij,hbjd->hbid", attn_low, value_rows).astype(low))
-    attended = streams + product(mixed_heads, attn_o)
-    ffn_low = rms_scale(attended, gain_f).astype(low)
-    gate = product(ffn_low, gate_w)
-    upward = product(ffn_low, up_w)
-    sigma = jax.nn.sigmoid(gate)
-    hidden = (gate * sigma * upward).astype(low)
-    ffn_out = jnp.concatenate([product(hidden, down_a), product(hidden, down_b)], axis=1)
-    block_out = (live * (attended + ffn_out)).astype(low)
-
-    def scattered(act, grad):
-        return weight_grad(act, grad).astype(low)
-
-    grad_block = live * out_grad.astype(f32)
-    down_low = grad_block.astype(low)
-    grad_down = scattered(hidden, down_low)
-    grad_hidden = input_grad(down_low[:, : D // 2], down_a) + input_grad(down_low[:, D // 2 :], down_b)
-    grad_gate_low = (grad_hidden * upward * sigma * (1.0 + gate * (1.0 - sigma))).astype(low)
-    grad_up_low = (grad_hidden * gate * sigma).astype(low)
-    grad_gate = scattered(ffn_low, grad_gate_low)
-    grad_up = scattered(ffn_low, grad_up_low)
-    grad_ffn_in = input_grad(grad_gate_low, gate_w) + input_grad(grad_up_low, up_w)
-    _, norm_back = jax.vjp(rms_scale, attended, gain_f)
-    grad_attended_norm, grad_gain_f = norm_back(grad_ffn_in)
-    grad_attended = grad_block + grad_attended_norm
-    attn_grad_low = grad_attended.astype(low)
-    grad_attn_out = scattered(mixed_heads, attn_grad_low)
-    grad_mixed = split_heads(input_grad(attn_grad_low, attn_o).astype(low))
-    grad_values = dot_f32("hbij,hbid->hbjd", attn_low, grad_mixed)
-    grad_weights = dot_f32("hbid,hbjd->hbij", grad_mixed, value_rows)
-    grad_scores = attn_weights * (
-        grad_weights - jnp.sum(attn_weights * grad_weights, axis=-1, keepdims=True)
-    )
-    scores_low = grad_scores.astype(low)
-    grad_queries = dot_f32("hbij,hbjd->hbid", scores_low, key_rows) * scale
-    grad_keys = dot_f32("hbij,hbid->hbjd", scores_low, queries) * scale
-    grad_qk = jnp.concatenate([join_heads(grad_queries.astype(low)), join_heads(grad_keys.astype(low))], axis=1)
-    grad_v = join_heads(grad_values.astype(low))
-    grad_qkv = scattered(normed, jnp.concatenate([grad_qk, grad_v], axis=1))
-    grad_normed = input_grad(grad_qk, qk) + input_grad(grad_v, vals)
-    _, norm_back = jax.vjp(rms_scale, streams, gain_a)
-    grad_streams_norm, grad_gain_a = norm_back(grad_normed)
-    grad_streams = grad_attended + grad_streams_norm
-
-    grad_patch_mix = grad_streams.reshape(patches, PATCH, D).sum(axis=1)
-    mix_low = grad_patch_mix.astype(low)
-    along = jnp.sum(mix_low.astype(f32) * raw_mixed, axis=1, keepdims=True)
-    pair = jnp.concatenate([mixer_r, along], axis=1)
-    pair_high = pair.astype(low)
-    pair_rest = (pair - pair_high.astype(f32)).astype(low)
-    extra = jnp.pad(jnp.concatenate([pair_high, pair_rest], axis=1), ((0, 0), (0, 124)))
-    gains = jnp.pad(jnp.stack([grad_gain_a, grad_gain_f]), ((0, 6), (0, 0)))
-    saved = (small, all_bytes, norm8, proj8, head_w, own8, maps8, step8, core8)
+    (block_out, grad_streams, mix, direct, gains), grads, patch_sum, saved = forward_call(
+        depth,
+        n_dev,
+        rows2,
+        patch_proj,
+        cols,
+        vectors,
+        out_proj,
+        heads_in,
+        doc_lengths,
+        byte_states,
+        out_grad,
+        qkv_proj,
+        attn_out,
+        gate_proj,
+        up_proj,
+        down_proj,
+    )
     (g_qkv, g_attn, g_gate, g_up, g_down, g_patch, back_rows, g_out, g_cols, g_maps, everyone) = backward_call(
         depth,
         n_dev,
-        jnp.concatenate([mix_low, extra], axis=1),
-        grad_patch_mix,
+        mix,
+        direct,
         patch_sum,
         gains,
         saved,
         patch_proj,
         heads_in,
-        (grad_qkv, grad_attn_out, grad_gate, grad_up, grad_down),
+        grads,
     )
     grad_states = grad_streams + back_rows.reshape(rows, D).astype(f32)
 

time: 641 us -> 521 us (0.81)
  the two profiles are of different devices: /device:TPU:0 before, /device:TPU:8 now
where the time goes in v5:
time: 521 us; the launch traced here: 511 us
  Pallas kernels  480 us (92%)
  local copies, waits for them, and re-layouts  22.3 us (4%)
  other arithmetic  7.21 us (1%)
    pallas_call x1, Pallas kernels, forward_call(): pl.pallas_call(partial(forward_kernel, depth), out_shape=outs, in_specs=[...  267 us
    pallas_call x1, Pallas kernels, backward_call(): pl.pallas_call(partial(backward_kernel, depth), out_shape=outs, in_specs=...  213 us

profile of v5, /device:TPU:8, one launch (start us, length us, event | category | flops | bytes accessed | tf_op | source)
XLA Modules:
  0.0 510.6 jit_solution(7299366943984653689)
XLA Ops:
  0.7 0.0 copy-start.14
  0.7 0.0 copy-start.13
  0.7 0.0 copy-start.12
  0.7 0.0 copy-start
  0.7 0.8 slice_bitcast_fusion.5
  1.6 0.7 slice.81
  2.4 0.7 convert_bitcast_fusion
  3.1 0.7 pad.47
  3.7 0.7 pad.48
  4.4 0.7 pad.49
  5.1 0.7 pad.50
  5.7 0.7 pad.51
  6.4 1.9 concatenate.13.vec_ref
  8.3 1.0 fusion.6
  9.2 0.2 reshape.104
  9.5 0.1 copy.63
  9.6 0.2 reshape.105
  9.8 0.2 reshape.106
  10.1 0.1 copy.62
  10.2 0.2 reshape.107
  10.4 0.7 pad_maximum_fusion.1.cols_ref
  11.1 0.0 copy-done.14
  11.1 0.0 copy-done.13
  11.1 0.0 copy-done.12
  11.1 0.6 select_maximum_fusion.heads_ref
  11.7 0.0 copy-done
  11.7 1.0 reshape.103.rows_ref
  12.8 266.8 %global_forward.1 = (bf16[1024,12288]{1,0:T(8,128)(2,1)}, bf16[4096,1024]{1,0:T(8,128)(2,1)}, bf16[256,1024]{1,0:T(8,128)(2,1)}, f32[256,1024]{1,0:T(8,128)}, bf...) custom-call(bf16[32,8192]{1,0:T(8,128)(2,1)} %reshape.103.rows_ref, ...), custom_call_target="tpu_custom_call" | custom-call | tf_op jit(solution)/shard_map/global_forward/pallas_call | solution.py:1563
  279.6 213.0 %global_backward.1 = (f32[32,3072]{1,0:T(8,128)}, f32[32,1024]{1,0:T(8,128)}, f32[32,4096]{1,0:T(8,128)}, f32[32,4096]{1,0:T(8,128)}, f32[128,1024]{1,0:T(8,128)...) custom-call(bf16[32,1152]{1,0:T(8,128)(2,1)} %get-tuple-element.52.m, ...), custom_call_target="tpu_custom_call" | custom-call | tf_op jit(solution)/shard_map/global_backward/pallas_call | solution.py:2106
  492.7 1.4 fusion
  494.1 0.6 slice_bitcast_fusion.1
  494.7 1.5 slice_convert_fusion
  496.2 0.2 reduce_sum.19
  496.5 0.1 reshape.118
  496.6 0.1 reshape.119
  496.7 0.1 fusion.1
  496.8 0.6 slice_bitcast_fusion
  497.4 0.5 slice_bitcast_fusion.4
  497.9 0.0 copy-done.7
  498.0 0.2 reshape.113
  498.2 0.3 copy.55
  498.5 0.0 copy-start.1
  498.6 0.2 reshape.114
  498.7 0.2 reshape.115
  499.0 0.3 copy.56
  499.3 0.2 reshape.116
  499.5 0.0 copy-done.11
  499.5 0.8 pad_maximum_fusion
  500.3 0.6 fusion.2
  501.0 0.1 reshape.120
  501.0 0.1 squeeze_reshape.3
  501.1 0.6 dynamic_slice.24
  501.7 1.2 reshape.121
  503.0 0.0 copy-start.3
  503.0 0.0 copy-done.1
  503.0 1.1 add.41
  504.1 0.8 copy.72
  504.9 1.0 copy.73
  505.9 0.7 copy.74
  506.6 0.7 copy.75
  507.3 0.7 copy.76
  508.0 0.8 copy.77
  508.8 0.8 copy.78
  509.6 0.8 copy.79
  (43 shorter events, 0.3 us)
Async XLA Ops:
  0.7 10.5 %copy-start.14 = (f32[32]{0:T(128)S(1)}, f32[32]{0:T(128)}, u32[]{:S(2)}) copy-start(f32[32]{0:T(128)} %param.29) | copy-start | bytes 388
  0.7 10.5 %copy-start.13 = (f32[32]{0:T(128)S(1)}, f32[32]{0:T(128)}, u32[]{:S(2)}) copy-start(f32[32]{0:T(128)} %param.28) | copy-start | bytes 388
  0.7 10.4 %copy-start.12 = (f32[32]{0:T(128)S(1)}, f32[32]{0:T(128)}, u32[]{:S(2)}) copy-start(f32[32]{0:T(128)} %param.30) | copy-start | bytes 388
  0.7 11.1 %copy-start = (bf16[256,1024]{1,0:T(8,128)(2,1)S(1)}, bf16[256,1024]{1,0:T(8,128)(2,1)}, u32[]{:S(2)}) copy-start(bf16[256,1024]{1,0:T(8,128)(2,1)} %states_ref.1) | copy-start | bytes 1572868
  494.7 3.2 copy-start.7
  497.9 1.6 copy-start.11
  498.5 4.4 copy-start.1
  500.3 4.6 copy-start.2
  503.0 1.2 copy-start.3
  503.0 2.9 copy-start.9
  503.0 3.6 copy-start.8
  503.0 4.4 copy-start.10
  504.1 3.9 copy-start.6
  504.1 4.7 copy-start.5
  504.9 4.7 copy-start.4

commit v6 on v5

--- a/solution.py
+++ b/solution.py
@@ -475,7 +475,9 @@
         self.z, self.x, self.y, self.c = dp // 2, dp % 2, fs // 2, fs % 2
         self.q = self.x * 4 + self.y * 2 + self.c
         self.plane = self.x * 2 + self.y
-        self.column = [(self.z + depth - j) % depth for j in range(depth)]
+        swap = lambda place: place + (place // 2) * (1 - 2 * (place % 2))
+        self.turn = swap(self.z)
+        self.column = [swap((self.turn + depth - j) % depth) for j in range(depth)]
 
     def flip(self, way):
         x = 1 - self.x if way & 2 else self.x
@@ -484,6 +486,10 @@
 
     def sibling(self):
         return device(self.z, self.x, self.y, 1 - self.c)
+
+    def onward(self):
+        place = (self.turn + 1) % self.depth
+        return device(place + (place // 2) * (1 - 2 * (place % 2)), self.x, self.y, self.c)
 
     def above(self, k):
         return device((self.z + k) % self.depth, self.x, self.y, self.c)
@@ -592,14 +598,14 @@
     yield
     for j in range(1, spot.depth):
         got([ring[j - 1]])
-        block = at(spot.column[j], spot.plane, spot.c)
+        block = at((spot.z + spot.depth - j) % spot.depth, spot.plane, spot.c)
         flat.append([wires.copy(block, block, spot.flip(way)[0]) for way in (1, 2, 3)])
         core.append(wires.copy(block, block, spot.sibling()))
     yield
     for j in range(spot.depth):
         for way in (1, 2, 3):
             got([flat[j][way - 1]])
-            block = at(spot.column[j], spot.flip(way)[1], spot.c)
+            block = at((spot.z + spot.depth - j) % spot.depth, spot.flip(way)[1], spot.c)
             core.append(wires.copy(block, block, spot.sibling()))
     yield
     got(core)
@@ -688,7 +694,7 @@
 
 def big_gather(wires, spot, ow, od, shards):
     down = od.shape[0] // spot.count
-    xn, yn, cn, zn = spot.flip(2)[0], spot.flip(1)[0], spot.sibling(), spot.above(1)
+    xn, yn, cn, zn = spot.flip(2)[0], spot.flip(1)[0], spot.sibling(), spot.onward()
     here, xp, yp, xy = spot.plane, spot.flip(2)[1], spot.flip(1)[1], spot.flip(3)[1]
     parts = {"C": (WIDE - FAR_F, FAR_F, None), ("A", 0): (0, 2 * D, None), ("B", 0): (2 * D, 2 * D, None)}
     begin, side, at = 4 * D, (WIDE - FAR_F - 4 * D) // 2, 0
@@ -779,14 +785,12 @@
             core[len(CUTS_F) + 1].append(go(T[j], plane, "C", cn))
 
     chunks, n = range(len(CUTS_F) + 1), spot.depth
-    steps = {"C%d" % j: partial(far, j) for j in range(-1, n)}
+    steps = {far_step(j): partial(far, j) for j in range(-1, n)}
     for i in chunks:
         for j in range(n):
-            steps["r%d%d" % (j, i)] = partial(climb_on, j, i)
-            steps["a%d%d" % (j, i)] = partial(first, j, i)
-            steps["b%d%d" % (j, i)] = partial(second, j, i)
-            steps["c%d%d" % (j, i)] = partial(third, j, i)
-        del steps["r%d%d" % (n - 1, i)]
+            for kind, act in enumerate((climb_on, first, second, third), 1):
+                if act is not climb_on or j < n - 1:
+                    steps[100 * kind + 10 * j + i] = partial(act, j, i)
 
     def close(which):
         for part in which:
@@ -794,6 +798,10 @@
                 got(copies)
 
     return steps, close
+
+
+def far_step(j):
+    return 510 + 10 * j
 
 
 class Ticker:
@@ -1146,92 +1154,92 @@
 
 N_WIRES = 512
 PLAN_F = (
-    ("C-1", "r00", "a00"),
+    (500, 100, 200),
     (),
     (),
     (),
-    ("b00", "a01"),
-    ("r10", "a10", "r01"),
+    (300, 201),
+    (110, 210, 101),
     (),
-    ("b10", "a02", "r20"),
-    ("c00",),
-    ("a20", "b01"),
-    ("b20", "r02", "r03", "a03"),
-    ("c10",),
-    ("b02",),
-    ("a30",),
-    ("r11", "a11"),
-    ("C0",),
-    ("b30",),
-    ("c20",),
-    ("r12", "a12"),
-    ("b03",),
-    ("r13", "a13"),
+    (310, 202, 120),
+    (400,),
+    (220, 301),
+    (320, 102, 103, 203),
+    (410,),
+    (302,),
+    (230,),
+    (111, 211),
+    (510,),
+    (330,),
+    (420,),
+    (112, 212),
+    (303,),
+    (113, 213),
     (),
-    ("c30", "b11", "b12"),
-    ("r21", "a21"),
-    ("b13", "r22", "a22"),
-    ("C1", "c01", "c02"),
-    ("r23", "a23", "b21"),
-    ("b22", "c03", "c11"),
-    ("a31", "b23", "c12"),
-    ("C2", "a32", "c13"),
+    (430, 311, 312),
+    (121, 221),
+    (313, 122, 222),
+    (520, 401, 402),
+    (123, 223, 321),
+    (322, 403, 411),
+    (231, 323, 412),
+    (530, 232, 413),
 )
 REST_F = (
-    "b31",
-    "a33",
-    "b32",
-    "b33",
-    "C3",
-    "c21",
-    "c22",
-    "c23",
-    "c31",
-    "c32",
-    "c33",
+    331,
+    233,
+    332,
+    333,
+    540,
+    421,
+    422,
+    423,
+    431,
+    432,
+    433,
 )
 PLAN_B = (
     (),
     (),
-    ("a00",),
-    ("a01", "a02"),
-    ("C0",),
-    ("a10",),
+    (200,),
+    (201, 202),
+    (510,),
+    (210,),
     (),
-    ("C1",),
-    ("a11",),
-    ("b00",),
-    ("a20",),
-    ("C2",),
-    ("c00",),
+    (520,),
+    (211,),
+    (300,),
+    (220,),
+    (530,),
+    (400,),
     (),
     (),
     (),
-    ("b01", "a12"),
+    (301, 212),
     (),
     (),
-    ("b02",),
-    ("b10", "a21"),
+    (302,),
+    (310, 221),
     (),
     (),
-    ("a22", "c01", "b11", "c10"),
-    ("a30", "b12", "c02"),
-    ("a31", "b20"),
-    ("c11", "a32", "b21", "C3"),
+    (222, 401, 311, 410),
+    (230, 312, 402),
+    (231, 320),
+    (411, 232, 321, 540),
 )
 REST_B = (
-    "c12",
-    "b22",
-    "c20",
-    "b30",
-    "c21",
-    "b31",
-    "c22",
-    "b32",
-    "C4",
-    "c30",
-    "c31",
-    "c32",
+    412,
+    322,
+    420,
+    330,
+    421,
+    331,
+    422,
+    332,
+    550,
+    430,
+    431,
+    432,
 )
 
 
@@ -1591,7 +1599,7 @@
     f32, low = jnp.float32, jnp.bfloat16
     held_w, held_d, stage_w, stage_d, near_w, near_d, last_w, last_d, ring_w, ring_d, climb_c, flat_c = bufs
     half, deep = (WIDE - FAR_B) // 2, held_d.shape[2]
-    xn, yn, cn, zn = spot.flip(2)[0], spot.flip(1)[0], spot.sibling(), spot.above(1)
+    xn, yn, cn, zn = spot.flip(2)[0], spot.flip(1)[0], spot.sibling(), spot.onward()
     here, xp, yp, xy = spot.plane, spot.flip(2)[1], spot.flip(1)[1], spot.flip(3)[1]
     T = [spot.column[k % spot.depth] for k in range(1, spot.depth + 1)]
     core, fetch, near, last, ring = {}, {}, {}, {}, {}
@@ -1600,13 +1608,13 @@
     climb, flat = {}, []
     DA, DB = pl.ds(0, deep // 2), pl.ds(deep // 2, deep // 2)
 
-    def load(k):
-        fetch[k] = []
+    def load(k, side):
+        fetch[k, side] = []
         for i, ref in enumerate(grads):
             dst = stage_w.at[:, :, pl.ds(*PARTS[i])] if i < 4 else stage_d
-            copy = pltpu.make_async_copy(ref.at[T[k], :, spot.c], dst, local.at[k * 5 + i])
+            copy = pltpu.make_async_copy(ref.at[T[k], pl.ds(2 * side, 2), spot.c], dst, local.at[k * 5 + i])
             copy.start()
-            fetch[k].append(copy)
+            fetch[k, side].append(copy)
 
     def open_core(k):
         core[k] = []
@@ -1617,17 +1625,25 @@
     def join(k):
         t = T[k]
         got(core[k])
-        for copy in fetch[k]:
-            copy.wait()
-        for plane in range(4):
-
-            def put_w(at, total, plane=plane):
-                held_w[t, plane, :, at] = total.astype(low)
-
-            add_to(put_w, [lambda at, p=plane: held_w[t, p, :, at], lambda at, p=plane: stage_w[p, :, at]], WIDE)
-            held_d[t, plane] = (held_d[t, plane].astype(f32) + stage_d[plane].astype(f32)).astype(low)
-        if k + 1 < spot.depth:
-            load(k + 1)
+        for side in range(2):
+            for copy in fetch[k, side]:
+                copy.wait()
+            for half_at in range(2):
+                plane = 2 * side + half_at
+
+                def put_w(at, total, plane=plane):
+                    held_w[t, plane, :, at] = total.astype(low)
+
+                add_to(
+                    put_w,
+                    [lambda at, p=plane: held_w[t, p, :, at], lambda at, h=half_at: stage_w[h, :, at]],
+                    WIDE,
+                )
+                held_d[t, plane] = (held_d[t, plane].astype(f32) + stage_d[half_at].astype(f32)).astype(low)
+            if side == 0:
+                load(k, 1)
+            elif k + 1 < spot.depth:
+                load(k + 1, 0)
 
     parts, at = [], 0
     for i, width in enumerate(CUTS):
@@ -1771,16 +1787,15 @@
             held_d[t, here] = down.astype(low)
             ring[k, i].append(wires.copy(held_d.at[t, here], ring_d.at[k], zn))
 
-    load(0)
+    load(0, 0)
     for k in range(spot.depth):
         open_core(k)
-    steps = {"C%d" % k: partial(far, k) for k in range(spot.depth)}
-    steps["C%d" % spot.depth] = far_end
+    steps = {far_step(k): partial(far, k) for k in range(spot.depth)}
+    steps[far_step(spot.depth)] = far_end
     for i in range(len(CUTS)):
         for k in range(spot.depth):
-            steps["a%d%d" % (k, i)] = partial(first, k, i)
-            steps["b%d%d" % (k, i)] = partial(second, k, i)
-            steps["c%d%d" % (k, i)] = partial(third, k, i)
+            for kind, act in enumerate((first, second, third), 2):
+                steps[100 * kind + 10 * k + i] = partial(act, k, i)
     return steps
 
 
@@ -1860,6 +1875,7 @@
     depth,
     mix_ref,
     direct_ref,
+    streams_ref,
     sum_ref,
     gains_ref,
     small_ref,
@@ -1884,11 +1900,12 @@
     o_up,
     o_down,
     o_patch,
-    o_rows,
+    o_states,
     o_head,
     o_cols,
     o_maps,
     all_ref,
+    o_rows,
     mix_all,
     rows_all,
     head_sum,
@@ -1962,6 +1979,7 @@
         rows_all[at] = back.rows
         tick()
         head = flat_dot(back.norm, d_patch, ((0,), (0,)))
+        head = head.reshape(TILE, PATCH, D)
         head_sum[...] = head if x == 0 else head_sum[...] + head
         new = [*back.taps, back.gain, back.bias, back.rate, back.skip]
         sums = new if sums is None else [a + b for a, b in zip(sums, new)]
@@ -1974,7 +1992,9 @@
     total8 = sum_plane(wires, spot, parts8, pair8, near8)
     next(total8)
     tick()
-    head_low[...] = head_sum[...].astype(low).reshape(depth, HEAD_M, D)
+    head_low[...] = head_sum[...].reshape(256, D).astype(low).reshape(depth, HEAD_M, D)
+    fetch = pltpu.make_async_copy(streams_ref, head_sum, local.at[5 * depth])
+    fetch.start()
     next(total8)
     tick()
     norm = norm_ref[...].reshape(2 * count, D)
@@ -2051,11 +2071,14 @@
     tick()
     tick.rest(REST_B)
     swap_rows.arrive()
+    fetch.wait()
+    for j in range(PATCH):
+        o_states[:, j] = head_sum[:, j] + o_rows[:, j * D : (j + 1) * D].astype(f32)
     wires.drain()
     swap_rows.leave()
 
 
-def backward_call(depth, n_dev, mix, direct, patch_sum, gains, saved, patch_proj, heads, grads):
+def backward_call(depth, n_dev, mix, direct, streams, patch_sum, gains, saved, patch_proj, heads, grads):
     f32, low = jnp.float32, jnp.bfloat16
     vmem = pl.BlockSpec(memory_space=pltpu.VMEM)
     anywhere = pl.BlockSpec(memory_space=pl.ANY)
@@ -2065,16 +2088,17 @@
     outs = [shape((TILE, width), f32) for _, width in PARTS] + [
         shape((deep, D), f32),
         shape((256, D), f32),
-        shape((TILE, PATCH * D), low),
+        shape((TILE, PATCH, D), f32),
         shape((HEAD_M, D), f32),
         shape((8, TILE, 512), f32),
         shape((TILE, COLS - 512), f32),
         shape((n_dev, SMALL_ROWS, D), low),
     ]
     scratch = [
+        pltpu.VMEM((TILE, PATCH * D), low),
         pltpu.VMEM((8, TILE, EXT), low),
         pltpu.VMEM((8 * TILE, COLS), low),
-        pltpu.VMEM((256, D), f32),
+        pltpu.VMEM((TILE, PATCH, D), f32),
         pltpu.VMEM((depth, HEAD_M, D), low),
         pltpu.VMEM((depth - 1, HEAD_M, D), low),
         pltpu.VMEM((n_dev, TILE, COLS), low),
@@ -2087,8 +2111,8 @@
         pltpu.VMEM((3, TILE, D), low),
         pltpu.VMEM((depth, 4, TILE, WIDE), low),
         pltpu.VMEM((depth, 4, deep, D), low),
-        pltpu.VMEM((4, TILE, WIDE), low),
-        pltpu.VMEM((4, deep, D), low),
+        pltpu.VMEM((2, TILE, WIDE), low),
+        pltpu.VMEM((2, deep, D), low),
         pltpu.VMEM((depth, 2, TILE, WIDE - FAR_B), low),
         pltpu.VMEM((depth, 2, deep, D), low),
         pltpu.VMEM((depth, TILE, WIDE - FAR_B), low),
@@ -2101,19 +2125,19 @@
         pltpu.SemaphoreType.DMA((N_WIRES,)),
         pltpu.SemaphoreType.DMA((n_dev,)),
         pltpu.SemaphoreType.DMA((n_dev,)),
-        pltpu.SemaphoreType.DMA((5 * depth,)),
+        pltpu.SemaphoreType.DMA((5 * depth + 1,)),
     ]
     return pl.pallas_call(
         partial(backward_kernel, depth),
         out_shape=outs,
-        in_specs=[vmem] * 15 + [anywhere] * 5,
+        in_specs=[vmem] * 2 + [anywhere] + [vmem] * 13 + [anywhere] * 5,
         out_specs=[vmem] * 11,
         scratch_shapes=scratch,
         compiler_params=pltpu.CompilerParams(
             collective_id=1, has_side_effects=True, vmem_limit_bytes=62 * 2**20
         ),
         name="global_backward",
-    )(mix, direct, patch_sum, gains, *saved, patch_proj, heads, *cut)
+    )(mix, direct, streams.reshape(TILE, PATCH, D), patch_sum, gains, *saved, patch_proj, heads, *cut)
 
 
 BC = 2 * STATE
@@ -2150,12 +2174,12 @@
 
     shard_rows = in_proj.shape[0]
     maps_and_steps = jnp.pad(in_proj[:, 2 * DI :], ((0, 0), (0, SMALL_COLS - BC - MHEADS)))
-    lines = [conv_weight[:, k] for k in range(CONV)]
-    lines += [conv_bias, global_gain, mixer_gain, attn_gain, ffn_gain, doc_lengths.reshape(-1).astype(low)]
-    lines = jnp.stack([jnp.pad(line, (0, SMALL_COLS - line.shape[0])) for line in lines])
-    vectors = jnp.concatenate(
-        [maps_and_steps, lines, jnp.zeros((SMALL_ROWS - shard_rows - lines.shape[0], SMALL_COLS), low)]
-    )
+    lines = []
+    for line in (conv_bias, global_gain, mixer_gain, attn_gain, ffn_gain, doc_lengths.reshape(-1).astype(low)):
+        lines += [line, jnp.zeros((SMALL_COLS - line.shape[0],), low)]
+    lines = jnp.concatenate(lines + [jnp.zeros((6 * SMALL_COLS,), low)]).reshape(-1, SMALL_COLS)
+    taps = jnp.pad(conv_weight.T, ((0, 0), (0, SMALL_COLS - conv_weight.shape[0])))
+    vectors = jnp.concatenate([maps_and_steps, taps, lines])
     by_place = lambda cols: cols.reshape(shard_rows, 4, 8, HEAD_M).transpose(2, 0, 1, 3).reshape(8, shard_rows, 256)
     cols = jnp.concatenate([by_place(in_proj[:, :DI]), by_place(in_proj[:, DI : 2 * DI])], axis=2)
     heads_in = jnp.pad(jnp.stack([dt_bias, -jnp.exp(a_log), skip_weight]), ((0, 5), (0, 128 - MHEADS)))
@@ -2178,11 +2202,12 @@
         up_proj,
         down_proj,
     )
-    (g_qkv, g_attn, g_gate, g_up, g_down, g_patch, back_rows, g_out, g_cols, g_maps, everyone) = backward_call(
+    (g_qkv, g_attn, g_gate, g_up, g_down, g_patch, grad_states, g_out, g_cols, g_maps, everyone) = backward_call(
         depth,
         n_dev,
         mix,
         direct,
+        grad_streams,
         patch_sum,
         gains,
         saved,
@@ -2190,7 +2215,6 @@
         heads_in,
         grads,
     )
-    grad_states = grad_streams + back_rows.reshape(rows, D).astype(f32)
 
     lines = everyone[:, shard_rows : shard_rows + 9].astype(f32)
     sums = jnp.sum(lines, axis=0)
@@ -2209,7 +2233,7 @@
     )
     return (
         block_out,
-        grad_states,
+        grad_states.reshape(rows, D),
         g_patch,
         own_part(sums[CONV + 4]),
         grad_in_proj,

time: 521 us -> 476 us (0.914)
  Pallas kernels: 480 us -> 442 us
    pallas_call x1, Pallas kernels: 267 us -> 234 us  [forward_call(): pl.pallas_call(partial(forward_kernel, depth), out_shape=outs, in_specs=[...]
    pallas_call x1, Pallas kernels: 213 us -> 208 us  [backward_call(): pl.pallas_call(partial(backward_kernel, depth), out_shape=outs, in_specs=...]
where the time goes in v6:
time: 476 us; the launch traced here: 467 us
  Pallas kernels  442 us (93%)
  local copies, waits for them, and re-layouts  17.4 us (4%)
  other arithmetic  6.08 us (1%)
    pallas_call x1, Pallas kernels, forward_call(): pl.pallas_call(partial(forward_kernel, depth), out_shape=outs, in_specs=[...  234 us
    pallas_call x1, Pallas kernels, backward_call(): pl.pallas_call(partial(backward_kernel, depth), out_shape=outs, in_specs=...  208 us

profile of v6, /device:TPU:8, one launch (start us, length us, event | category | flops | bytes accessed | tf_op | source)
XLA Modules:
  0.0 466.8 jit_solution(16626226981243587824)
XLA Ops:
  0.7 0.0 slice-start
  0.7 0.0 copy-start.21
  0.7 0.0 copy-start.19
  0.7 0.0 copy-start.18
  0.7 0.0 copy-start
  0.7 0.0 copy-start.20
  0.7 0.0 copy-start.14
  0.7 0.0 copy-start.13
  0.7 0.0 copy-start.15
  0.8 0.0 copy-start.16
  0.8 0.0 copy-start.17
  0.8 0.0 copy-start.12
  0.8 1.0 fusion.11
  1.8 0.2 reshape.110
  2.1 0.1 copy.63
  2.2 0.2 reshape.111
  2.4 0.2 reshape.112
  2.7 0.1 copy.62
  2.8 0.2 reshape.113
  3.0 0.7 pad_maximum_fusion.1.cols_ref
  3.7 0.0 copy-done.21
  3.7 0.0 copy-done.19
  3.7 0.0 copy-done.18
  3.7 0.6 select_maximum_fusion.heads_ref
  4.3 0.0 copy-done
  4.3 1.0 reshape.109.rows_ref
  5.4 0.0 copy-done.20
  5.5 0.1 concatenate.16
  5.6 0.6 fusion.5.vec_ref
  6.2 234.2 %global_forward.1 = (bf16[1024,12288]{1,0:T(8,128)(2,1)}, bf16[4096,1024]{1,0:T(8,128)(2,1)}, bf16[256,1024]{1,0:T(8,128)(2,1)}, f32[256,1024]{1,0:T(8,128)}, bf...) custom-call(bf16[32,8192]{1,0:T(8,128)(2,1)} %reshape.109.rows_ref, ...), custom_call_target="tpu_custom_call" | custom-call | tf_op jit(solution)/shard_map/global_forward/pallas_call | solution.py:1571
  240.5 207.8 %global_backward.1 = (f32[32,3072]{1,0:T(8,128)}, f32[32,1024]{1,0:T(8,128)}, f32[32,4096]{1,0:T(8,128)}, f32[32,4096]{1,0:T(8,128)}, f32[128,1024]{1,0:T(8,128)...) custom-call(bf16[32,1152]{1,0:T(8,128)(2,1)} %get-tuple-element.51.m, ...), custom_call_target="tpu_custom_call" | custom-call | tf_op jit(solution)/shard_map/global_backward/pallas_call | solution.py:2130
  448.3 1.4 fusion
  449.7 0.6 slice_bitcast_fusion.1
  450.3 1.5 slice_convert_fusion
  451.8 0.2 reduce_sum.19
  452.1 0.0 copy-start.3
  452.1 0.1 reshape.127
  452.2 0.1 reshape.128
  452.3 0.1 fusion.6
  452.4 0.6 slice_bitcast_fusion
  453.0 0.5 slice_bitcast_fusion.4
  453.5 0.0 copy-done.7
  453.6 0.2 reshape.122
  453.8 0.3 copy.55
  454.2 0.2 reshape.123
  454.3 0.2 reshape.124
  454.6 0.3 copy.56
  454.9 0.2 reshape.125
  455.1 0.0 copy-start.9
  455.1 0.8 pad_maximum_fusion
  456.0 0.9 slice_reduce_fusion
  456.9 0.1 reshape.129
  457.0 0.1 squeeze_reshape.3
  457.0 0.6 dynamic_slice.24
  457.6 0.6 fusion.7
  458.2 1.9 copy.73
  460.1 1.0 copy.74
  461.1 1.0 copy.75
  462.1 0.7 copy.76
  462.8 0.7 copy.77
  463.5 0.7 copy.78
  464.2 0.8 copy.79
  465.0 0.8 copy.80
  465.8 0.8 copy.81
  (41 shorter events, 0.2 us)
Async XLA Ops:
  0.7 4.9 %slice-start = ((bf16[32,4384]{1,0:T(8,128)(2,1)}), bf16[32,288]{1,0:T(8,128)(2,1)S(1)}, s32[]{:S(2)}) async-start(bf16[32,4384]{1,0:T(8,128)(2,1)} %param.25), calls=%async_computation | async-start | bytes 49152 | tf_op jit(solution)/shard_map/slice | solution.py:2176
  0.7 3.0 copy-start.21
  0.7 3.0 copy-start.19
  0.7 3.0 copy-start.18
  0.7 3.6 copy-start
  0.7 4.7 copy-start.20
  0.7 4.7 %copy-start.14 = (bf16[32]{0:T(256)(128)(2,1)S(1)}, bf16[32]{0:T(256)(128)(2,1)}, u32[]{:S(2)}) copy-start(bf16[32]{0:T(256)(128)(2,1)} %param.24) | copy-start | bytes 196
  0.7 4.7 %copy-start.13 = (bf16[72]{0:T(256)(128)(2,1)S(1)}, bf16[72]{0:T(256)(128)(2,1)}, u32[]{:S(2)}) copy-start(bf16[72]{0:T(256)(128)(2,1)} %param.27) | copy-start | bytes 436
  0.7 4.7 %copy-start.15 = (bf16[64]{0:T(256)(128)(2,1)S(1)}, bf16[64]{0:T(256)(128)(2,1)}, u32[]{:S(2)}) copy-start(bf16[64]{0:T(256)(128)(2,1)} %param.31) | copy-start | bytes 388
  0.8 4.7 %copy-start.16 = (bf16[32]{0:T(256)(128)(2,1)S(1)}, bf16[32]{0:T(256)(128)(2,1)}, u32[]{:S(2)}) copy-start(bf16[32]{0:T(256)(128)(2,1)} %param.33) | copy-start | bytes 196
  0.8 4.7 %copy-start.17 = (bf16[32]{0:T(256)(128)(2,1)S(1)}, bf16[32]{0:T(256)(128)(2,1)}, u32[]{:S(2)}) copy-start(bf16[32]{0:T(256)(128)(2,1)} %param.36) | copy-start | bytes 196
  0.8 4.8 %copy-start.12 = (bf16[72,4]{0,1:T(4,128)(2,1)S(1)}, bf16[72,4]{0,1:T(4,128)(2,1)}, u32[]{:S(2)}) copy-start(bf16[72,4]{0,1:T(4,128)(2,1)} %param.26) | copy-start | bytes 1732
  450.3 3.2 copy-start.7
  452.1 1.8 copy-start.3
  453.5 1.6 copy-start.11
  453.8 6.3 %copy-start.2 = (f32[32,8,1024]{2,1,0:T(8,128)S(1)}, f32[32,8,1024]{2,1,0:T(8,128)}, u32[]{:S(2)}) copy-start(f32[32,8,1024]{2,1,0:T(8,128)} %get-tuple-element.70) | copy-start | bytes 3145732
  454.6 6.5 %copy-start.1 = (f32[256,1024]{1,0:T(8,128)S(1)}, f32[256,1024]{1,0:T(8,128)}, u32[]{:S(2)}) copy-start(f32[256,1024]{1,0:T(8,128)} %get-tuple-element.115) | copy-start | bytes 3145732
  455.1 7.0 %copy-start.9 = (f32[64,1024]{1,0:T(8,128)S(1)}, f32[64,1024]{1,0:T(8,128)}, u32[]{:S(2)}) copy-start(f32[64,1024]{1,0:T(8,128)} %get-tuple-element.124) | copy-start | bytes 786436
  456.0 6.8 %copy-start.8 = (f32[32,3072]{1,0:T(8,128)S(1)}, f32[32,3072]{1,0:T(8,128)}, u32[]{:S(2)}) copy-start(f32[32,3072]{1,0:T(8,128)} %get-tuple-element.126) | copy-start | bytes 1179652
  458.2 5.3 %copy-start.10 = (f32[32,1024]{1,0:T(8,128)S(1)}, f32[32,1024]{1,0:T(8,128)}, u32[]{:S(2)}) copy-start(f32[32,1024]{1,0:T(8,128)} %get-tuple-element.127) | copy-start | bytes 393220
  460.1 4.1 copy-start.6
  460.1 4.9 %copy-start.5 = (f32[32,4096]{1,0:T(8,128)S(1)}, f32[32,4096]{1,0:T(8,128)}, u32[]{:S(2)}) copy-start(f32[32,4096]{1,0:T(8,128)} %get-tuple-element.130) | copy-start | bytes 1572868
  461.1 4.7 %copy-start.4 = (f32[128,1024]{1,0:T(8,128)S(1)}, f32[128,1024]{1,0:T(8,128)}, u32[]{:S(2)}) copy-start(f32[128,1024]{1,0:T(8,128)} %get-tuple-element.131) | copy-start | bytes 1572868
